TPU v7x, 32 devices: a whole 2x2x4 slice. The times are simulated.
32 devices in a mesh: dp: 16 (over z, y, x), mp: 2 (over core).
Axes of the slice: x: 2, y: 2, z: 4, core: 2. Of those that a mesh axis runs over, the one named last changes fastest.
Arguments:
- tokens: bfloat16 [32768, 768], P('dp'), may hold values from -6 to 6
- out_grad: bfloat16 [32768, 768], P('dp'), may hold values from -6 to 6
- lengths: int32 [16, 4], P('dp'), may hold values from 1 to 1024, 2048 in all within a row
- counts: int32 [16, 4], P('dp'), may hold values from 1 to 1024
- dest_slot: int32 [4096], replicated, may hold values from 0 to 4095, as said below
- qkv_weight: bfloat16 [3, 768, 768], P(None, None, 'mp'), may hold values from -0.3125 to 0.3125
- out_weight: bfloat16 [768, 768], P('mp'), may hold values from -0.875 to 0.875
- up_weight: bfloat16 [768, 3072], P(None, 'mp'), may hold values from -0.21875 to 0.21875
- down_weight: bfloat16 [3072, 768], P('mp'), may hold values from -0.109375 to 0.109375
- norm1_gain: float32 [768], replicated, may hold values from 0.5 to 1.5
- norm1_shift: float32 [768], replicated, may hold values from -3 to 3
- norm2_gain: float32 [768], replicated, may hold values from 0.5 to 1.5
- norm2_shift: float32 [768], replicated, may hold values from -3 to 3
Outputs:
- mixed_out: bfloat16 [32768, 768], P('dp')
- input_grad: bfloat16 [32768, 768], P('dp')
- qkv_grad: float32 [3, 768, 768], P(None, None, 'mp')
- out_weight_grad: float32 [768, 768], P('mp')
- up_grad: float32 [768, 3072], P(None, 'mp')
- down_grad: float32 [3072, 768], P('mp')
- norm1_gain_grad: float32 [768], replicated
- norm1_shift_grad: float32 [768], replicated
- norm2_gain_grad: float32 [768], replicated
- norm2_shift_grad: float32 [768], replicated
Inputs may be any that keep to these rules, and one draw needn't show every extreme that they name: `dest_slot`: a permutation; every group receives 256 pieces, the pieces of one group go to 16 groups, exactly 16 to each. `lengths`: each row sums to 2048.
All inputs are finite; a program needn't handle non-finite values.
Results may differ from a plain program's by a relative error of at most 0.015.
Values may be sent and summed in bfloat16 or wider, within the bound.
A program may use at most 256 MiB of HBM per device.

v0:
```python
import functools

import jax
import jax.numpy as jnp
from jax import lax
from jax.experimental import pallas as pl
from jax.experimental.pallas import tpu as pltpu
from jax.sharding import PartitionSpec as P

HEAD_DIM = 64
PIECE = 8
NORM_EPS = 1e-05
MASKED = -1e30
MIB = 2**20
VMEM = pl.BlockSpec(memory_space=pltpu.VMEM)
SMEM = pl.BlockSpec(memory_space=pltpu.SMEM)
NT = (((1,), (1,)), ((), ()))
TN = (((0,), (0,)), ((), ()))


def params(mib):
    return pltpu.CompilerParams(vmem_limit_bytes=mib * MIB)


def cost(flops, nbytes, transcendentals=0):
    return pl.CostEstimate(
        flops=int(flops), bytes_accessed=int(nbytes), transcendentals=int(transcendentals)
    )


def struct(shape, dtype):
    return jax.ShapeDtypeStruct(shape, dtype)


def dot(a, b, dims=None):
    if dims is None:
        return jnp.dot(a, b, preferred_element_type=jnp.float32)
    return lax.dot_general(a, b, dims, preferred_element_type=jnp.float32)


def norm_unit(values):
    mean = jnp.mean(values, axis=-1, keepdims=True)
    centred = values - mean
    variance = jnp.mean(centred * centred, axis=-1, keepdims=True)
    inverse = lax.rsqrt(variance + NORM_EPS)
    return centred * inverse, inverse


def norm_back(grad_unit, unit, inverse):
    first = jnp.mean(grad_unit, axis=-1, keepdims=True)
    second = jnp.mean(grad_unit * unit, axis=-1, keepdims=True)
    return inverse * (grad_unit - first - unit * second)


def slot_table(chosen, values, capacity):
    per = chosen.shape[1]
    place = lax.broadcasted_iota(jnp.int32, (per, per), 0)
    earlier = place < lax.broadcasted_iota(jnp.int32, (per, per), 1)
    rank = dot(chosen.astype(jnp.bfloat16), earlier.astype(jnp.bfloat16)).astype(jnp.int32)
    rank = jnp.where(chosen, rank, -1)
    ranks = jnp.arange(capacity, dtype=jnp.int32)
    hit = rank[:, None, :] == ranks[None, :, None]
    return jnp.sum(jnp.where(hit, values[:, None, :], 0), axis=2)


def gather_kernel(index_ref, source_ref, out_ref):
    def step(j, carry):
        out_ref[j] = source_ref[index_ref[j]]
        return carry

    lax.fori_loop(0, out_ref.shape[0], step, 0, unroll=8)


def gather_pieces(index, source):
    rows, width = source.shape
    count = index.shape[0]
    out = pl.pallas_call(
        gather_kernel,
        out_shape=struct((count, PIECE, width), source.dtype),
        in_specs=[SMEM, VMEM],
        out_specs=VMEM,
        compiler_params=params(32),
        cost_estimate=cost(0, 3 * rows * width),
        name="gather_pieces",
    )(index, source.reshape(rows // PIECE, PIECE, width))
    return out.reshape(count * PIECE, width)


def split_kernel(own_ref, other_ref, source_ref, own_out, other_out):
    def step(j, carry):
        own_out[j] = source_ref[own_ref[j]]
        other_out[j] = source_ref[other_ref[j]]
        return carry

    lax.fori_loop(0, own_out.shape[0], step, 0, unroll=8)


def split_pieces(own, other, source):
    rows, width = source.shape
    count = own.shape[0]
    outs = pl.pallas_call(
        split_kernel,
        out_shape=[struct((count, PIECE, width), source.dtype)] * 2,
        in_specs=[SMEM, SMEM, VMEM],
        out_specs=[VMEM, VMEM],
        compiler_params=params(32),
        cost_estimate=cost(0, 4 * rows * width),
        name="split_pieces",
    )(own, other, source.reshape(rows // PIECE, PIECE, width))
    return tuple(o.reshape(count * PIECE, width) for o in outs)


def merge_kernel(own_ref, other_ref, own_in, other_in, out_ref):
    def step(j, carry):
        out_ref[own_ref[j]] = own_in[j]
        out_ref[other_ref[j]] = other_in[j]
        return carry

    lax.fori_loop(0, own_in.shape[0], step, 0, unroll=8)


def merge_pieces(own, other, own_rows, other_rows):
    rows, width = own_rows.shape
    out = pl.pallas_call(
        merge_kernel,
        out_shape=struct((2 * rows // PIECE, PIECE, width), own_rows.dtype),
        in_specs=[SMEM, SMEM, VMEM, VMEM],
        out_specs=VMEM,
        compiler_params=params(32),
        cost_estimate=cost(0, 8 * rows * width),
        name="merge_pieces",
    )(
        own,
        other,
        own_rows.reshape(rows // PIECE, PIECE, width),
        other_rows.reshape(rows // PIECE, PIECE, width),
    )
    return out.reshape(2 * rows, width)


def project_kernel(
    own_ref, other_ref, own_in, other_in, gain_ref, shift_ref, w_ref, wt_ref,
    ht_ref, q_ref, k_ref, v_ref, qt_ref, kt_ref, vt_ref, x_all,
):
    @pl.when(pl.program_id(0) == 0)
    def _():
        def step(j, carry):
            x_all[own_ref[j]] = own_in[j]
            x_all[other_ref[j]] = other_in[j]
            return carry

        lax.fori_loop(0, own_in.shape[0], step, 0, unroll=8)

    block, local = q_ref.shape
    pieces = block // PIECE
    x = x_all[pl.ds(pl.program_id(0) * pieces, pieces)].astype(jnp.float32).reshape(block, -1)
    unit, _ = norm_unit(x)
    h = (unit * gain_ref[...] + shift_ref[...]).astype(jnp.bfloat16)
    ht_ref[...] = h.T
    natural = dot(h, w_ref[...]).astype(jnp.bfloat16)
    turned = dot(wt_ref[...], h, NT).astype(jnp.bfloat16)
    for i, (n_ref, t_ref) in enumerate(((q_ref, qt_ref), (k_ref, kt_ref), (v_ref, vt_ref))):
        n_ref[...] = natural[:, i * local : (i + 1) * local]
        t_ref[...] = turned[i * local : (i + 1) * local]


def project(own, other, x_own, x_other, gain, shift, w, wt):
    half, width = x_own.shape
    rows, outs = 2 * half, w.shape[1]
    local = outs // 3
    pieces = half // PIECE
    block = min(256, rows)
    bf16 = jnp.bfloat16

    def whole(shape):
        return pl.BlockSpec(shape, lambda i: (0,) * len(shape), pipeline_mode=pl.Buffered(1))

    natural = pl.BlockSpec((block, local), lambda i: (i, 0))
    turned = pl.BlockSpec((local, block), lambda i: (0, i))
    return pl.pallas_call(
        project_kernel,
        grid=(rows // block,),
        out_shape=[struct((width, rows), bf16)] + [struct((rows, local), bf16)] * 3 + [struct((local, rows), bf16)] * 3,
        in_specs=[SMEM, SMEM]
        + [whole((pieces, PIECE, width))] * 2
        + [whole((1, width))] * 2
        + [whole((width, outs)), whole((outs, width))],
        out_specs=[pl.BlockSpec((width, block), lambda i: (0, i))] + [natural] * 3 + [turned] * 3,
        scratch_shapes=[pltpu.VMEM((rows // PIECE, PIECE, width), bf16)],
        compiler_params=params(40),
        cost_estimate=cost(4 * rows * width * outs, 20e6),
        name="project",
    )(own, other, x_own.reshape(pieces, PIECE, width), x_other.reshape(pieces, PIECE, width), gain, shift, w, wt)


def cell_bounds(len_ref, cnt_ref):
    cells = len_ref.shape[1]
    starts, lives, start = [], [], jnp.int32(0)
    for c in range(cells):
        length = len_ref[0, c]
        starts.append(start)
        lives.append(start + jnp.minimum(length, cnt_ref[0, c]))
        start = start + length
    return starts, lives


def key_range(pos, starts, lives):
    low = jnp.zeros_like(pos) + starts[0]
    high = jnp.zeros_like(pos) + lives[0]
    for start, live in zip(starts[1:], lives[1:]):
        inside = pos >= start
        low = jnp.where(inside, start, low)
        high = jnp.where(inside, live, high)
    return low, high


def attend_kernel(
    own_ref, other_ref, len_ref, cnt_ref, k_ref, qt_ref, vt_ref,
    ot_ref, own_out, other_out, lse_ref,
    natural, bias, top, total, acc,
):
    rows, width = k_ref.shape
    heads = width // HEAD_DIM
    bk, bq = bias.shape
    starts, lives = cell_bounds(len_ref, cnt_ref)
    zeros = jnp.zeros((HEAD_DIM, bq), jnp.bfloat16)
    ones = jnp.ones((16, bk), jnp.bfloat16)

    def query_step(i, carry):
        q0 = pl.multiple_of(i * bq, bq)
        cols = pl.ds(q0, bq)
        low, high = key_range(q0 + lax.broadcasted_iota(jnp.int32, (1, bq), 1), starts, lives)
        first, _ = key_range(q0, starts, lives)
        _, last = key_range(q0 + bq - 1, starts, lives)
        origin = first // 128 * 128
        top[...] = jnp.full_like(top, MASKED)
        total[...] = jnp.zeros_like(total)
        acc[...] = jnp.zeros_like(acc)

        def key_step(j, carry):
            begin = origin + j * bk
            k0 = pl.multiple_of(jnp.minimum(begin, rows - bk), 128)
            keys = pl.ds(k0, bk)
            kpos = k0 + lax.broadcasted_iota(jnp.int32, (bk, bq), 0)
            bias[...] = jnp.where((kpos >= jnp.maximum(low, begin)) & (kpos < high), 0.0, MASKED)

            def score(h):
                lanes = slice(h // 2 * 128, h // 2 * 128 + 128)
                q = qt_ref[h * HEAD_DIM : (h + 1) * HEAD_DIM, cols]
                q = jnp.concatenate([q, zeros] if h % 2 == 0 else [zeros, q], axis=0)
                return dot(k_ref[keys, lanes], q)

            s = [score(0), score(1)]
            ps = {}

            def mix(h):
                p, decay = ps.pop(h)
                sub = slice(h * HEAD_DIM, (h + 1) * HEAD_DIM)
                v = jnp.concatenate([vt_ref[sub, keys], ones], axis=0)
                r = dot(v, p)
                acc[sub, :] = acc[sub, :] * decay + r[:HEAD_DIM]
                total[h : h + 1, :] = total[h : h + 1, :] * decay + r[HEAD_DIM : HEAD_DIM + 1]

            for h in range(heads):
                if h + 2 < heads:
                    s.append(score(h + 2))
                x = s[h] + bias[...]
                old = top[h : h + 1, :]
                new = jnp.maximum(old, jnp.max(x, axis=0, keepdims=True))
                p = jnp.exp(x - new).astype(jnp.bfloat16)
                ps[h] = (p, jnp.exp(old - new))
                top[h : h + 1, :] = new
                if h >= 1:
                    mix(h - 1)
            mix(heads - 1)
            return carry

        lax.fori_loop(0, (last - origin + bk - 1) // bk, key_step, 0)
        for h in range(heads):
            sub = slice(h * HEAD_DIM, (h + 1) * HEAD_DIM)
            acc[sub, :] = acc[sub, :] / total[h : h + 1, :]
            lse_ref[h : h + 1, cols] = top[h : h + 1, :] + jnp.log(total[h : h + 1, :])
        mixed = acc[...]
        ot_ref[:, cols] = mixed.astype(jnp.bfloat16)
        natural[pl.ds(i * (bq // PIECE), bq // PIECE)] = mixed.T.reshape(bq // PIECE, PIECE, width)
        return carry

    lax.fori_loop(0, rows // bq, query_step, 0)

    def step(j, carry):
        own_out[j] = natural[own_ref[j]].astype(jnp.bfloat16)
        other_out[j] = natural[other_ref[j]].astype(jnp.bfloat16)
        return carry

    lax.fori_loop(0, own_out.shape[0], step, 0, unroll=8)


def attend(own, other, lengths, counts, k, qt, vt):
    rows, width = k.shape
    count = own.shape[0]
    bk, bq = min(640, rows), min(256, rows)
    heads = width // HEAD_DIM
    ot, o_own, o_other, lse = pl.pallas_call(
        attend_kernel,
        out_shape=[
            struct((width, rows), jnp.bfloat16),
            struct((count, PIECE, width), jnp.bfloat16),
            struct((count, PIECE, width), jnp.bfloat16),
            struct((8, rows), jnp.float32),
        ],
        in_specs=[SMEM] * 4 + [VMEM] * 3,
        out_specs=[VMEM] * 4,
        scratch_shapes=[
            pltpu.VMEM((rows // PIECE, PIECE, width), jnp.float32),
            pltpu.VMEM((bk, bq), jnp.float32),
            pltpu.VMEM((8, bq), jnp.float32),
            pltpu.VMEM((8, bq), jnp.float32),
            pltpu.VMEM((width, bq), jnp.float32),
        ],
        compiler_params=params(56),
        cost_estimate=cost(2e10, 10e6, heads * rows * rows // 2),
        name="attend",
    )(own, other, lengths, counts, k, qt, vt)
    return ot, o_own.reshape(count * PIECE, width), o_other.reshape(count * PIECE, width), lse


def attend_back_kernel(
    own_ref, other_ref, len_ref, cnt_ref, q_ref, k_ref, v_ref, qt_ref, kt_ref, ot_ref, lse_ref,
    own_in, other_in, out_ref,
    natural, do_t, do_m, q_m, delta, dq_t, dk_acc, dv_acc, bias,
):
    rows, width = k_ref.shape
    heads = width // HEAD_DIM
    bk, bq = bias.shape
    pieces = bq // PIECE
    starts, lives = cell_bounds(len_ref, cnt_ref)
    zeros = jnp.zeros((HEAD_DIM, bq), jnp.bfloat16)

    def place(j, carry):
        natural[own_ref[j]] = own_in[j].astype(jnp.float32)
        natural[other_ref[j]] = other_in[j].astype(jnp.float32)
        return carry

    lax.fori_loop(0, own_in.shape[0], place, 0, unroll=8)
    lane = lax.broadcasted_iota(jnp.int32, (bq, 128), 1)

    def prepare(i, carry):
        q0 = pl.multiple_of(i * bq, bq)
        at = pl.ds(q0, bq)
        do = natural[pl.ds(i * pieces, pieces)].reshape(bq, width)
        dot_t = do.T
        do_t[:, at] = dot_t.astype(jnp.bfloat16)
        for h in range(heads):
            sub = slice(h * HEAD_DIM, (h + 1) * HEAD_DIM)
            delta[h : h + 1, at] = jnp.sum(
                dot_t[sub, :] * ot_ref[sub, at].astype(jnp.float32), axis=0, keepdims=True
            )
            lanes = slice(h // 2 * 128, h // 2 * 128 + 128)
            mine = (lane < HEAD_DIM) if h % 2 == 0 else (lane >= HEAD_DIM)
            do_m[h, at, :] = jnp.where(mine, do[:, lanes], 0.0).astype(jnp.bfloat16)
            q_m[h, at, :] = jnp.where(mine, q_ref[at, lanes].astype(jnp.float32), 0.0).astype(jnp.bfloat16)
        dq_t[:, at] = jnp.zeros((width, bq), jnp.float32)
        return carry

    lax.fori_loop(0, rows // bq, prepare, 0)

    def key_step(j, carry):
        k0 = pl.multiple_of(j * bk, bk)
        keys = pl.ds(k0, bk)
        first, last = jnp.int32(rows), jnp.int32(0)
        for start, live in zip(starts, lives):
            met = (start < k0 + bk) & (live > k0)
            first = jnp.where(met, jnp.minimum(first, start), first)
            last = jnp.where(met, live, last)
        origin = first // 128 * 128
        dk_acc[...] = jnp.zeros_like(dk_acc)
        dv_acc[...] = jnp.zeros_like(dv_acc)

        def query_step(i, carry):
            begin = origin + i * bq
            q0 = pl.multiple_of(jnp.minimum(begin, rows - bq), 128)
            cols = pl.ds(q0, bq)
            qpos = q0 + lax.broadcasted_iota(jnp.int32, (1, bq), 1)
            low, high = key_range(qpos, starts, lives)
            low = jnp.where(qpos < begin, rows, low)
            kpos = k0 + lax.broadcasted_iota(jnp.int32, (bk, bq), 0)
            bias[...] = jnp.where((kpos >= low) & (kpos < high), 0.0, MASKED)

            def first_half(g):
                lanes = slice(g // 2 * 128, g // 2 * 128 + 128)
                sub = slice(g * HEAD_DIM, (g + 1) * HEAD_DIM)
                q, d = qt_ref[sub, cols], do_t[sub, cols]
                order = (lambda t: [t, zeros]) if g % 2 == 0 else (lambda t: [zeros, t])
                s = dot(k_ref[keys, lanes], jnp.concatenate(order(q), axis=0))
                dp = dot(v_ref[keys, lanes], jnp.concatenate(order(d), axis=0))
                return s, dp

            def second_half(g, p, ds):
                lanes = slice(g // 2 * 128, g // 2 * 128 + 128)
                sub = slice(g * HEAD_DIM, (g + 1) * HEAD_DIM)
                dv_acc[:, lanes] += dot(p, do_m[g, cols, :])
                dk_acc[:, lanes] += dot(ds, q_m[g, cols, :])
                dq_t[sub, cols] += dot(kt_ref[sub, keys], ds)

            ready = [first_half(0)]
            last_pair = None
            for g in range(heads):
                if g + 1 < heads:
                    ready.append(first_half(g + 1))
                s, dp = ready[g]
                p = jnp.exp(s + bias[...] - lse_ref[g : g + 1, cols])
                ds = (p * (dp - delta[g : g + 1, cols])).astype(jnp.bfloat16)
                if last_pair is not None:
                    second_half(*last_pair)
                last_pair = (g, p.astype(jnp.bfloat16), ds)
            second_half(*last_pair)
            return carry

        lax.fori_loop(0, (last - origin + bq - 1) // bq, query_step, 0)
        out_ref[1, keys, :] = dk_acc[...].astype(jnp.bfloat16)
        out_ref[2, keys, :] = dv_acc[...].astype(jnp.bfloat16)
        return carry

    lax.fori_loop(0, rows // bk, key_step, 0)

    def finish(i, carry):
        at = pl.ds(pl.multiple_of(i * bq, bq), bq)
        out_ref[0, at, :] = (dq_t[:, at].T * HEAD_DIM**-0.5).astype(jnp.bfloat16)
        return carry

    lax.fori_loop(0, rows // bq, finish, 0)


def attend_back(own, other, lengths, counts, q, k, v, qt, kt, ot, lse, do_own, do_other):
    rows, width = k.shape
    count = own.shape[0]
    bk = bq = min(256, rows)
    heads = width // HEAD_DIM
    return pl.pallas_call(
        attend_back_kernel,
        out_shape=struct((3, rows, width), jnp.bfloat16),
        in_specs=[SMEM] * 4 + [VMEM] * 9,
        out_specs=VMEM,
        scratch_shapes=[
            pltpu.VMEM((rows // PIECE, PIECE, width), jnp.float32),
            pltpu.VMEM((width, rows), jnp.bfloat16),
            pltpu.VMEM((heads, rows, 128), jnp.bfloat16),
            pltpu.VMEM((heads, rows, 128), jnp.bfloat16),
            pltpu.VMEM((8, rows), jnp.float32),
            pltpu.VMEM((width, rows), jnp.float32),
            pltpu.VMEM((bk, width), jnp.float32),
            pltpu.VMEM((bk, width), jnp.float32),
            pltpu.VMEM((bk, bq), jnp.float32),
        ],
        compiler_params=params(58),
        cost_estimate=cost(5e10, 20e6, heads * rows * rows // 2),
        name="attend_back",
    )(
        own, other, lengths, counts, q, k, v, qt, kt, ot, lse,
        do_own.reshape(count, PIECE, width), do_other.reshape(count, PIECE, width),
    )


def feed_kernel(
    x_ref, oa_ref, ob_ref, dy_ref, real_ref, wo_a, wo_b, up_a, up_b, down_a, down_b, gain_ref, shift_ref,
    out_ref, up_left_a, up_left_b, down_left_a, down_left_b, h_ref, right_ref, doa_ref, dob_ref, dy1_ref, norm_ref,
):
    x = x_ref[...].astype(jnp.float32)
    y1 = x + dot(oa_ref[...], wo_a[...]) + dot(ob_ref[...], wo_b[...])
    unit, inverse = norm_unit(y1)
    h = (unit * gain_ref[...] + shift_ref[...]).astype(jnp.bfloat16)
    h_ref[...] = h
    g = dy_ref[...].astype(jnp.float32) * real_ref[...]
    gr = g.astype(jnp.bfloat16)
    right_ref[0] = gr
    mlp = None
    dh = None
    for up, down, up_left, down_left, o_ref in (
        (up_a, down_a, up_left_a, down_left_a, oa_ref),
        (up_b, down_b, up_left_b, down_left_b, ob_ref),
    ):
        hidden = up.shape[1]
        part = min(768, hidden)
        for at in range(0, hidden, part):
            cols = slice(at, at + part)
            u = dot(h, up[:, cols])
            phi = 0.5 * (1.0 + lax.erf(u * 0.7071067811865476))
            act = (u * phi).astype(jnp.bfloat16)
            down_left[:, cols] = act
            slope = phi + u * 0.3989422804014327 * jnp.exp(-0.5 * u * u)
            du = (dot(gr, down[cols, :], NT) * slope).astype(jnp.bfloat16)
            up_left[:, cols] = du
            m = dot(act, down[cols, :])
            d = dot(du, up[:, cols], NT)
            mlp = m if mlp is None else mlp + m
            dh = d if dh is None else dh + d
        local = o_ref.shape[1]
        down_left[:, hidden : hidden + local] = o_ref[...]
        down_left[:, hidden + local :] = jnp.zeros_like(down_left[:, hidden + local :])
    out_ref[...] = (y1 + mlp).astype(jnp.bfloat16)
    sums = jnp.concatenate(
        [jnp.sum(dh * unit, axis=0, keepdims=True), jnp.sum(dh, axis=0, keepdims=True)], axis=0
    )

    @pl.when(pl.program_id(0) == 0)
    def _():
        norm_ref[...] = sums

    @pl.when(pl.program_id(0) > 0)
    def _():
        norm_ref[...] += sums

    dy1 = g + norm_back(dh * gain_ref[...], unit, inverse)
    dy1_ref[...] = dy1
    dar = dy1.astype(jnp.bfloat16)
    right_ref[1] = dar
    doa_ref[...] = dot(dar, wo_a[...], NT).astype(jnp.bfloat16)
    dob_ref[...] = dot(dar, wo_b[...], NT).astype(jnp.bfloat16)


def feed(x, o_own, o_other, dy, real, wo, up, down, gain, shift):
    rows, width = x.shape
    local = o_own.shape[1]
    hidden = up[0].shape[1]
    block = min(256, rows)

    def tall(cols):
        return pl.BlockSpec((block, cols), lambda i: (i, 0))

    def whole(shape):
        return pl.BlockSpec(shape, lambda i: (0, 0), pipeline_mode=pl.Buffered(1))

    bf16 = jnp.bfloat16
    lefts = hidden // 3 * 4
    return pl.pallas_call(
        feed_kernel,
        grid=(rows // block,),
        out_shape=[
            struct((rows, width), bf16),
            struct((rows, hidden), bf16),
            struct((rows, hidden), bf16),
            struct((rows, lefts), bf16),
            struct((rows, lefts), bf16),
            struct((rows, width), bf16),
            struct((2, rows, width), bf16),
            struct((rows, local), bf16),
            struct((rows, local), bf16),
            struct((rows, width), jnp.float32),
            struct((2, width), jnp.float32),
        ],
        in_specs=[tall(width), tall(local), tall(local), tall(width), tall(1)]
        + [whole((local, width))] * 2
        + [whole((width, hidden))] * 2
        + [whole((hidden, width))] * 2
        + [whole((1, width))] * 2,
        out_specs=[
            tall(width),
            tall(hidden),
            tall(hidden),
            tall(lefts),
            tall(lefts),
            tall(width),
            pl.BlockSpec((2, block, width), lambda i: (0, i, 0)),
            tall(local),
            tall(local),
            tall(width),
            pl.BlockSpec((2, width), lambda i: (0, 0)),
        ],
        compiler_params=params(58),
        cost_estimate=cost(2 * rows * width * (hidden * 8 + local * 4), 50e6, rows * hidden * 4),
        name="feed",
    )(x, o_own, o_other, dy, real, *wo, *up, *down, gain, shift)


def weight_kernel(order_ref, left_ref, right_ref, out_ref):
    out_ref[0] = dot(left_ref[...], right_ref[0], TN).astype(jnp.bfloat16)


def weight_add_kernel(order_ref, left_ref, right_ref, more_ref, out_ref):
    out_ref[0] = (dot(left_ref[...], right_ref[0], TN) + more_ref[0].astype(jnp.float32)).astype(jnp.bfloat16)


def weight_grads(left, right, order, more=None):
    rows, lefts = left.shape
    count, _, width = right.shape
    block = lefts // NEAR

    def pick(i, order):
        return (order[i] // (NEAR - 1) if count == 2 else 0, 0, 0)

    out = pl.BlockSpec((1, block, width), lambda i, order: (i, 0, 0))
    operands = (left, right) if more is None else (left, right, more)
    return pl.pallas_call(
        weight_kernel if more is None else weight_add_kernel,
        grid_spec=pltpu.PrefetchScalarGridSpec(
            num_scalar_prefetch=1,
            grid=(NEAR,),
            in_specs=[
                pl.BlockSpec((rows, block), lambda i, order: (0, order[i])),
                pl.BlockSpec((1, rows, width), pick),
            ]
            + ([] if more is None else [pl.BlockSpec((1, block, width), lambda i, order: (order[i], 0, 0))]),
            out_specs=out,
        ),
        out_shape=struct((NEAR, block, width), jnp.bfloat16),
        compiler_params=params(40),
        cost_estimate=cost(2 * rows * width * lefts, 20e6),
        name="weight_grads",
    )(order, *operands)


NEAR = 4
MESH = pl.DeviceIdType.MESH


def padded(rows, size):
    return -(-rows // (16 * size)) * 16 * size


def near_send(block, d, size):
    return lax.ppermute(block, "dp", [(i, i ^ d) for i in range(size)])


def add_up(blocks):
    total = blocks[0].astype(jnp.float32)
    for block in blocks[1:]:
        total = total + block.astype(jnp.float32)
    return total.astype(jnp.bfloat16)


def close_kernel(
    size, own_ref, other_ref, chunk_ref, grads_ref, ht_ref, w_ref, x_ref, dy1_ref, gain_ref, norm2_ref,
    first_out, second_out, rows_own, rows_other, norms_out,
    part, natural, swap_s, swap_r, dx, acc_a, acc_b, land_a, land_b, near_b, sum_b, norm_s, norm_r, norm_t,
    near_sem_s, near_sem_r, far_sem_s, far_sem_r, part_s, part_r, trade_s, trade_r, pass_s, pass_r,
    small_s, small_r, mp_s, mp_r, local,
):
    far = size // NEAR
    bits = [1 << b for b in range(far.bit_length() - 1)]
    me = lax.axis_index("dp")
    core = lax.axis_index("mp")
    f, e = me // NEAR, me % NEAR
    rows_all, local_width = grads_ref.shape[1:]
    width = w_ref.shape[1]
    block = min(256, rows_all)
    bf16 = jnp.bfloat16

    def flip(value, mask, top):
        out, b = 0, 1
        while b < top:
            out = out + b * ((value // b + mask // b) % 2)
            b *= 2
        return out

    barrier = pltpu.get_barrier_semaphore()

    def greet(d, carry):
        pl.semaphore_signal(barrier, inc=1, device_id={"dp": (me + d) % size}, device_id_type=MESH)
        return carry

    lax.fori_loop(1, size, greet, 0)
    pl.semaphore_signal(barrier, inc=1, device_id={"mp": 1 - core}, device_id_type=MESH)
    pl.semaphore_wait(barrier, size)

    def remote(source, target, send, recv, device):
        return pltpu.make_async_remote_copy(
            source, target, send, recv, device_id={"dp": device}, device_id_type=MESH
        )

    def beside(source, target, send, recv):
        return pltpu.make_async_remote_copy(
            source, target, send, recv, device_id={"mp": 1 - core}, device_id_type=MESH
        )

    cut = chunk_ref.shape[1] // 2
    halves = (slice(0, cut), slice(cut, 2 * cut))

    def views(first, second):
        return lambda s, *at: first.at[(*at, halves[s])] if s < 2 else second.at[at]

    inputs, accs = views(chunk_ref, sum_b), views(acc_a, acc_b)
    lands, outs = views(land_a, land_b), views(first_out, second_out)
    held = {b: [m for m in range(far) if m % (2 * b) == 0] for b in bits}
    slot = {}
    for b in bits:
        for m in held[b]:
            slot[b, m] = len(slot)
    arrivals = [(b, m) for b in reversed(bits) for m in held[b]]

    def reduce_copy(s, b, m):
        source = inputs(s, flip(f, m + b, far)) if b == 1 else accs(s, m + b)
        k = slot[b, m]
        return remote(source, lands(s, k), far_sem_s.at[s, k], far_sem_r.at[s, k], flip(f, b, far) * NEAR + e)

    def reduce_start(s, b):
        for m in held[b]:
            reduce_copy(s, b, m).start()

    def reduce_step(s, b):
        for m in held[b]:
            reduce_copy(s, b, m).wait_recv()
            base = inputs(s, flip(f, m, far)) if b == 1 else accs(s, m)
            total = (base[...].astype(jnp.float32) + lands(s, slot[b, m])[...].astype(jnp.float32)).astype(bf16)
            if 2 * b == far:
                outs(s, e, f)[...] = total
            else:
                accs(s, m)[...] = total
        if 2 * b < far:
            reduce_start(s, 2 * b)
        else:
            available(s, 0)

    def spread_copy(s, b, m):
        piece = outs(s, e, flip(f, m, far))
        k = slot[b, m]
        return remote(piece, piece, far_sem_s.at[3 + s, k], far_sem_r.at[3 + s, k], flip(f, b, far) * NEAR + e)

    def spread_arrival(s, b, m):
        piece = outs(s, e, flip(f, m + b, far))
        k = slot[b, m]
        return remote(piece, piece, far_sem_s.at[3 + s, k], far_sem_r.at[3 + s, k], flip(f, b, far) * NEAR + e)

    def near_copy(s, d, m):
        piece = outs(s, e, flip(f, m, far))
        return remote(piece, piece, near_sem_s.at[s, d, m], near_sem_r.at[s, d, m], f * NEAR + flip(e, d, NEAR))

    def near_arrival(s, d, m):
        piece = outs(s, flip(e, d, NEAR), flip(f, m, far))
        return remote(piece, piece, near_sem_s.at[s, d, m], near_sem_r.at[s, d, m], f * NEAR + flip(e, d, NEAR))

    def near_pass(s, m):
        source, to = (1, 2) if m % 2 == 0 else (2, 1)
        piece = outs(s, flip(e, source, NEAR), flip(f, m, far))
        return remote(piece, piece, near_sem_s.at[s, 3, m], near_sem_r.at[s, 3, m], f * NEAR + flip(e, to, NEAR))

    def near_passed(s, m):
        to = 2 if m % 2 == 0 else 1
        piece = outs(s, flip(e, 3, NEAR), flip(f, m, far))
        return remote(piece, piece, near_sem_s.at[s, 3, m], near_sem_r.at[s, 3, m], f * NEAR + flip(e, to, NEAR))

    def available(s, m):
        for b in reversed(bits):
            if m % (2 * b) == 0:
                spread_copy(s, b, m).start()
        for d in (1, 2):
            near_copy(s, d, m).start()

    def arrive(s, b, m):
        spread_arrival(s, b, m).wait_recv()
        available(s, m + b)

    def pass_on(s, m):
        for d in (1, 2):
            near_arrival(s, d, m).wait_recv()
        near_pass(s, m).start()

    share = land_b.shape[1]

    def near_block(index):
        return pl.ds(pl.multiple_of(index * (far * share), 16), far * share)

    def part_copy(d):
        to = flip(e, d, NEAR)
        return remote(part.at[near_block(to)], near_b.at[d], part_s.at[d], part_r.at[d], f * NEAR + to)

    def trade(d):
        to = (me + d) % size
        return remote(dx.at[to], rows_own.at[me], trade_s.at[d], trade_r.at[d], to)

    def trade_arrival(d):
        source = (me - d + size) % size
        return remote(dx.at[source], rows_own.at[source], trade_s.at[d], trade_r.at[d], source)

    def passing(d):
        source = (me - d + size) % size
        return beside(rows_own.at[source], rows_other.at[source], pass_s.at[d], pass_r.at[d])

    def small(d):
        to = (me + d) % size
        return remote(norm_s, norm_r.at[me], small_s.at[d], small_r.at[d], to)

    def small_arrival(d):
        source = (me - d + size) % size
        return remote(norm_s, norm_r.at[source], small_s.at[d], small_r.at[d], source)

    reduce_start(0, 1)
    reduce_start(1, 1)

    tall = width // 4

    def part_step(i, carry):
        for c in range(4):
            value = dot(ht_ref[c * tall : (c + 1) * tall, :], grads_ref[i])
            at = pl.multiple_of(i * width + c * tall, 16)
            part[pl.ds(at, tall), :] = value.astype(bf16)
        return carry

    lax.fori_loop(0, 3, part_step, 0)
    used = 3 * width
    if part.shape[0] > used:
        part[used:, :] = jnp.zeros((part.shape[0] - used, local_width), bf16)
    for d in range(1, NEAR):
        part_copy(d).start()
    reduce_step(0, 1)

    pieces = block // PIECE

    def grad_step(i, carry):
        at = pl.ds(pl.multiple_of(i * block, block), block)
        value = dot(grads_ref[0, at, :], w_ref[0], NT)
        value += dot(grads_ref[1, at, :], w_ref[1], NT)
        value += dot(grads_ref[2, at, :], w_ref[2], NT)
        natural[pl.ds(i * pieces, pieces)] = value.reshape(pieces, PIECE, width)
        return carry

    lax.fori_loop(0, rows_all // block, grad_step, 0)

    def pack(j, carry):
        swap_s[j] = natural[other_ref[j]].astype(bf16)
        return carry

    lax.fori_loop(0, swap_s.shape[0], pack, 0, unroll=8)
    half = beside(swap_s, swap_r, mp_s.at[0], mp_r.at[0])
    half.start()
    reduce_step(1, 1)
    for b in bits[1:]:
        reduce_step(0, b)

    half.wait_recv()
    group_rows = dx.shape[1]
    norm_s[...] = jnp.zeros_like(norm_s)
    norm_s[2:4, :] = norm2_ref[...]
    mine = x_ref.shape[0]
    step_rows = min(256, mine)
    step_pieces = step_rows // PIECE

    def finish_step(i, carry):
        def take(j, inner):
            k = i * step_pieces + j
            natural_own[j] = natural[own_ref[k]] + swap_r[k].astype(jnp.float32)
            return inner

        lax.fori_loop(0, step_pieces, take, 0, unroll=8)
        at = pl.ds(pl.multiple_of(i * step_rows, step_rows), step_rows)
        dh = natural_own[...].reshape(step_rows, width)
        unit, inverse = norm_unit(x_ref[at, :].astype(jnp.float32))
        norm_s[0:1, :] += jnp.sum(dh * unit, axis=0, keepdims=True)
        norm_s[1:2, :] += jnp.sum(dh, axis=0, keepdims=True)
        value = dy1_ref[at, :] + norm_back(dh * gain_ref[...], unit, inverse)
        per_step = step_rows // group_rows
        dx[pl.ds(i * per_step, per_step)] = value.astype(bf16).reshape(per_step, group_rows, width)
        return carry

    natural_own = norm_t
    lax.fori_loop(0, mine // step_rows, finish_step, 0)

    def send(d, carry):
        trade(d).start()
        return carry

    lax.fori_loop(1, size, send, 0)

    def send_small(d, carry):
        small(d).start()
        return carry

    lax.fori_loop(1, size, send_small, 0)
    keep = pltpu.make_async_copy(dx.at[me], rows_own.at[me], local.at[0])
    keep.start()
    keep_small = pltpu.make_async_copy(norm_s, norm_r.at[me], local.at[1])
    keep_small.start()

    for b in bits[1:]:
        reduce_step(1, b)
    for d in range(1, NEAR):
        part_copy(d).wait_recv()
    own_part = part.at[near_block(e)]
    for j in range(far):
        at = slice(j * share, (j + 1) * share)
        total = own_part[at, :].astype(jnp.float32)
        for d in range(1, NEAR):
            total = total + near_b[d, at, :].astype(jnp.float32)
        sum_b[j] = total.astype(bf16)
    reduce_start(2, 1)

    top = bits[-1]
    pass_on(0, 0)
    arrive(0, top, 0)
    pass_on(1, 0)
    reduce_step(2, 1)
    arrive(1, top, 0)
    for b, m in arrivals[1:]:
        arrive(0, b, m)
    for b in bits[1:]:
        reduce_step(2, b)
    for b, m in arrivals[1:]:
        arrive(1, b, m)
    for s in range(2):
        for b, m in arrivals:
            pass_on(s, m + b)
    pass_on(2, 0)
    for b, m in arrivals:
        arrive(2, b, m)
    for b, m in arrivals:
        pass_on(2, m + b)
    keep.wait()
    passing(0).start()

    def settle(d, carry):
        trade_arrival(d).wait_recv()
        passing(d).start()
        return carry

    lax.fori_loop(1, size, settle, 0)
    keep_small.wait()

    def settle_small(d, carry):
        small_arrival(d).wait_recv()
        return carry

    lax.fori_loop(1, size, settle_small, 0)

    def add(g, carry):
        return carry + norm_r[g]

    total = lax.fori_loop(0, size, add, jnp.zeros(norm_s.shape, jnp.float32))
    for d in range(1, size):
        small(d).wait_send()
    norm_s[...] = total
    last = beside(norm_s, norm_r.at[size], mp_s.at[1], mp_r.at[1])
    last.start()
    last.wait()
    norms_out[...] = norm_s[...] + norm_r[size]

    for s in range(3):
        for m in range(far):
            near_passed(s, m).wait_recv()
    half.wait_send()
    for d in range(1, NEAR):
        part_copy(d).wait_send()
    for s in range(3):
        for b in bits:
            for m in held[b]:
                reduce_copy(s, b, m).wait_send()
                spread_copy(s, b, m).wait_send()
        for m in range(far):
            near_copy(s, 1, m).wait_send()
            near_copy(s, 2, m).wait_send()
            near_pass(s, m).wait_send()

    passing(0).wait()

    def close(d, carry):
        trade(d).wait_send()
        passing(d).wait()
        return carry

    lax.fori_loop(1, size, close, 0)


def close(own, other, chunk, grads, ht, w, x, dy1, gain, norm2, size):
    far = size // NEAR
    a, width = chunk.shape
    rows, local = grads.shape[1:]
    b = padded(3 * width, size)
    n = x.shape[0] // size
    bf16, f32 = jnp.bfloat16, jnp.float32
    share_a, share_b = a // far, b // size
    dma = pltpu.SemaphoreType.DMA
    step = min(256, x.shape[0])
    first, second, rows_own, rows_other, norms = pl.pallas_call(
        functools.partial(close_kernel, size),
        out_shape=[
            struct((NEAR, far, share_a, width), bf16),
            struct((NEAR, far, share_b, local), bf16),
            struct((size, n, width), bf16),
            struct((size, n, width), bf16),
            struct((8, width), f32),
        ],
        in_specs=[SMEM, SMEM] + [VMEM] * 8,
        out_specs=[VMEM] * 5,
        scratch_shapes=[
            pltpu.VMEM((b, local), bf16),
            pltpu.VMEM((rows // PIECE, PIECE, width), f32),
            pltpu.VMEM((x.shape[0] // PIECE, PIECE, width), bf16),
            pltpu.VMEM((x.shape[0] // PIECE, PIECE, width), bf16),
            pltpu.VMEM((size, n, width), bf16),
            pltpu.VMEM((far, share_a, width), bf16),
            pltpu.VMEM((far, share_b, local), bf16),
            pltpu.VMEM((far, share_a, width), bf16),
            pltpu.VMEM((far, share_b, local), bf16),
            pltpu.VMEM((NEAR, b // NEAR, local), bf16),
            pltpu.VMEM((far, share_b, local), bf16),
            pltpu.VMEM((8, width), f32),
            pltpu.VMEM((size + 1, 8, width), f32),
            pltpu.VMEM((step // PIECE, PIECE, width), f32),
            dma((3, NEAR, far)),
            dma((3, NEAR, far)),
            dma((6, far)),
            dma((6, far)),
            dma((NEAR,)),
            dma((NEAR,)),
            dma((size,)),
            dma((size,)),
            dma((size,)),
            dma((size,)),
            dma((size,)),
            dma((size,)),
            dma((2,)),
            dma((2,)),
            dma((2,)),
        ],
        compiler_params=pltpu.CompilerParams(
            collective_id=0, has_side_effects=True, vmem_limit_bytes=60 * MIB
        ),
        cost_estimate=cost(8 * rows * width * local, 1e8),
        name="close",
    )(own, other, chunk.reshape(far, share_a, width), grads, ht, w, x, dy1, gain, norm2)
    return (
        first.reshape(NEAR * a, width),
        second.reshape(b, local),
        rows_own.reshape(-1, width),
        rows_other.reshape(-1, width),
        norms,
    )


def widen_kernel(first_ref, second_ref, up_ref, down_ref, out_ref, qkv_ref):
    f32 = jnp.float32
    count = first_ref.shape[0]
    up_rows = up_ref.shape[1] // count
    down_rows = down_ref.shape[0] // (count - 1)
    for e in range(count):
        up_ref[:, e * up_rows : (e + 1) * up_rows] = first_ref[e, :up_rows, :].astype(f32).T
    for e in range(count - 1):
        at = slice(e * down_rows, (e + 1) * down_rows)
        down_ref[at, :] = first_ref[e, up_rows : up_rows + down_rows, :].astype(f32)
    out_ref[...] = first_ref[count - 1, up_rows : up_rows + out_ref.shape[0], :].astype(f32)
    qkv_ref[...] = second_ref[: qkv_ref.shape[0], :].astype(f32)


def widen(first, second, hidden, local, rows):
    width = first.shape[2]
    f32 = jnp.float32
    return pl.pallas_call(
        widen_kernel,
        out_shape=[
            struct((width, hidden), f32),
            struct((hidden, width), f32),
            struct((local, width), f32),
            struct((rows, second.shape[1]), f32),
        ],
        in_specs=[VMEM] * 2,
        out_specs=[VMEM] * 4,
        compiler_params=params(40),
        cost_estimate=cost(0, 22e6),
        name="widen",
    )(first, second)


def swap(value):
    return lax.ppermute(value, "mp", [(0, 1), (1, 0)])


def exchange(value):
    return lax.all_to_all(value, "dp", split_axis=0, concat_axis=0, tiled=True)


def body(
    tokens, out_grad, lengths, counts, dest_slot, qkv_weight, out_weight, up_weight, down_weight,
    norm1_gain, norm1_shift, norm2_gain, norm2_shift,
):
    groups = lax.axis_size("dp")
    me = lax.axis_index("dp")
    core = lax.axis_index("mp")
    rows, width = tokens.shape
    per = rows // PIECE
    capacity = per // groups
    half = capacity // 2
    local = qkv_weight.shape[2]
    bf16 = jnp.bfloat16

    slots = dest_slot.reshape(groups, per)
    my_slots = lax.dynamic_index_in_dim(slots, me, 0, keepdims=True)
    group_ids = jnp.arange(groups, dtype=jnp.int32)[:, None]
    piece_ids = jnp.broadcast_to(jnp.arange(per, dtype=jnp.int32)[None, :], (groups, per))
    source = slot_table(my_slots // per == group_ids, piece_ids, capacity)
    target = slot_table(slots // per == me, slots - me * per, capacity)

    def halves(table):
        own = lax.dynamic_slice_in_dim(table, core * half, half, 1)
        other = lax.dynamic_slice_in_dim(table, (1 - core) * half, half, 1)
        return own.reshape(-1), other.reshape(-1)

    src_own, src_other = halves(source)
    own, other = halves(target)

    x_own = exchange(gather_pieces(src_own, tokens))
    dy_send = gather_pieces(src_own, out_grad)
    scaled = jnp.concatenate(
        [qkv_weight[0] * jnp.asarray(HEAD_DIM**-0.5, bf16), qkv_weight[1], qkv_weight[2]], axis=1
    )
    scaled_t = scaled.T
    wo_other, up_other, down_other = swap(out_weight), swap(up_weight), swap(down_weight)
    gain1, shift1 = norm1_gain[None], norm1_shift[None]
    gain2, shift2 = norm2_gain[None], norm2_shift[None]
    x_own, dy_send, scaled, scaled_t, wo_other, up_other, down_other, own, other, gain1, shift1, gain2, shift2 = (
        lax.optimization_barrier(
            (
                x_own, dy_send, scaled, scaled_t, wo_other, up_other, down_other,
                own, other, gain1, shift1, gain2, shift2,
            )
        )
    )
    wo, up, down = (out_weight, wo_other), (up_weight, up_other), (down_weight, down_other)
    x_other = swap(x_own)

    h1_t, q, k, v, qt, kt, vt = project(own, other, x_own, x_other, gain1, shift1, scaled, scaled_t)

    dy_own = exchange(dy_send)
    ot, o_own, o_send, lse = attend(own, other, lengths, counts, k, qt, vt)
    o_other = swap(o_send)

    place = (own[:, None] * PIECE + jnp.arange(PIECE, dtype=jnp.int32)[None, :]).reshape(-1, 1)
    real, start = jnp.zeros(place.shape, jnp.bool_), jnp.int32(0)
    for c in range(lengths.shape[1]):
        live = start + jnp.minimum(lengths[0, c], counts[0, c])
        real, start = real | ((place >= start) & (place < live)), start + lengths[0, c]
    real = real.astype(jnp.float32)

    out_rows, up_own, up_other_left, down_own, down_other_left, h2, right, do_own, do_send, dy1, norm2 = feed(
        x_own, o_own, o_other, dy_own, real, wo, up, down, gain2, shift2
    )
    do_other = swap(do_send)
    out_back = exchange(out_rows)

    e = me % NEAR
    natural_order = jnp.arange(NEAR, dtype=jnp.int32)
    order = natural_order ^ e
    up_more = swap(weight_grads(up_other_left, h2[None], natural_order))
    down_send = weight_grads(down_other_left, right, natural_order)
    up_blocks = weight_grads(up_own, h2[None], order, up_more)
    down_own, up_blocks = lax.optimization_barrier((down_own, up_blocks))
    up_got = [near_send(up_blocks[d], d, groups) for d in (1, 2)]
    down_blocks = weight_grads(down_own, right, order, swap(down_send))
    down_blocks, do_own, do_other = lax.optimization_barrier((down_blocks, do_own, do_other))
    down_got = [near_send(down_blocks[d], d, groups) for d in (1, 2)]
    both_got = near_send(jnp.concatenate([up_blocks[3], down_blocks[3]], axis=0), 3, groups)
    grads = attend_back(own, other, lengths, counts, q, k, v, qt, kt, ot, lse, do_own, do_other)
    up_got, down_got, both_got, grads, out_back = lax.optimization_barrier(
        (up_got, down_got, both_got, grads, out_back)
    )
    up_rows = up_blocks.shape[1]
    chunk = jnp.concatenate(
        [
            add_up([up_blocks[0], *up_got, both_got[:up_rows]]),
            add_up([down_blocks[0], *down_got, both_got[up_rows:]]),
        ],
        axis=0,
    )
    used = chunk.shape[0]
    chunk = jnp.pad(chunk, ((0, -used % (32 * (groups // NEAR))), (0, 0)))
    weights, qkv_grad, dx_own, dx_other, norms = close(
        own, other, chunk, grads, h1_t, qkv_weight, x_own, dy1, gain1, norm2, groups
    )
    weights, qkv_grad, dx_own, dx_other, norms, out_back = lax.optimization_barrier(
        (weights, qkv_grad, dx_own, dx_other, norms, out_back)
    )
    hidden = up_weight.shape[1]
    up_grad, down_grad, wo_grad, qkv_grad = widen(
        weights.reshape(NEAR, -1, width), qkv_grad, hidden, local, 3 * width
    )
    qkv_grad = qkv_grad.reshape(3, width, local)

    mixed_out = merge_pieces(src_own, src_other, out_back, swap(out_back))
    input_grad = merge_pieces(src_own, src_other, dx_own, dx_other)
    return (
        mixed_out, input_grad, qkv_grad, wo_grad, up_grad, down_grad,
        norms[0], norms[1], norms[2], norms[3],
    )


def solution(mesh):
    in_specs = (
        P("dp", None), P("dp", None), P("dp", None), P("dp", None), P(),
        P(None, None, "mp"), P("mp", None), P(None, "mp"), P("mp", None), P(), P(), P(), P(),
    )
    out_specs = (
        P("dp", None), P("dp", None), P(None, None, "mp"), P("mp", None), P(None, "mp"), P("mp", None),
        P(), P(), P(), P(),
    )
    return jax.shard_map(body, mesh=mesh, in_specs=in_specs, out_specs=out_specs, check_vma=False)
```

profile of v0, /device:TPU:0, one launch (start us, length us, event | category | flops | bytes accessed | tf_op | source)
XLA Modules:
  0.0 438.5 jit_solution(6337539878644479346)
XLA Ops:
  0.6 0.7 reshape.269
  2.6 1.9 copy-done.3
  4.5 1.9 gather_pieces.2
  6.4 8.6 %all-to-all-start = ((bf16[16,64,768]{2,1,0:T(8,128)(2,1)}), bf16[16,64,768]{2,1,0:T(8,128)(2,1)}, u32[]{:S(2)}, u32[]{:S(2)}) async-start(bf16[16,64,768]{2,1,0:T(8,128)(2,1)} %bitcast.2), calls=%async_computation | async-start | bytes 3145728 | tf_op jit(solution)/shard_map/all_to_all | solution.py:1066
  15.7 1.9 gather_pieces.3
  20.1 2.0 fusion.42
  22.1 2.1 collective-permute-done.wo_b
  24.2 25.1 %all-to-all-done = bf16[16,64,768]{2,1,0:T(8,128)(2,1)} async-done(((bf16[16,64,768]{2,1,0:T(8,128)(2,1)}), bf16[16,64,768]{2,1,0:T(8,128)(2,1)}, u32[]{:S(2)}, u32[]{:S(2)}) %all-to-all-start) | async-done | bytes 1572896 | tf_op jit(solution)/shard_map/all_to_all | solution.py:1066
  49.3 2.7 copy.40.w_ref
  52.0 7.7 %all-to-all-start.1 = ((bf16[16,64,768]{2,1,0:T(8,128)(2,1)}), bf16[16,64,768]{2,1,0:T(8,128)(2,1)S(1)}, u32[]{:S(2)}, u32[]{:S(2)}) async-start(bf16[16,64,768]{2,1,0:T(8,128)(2,1)} %bitcast.14), calls=%async_computation.1 | async-start | bytes 3145728 | tf_op jit(solution)/shard_map/all_to_all | solution.py:1066
  59.7 15.4 %project.1 = (bf16[768,2048]{1,0:T(8,128)(2,1)}, bf16[2048,384]{1,0:T(8,128)(2,1)S(1)}, bf16[2048,384]{1,0:T(8,128)(2,1)S(1)}, bf16[2048,384]{1,0:T(8,128)(2,1)S...) custom-call(s32[128]{0:T(128)S(1)} %reshape.275.own_ref, ...), custom_call_target="tpu_custom_call" | custom-call | flops 7247757312 | bytes 20000000 | tf_op jit(solution)/shard_map/project/pallas_call | solution.py:180
  75.1 1.1 copy-done.19
  76.3 1.1 copy-done.20
  77.4 1.2 copy-done.21
  78.6 1.1 copy-done.22
  79.7 1.2 copy-done.23
  80.9 1.1 copy-done.24
  82.1 32.0 %attend.1 = (bf16[384,2048]{1,0:T(8,128)(2,1)}, bf16[128,8,384]{2,1,0:T(8,128)(2,1)}, bf16[128,8,384]{2,1,0:T(8,128)(2,1)}, f32[8,2048]{1,0:T(8,128)}) custom-call(s32[128]{0:T(128)} %copy-done.14, s32[128]{0:T(128)} %copy-done.16, s32[1,4]{1,0:T(1,128)} %len_ref.3, s32[1,4]{1,0:T(1,128)} %cnt_ref.3, bf16[2048,384]{1,0:T(8,128)(2,1)} %copy-done.20, ...), custom_call_target="tpu_custom_call" | custom-call | flops 20000000000 | bytes 10000000 | tf_op jit(solution)/shard_map/attend/pallas_call | solution.py:303
  114.3 0.7 fusion.44
  123.3 1.0 reshape.301.real_ref
  124.3 0.9 copy-done.34
  125.6 35.4 %feed.1 = (bf16[1024,768]{1,0:T(8,128)(2,1)}, bf16[1024,1536]{1,0:T(8,128)(2,1)}, bf16[1024,1536]{1,0:T(8,128)(2,1)}, bf16[1024,2048]{1,0:T(8,128)(2,1)}, bf16[1...) custom-call(bf16[1024,768]{1,0:T(8,128)(2,1)} %bitcast.3.x_ref, ...), custom_call_target="tpu_custom_call" | custom-call | flops 21743271936 | bytes 50000000 | tf_op jit(solution)/shard_map/feed/pallas_call | solution.py:535
  161.1 1.9 copy-done.5
  163.0 2.2 copy-done.17
  165.2 5.9 %weight_grads.6 = bf16[4,512,768]{2,1,0:T(8,128)(2,1)} custom-call(s32[4]{0:T(128)S(1)} %iota.54.order_ref, bf16[1024,2048]{1,0:T(8,128)(2,1)S(1)} %copy-done.17, bf16[2,1024,768]{2,1,0:T(8,128)(2,1)S(1)} %copy-done.5), custom_call_target="tpu_custom_call" | custom-call | flops 3221225472 | bytes 20000000 | tf_op jit(solution)/shard_map/weight_grads/pallas_call | solution.py:593
  171.4 5.1 %weight_grads.4 = bf16[4,384,768]{2,1,0:T(8,128)(2,1)} custom-call(s32[4]{0:T(128)S(1)} %iota.53.order_ref, bf16[1024,1536]{1,0:T(8,128)(2,1)S(1)} %copy-done.18, bf16[1,1024,768]{2,1,0:T(8,128)(2,1)S(1)} %bitcast.65), custom_call_target="tpu_custom_call" | custom-call | flops 2415919104 | bytes 20000000 | tf_op jit(solution)/shard_map/weight_grads/pallas_call | solution.py:593
  177.0 5.3 %all-to-all-start.2 = ((bf16[16,64,768]{2,1,0:T(8,128)(2,1)}), bf16[16,64,768]{2,1,0:T(8,128)(2,1)}, u32[]{:S(2)}, u32[]{:S(2)}) async-start(bf16[16,64,768]{2,1,0:T(8,128)(2,1)} %bitcast.74), calls=%async_computation.2 | async-start | bytes 3145728 | tf_op jit(solution)/shard_map/all_to_all | solution.py:1066
  182.3 1.4 copy-done.10
  183.7 5.9 %weight_grads.5 = bf16[4,384,768]{2,1,0:T(8,128)(2,1)S(1)} custom-call(s32[4]{0:T(128)S(1)} %iota_xor_fusion.order_ref, bf16[1024,1536]{1,0:T(8,128)(2,1)S(1)} %copy-done.7, bf16[1,1024,768]{2,1,0:T(8,128)(2,1)S(1)} %bitcast.66, bf16[4,384,768]{2,1,0:T(8,128)(2,1)} %collective-permute-done.5.more_ref), custom_call_target="tpu_custom_call" | custom-call | flops 2415919104 | bytes 20000000 | tf_op jit(solution)/shard_map/weight_grads/pallas_call | solution.py:593
  189.6 1.1 slice_bitcast_fusion.3
  191.4 1.9 collective-permute-start.6
  193.3 1.5 collective-permute-start.7
  194.8 6.2 %weight_grads.7 = bf16[4,512,768]{2,1,0:T(8,128)(2,1)S(1)} custom-call(s32[4]{0:T(128)S(1)} %iota_xor_fusion.order_ref, bf16[1024,2048]{1,0:T(8,128)(2,1)S(1)} %copy-done.2, bf16[2,1024,768]{2,1,0:T(8,128)(2,1)S(1)} %copy-done.6, bf16[4,512,768]{2,1,0:T(8,128)(2,1)} %collective-permute-done.8.more_ref), custom_call_target="tpu_custom_call" | custom-call | flops 3221225472 | bytes 20000000 | tf_op jit(solution)/shard_map/weight_grads/pallas_call | solution.py:593
  201.0 1.3 slice_bitcast_fusion
  202.9 0.8 collective-permute-start.11
  203.7 1.2 pad_maximum_fusion.1
  204.8 2.1 collective-permute-start.12
  206.9 30.5 %attend_back.1.grads_ref = bf16[3,2048,384]{2,1,0:T(8,128)(2,1)} custom-call(s32[128]{0:T(128)} %copy-done.14, s32[128]{0:T(128)} %copy-done.16, s32[1,4]{1,0:T(1,128)} %len_ref.3, s32[1,4]{1,0:T(1,128)} %cnt_ref.3, bf16[2048,384]{1,0:T(8,128)(2,1)} %copy-done.19, bf16[2048,384]{1,0:T(8,128)(2,1)} %copy-done.20, bf16[2048,384]{1,0:T(8,128)(2,1)} %copy-done.21, ...), custom_call_target="tpu_custom_call" | custom-call | flops 49999998976 | bytes 20000000 | tf_op jit(solution)/shard_map/attend_back/pallas_call | solution.py:439
  237.5 28.6 %collective-permute-done.12 = bf16[896,768]{1,0:T(8,128)(2,1)} collective-permute-done((bf16[896,768]{1,0:T(8,128)(2,1)}, bf16[896,768]{1,0:T(8,128)(2,1)}, u32[]{:S(2)}, u32[]{:S(2)}) %collective-permute-start.12) | collective-permute-done | bytes 1376288 | tf_op jit(solution)/shard_map/ppermute | solution.py:621
  266.1 2.0 fusion.2
  268.1 1.9 fusion.5
  270.0 1.2 pad_maximum_fusion.2
  271.2 150.1 %close.1 = (bf16[4,4,224,768]{3,2,1,0:T(8,128)(2,1)}, bf16[4,4,144,384]{3,2,1,0:T(8,128)(2,1)}, bf16[16,64,768]{2,1,0:T(8,128)(2,1)}, bf16[16,64,768]{2,1,0:T(8,128)(2,1)}, f32[8,768]{1,0:T(8,128)}) custom-call(s32[128]{0:T(128)} %copy-done.14, s32[128]{0:T(128)} %copy-done.16, bf16[4,224,768]{2,1,0:T(8,128)(2,1)} %bitcast.76, ...), custom_call_target="tpu_custom_call" | custom-call | flops 4831838208 | bytes 100000000 | tf_op jit(solution)/shard_map/close/pallas_call | solution.py:971
  421.8 2.6 copy-done.1
  424.4 1.5 copy-done.8
  425.9 5.9 %widen.1 = (f32[768,1536]{1,0:T(8,128)}, f32[1536,768]{1,0:T(8,128)}, f32[384,768]{1,0:T(8,128)}, f32[2304,384]{1,0:T(8,128)}) custom-call(bf16[4,896,768]{2,1,0:T(8,128)(2,1)S(1)} %bitcast.61, bf16[2304,384]{1,0:T(8,128)(2,1)S(1)} %bitcast.64), custom_call_target="tpu_custom_call" | custom-call | bytes 22000000 | tf_op jit(solution)/shard_map/widen/pallas_call | solution.py:1045
  431.8 2.6 merge_pieces.3
  435.0 3.5 merge_pieces.2
  (108 shorter events, 9.0 us)
Async XLA Ops:
  2.6 1.9 copy-start.3
  6.4 9.3 %copy-start.4 = (bf16[2048,768]{1,0:T(8,128)(2,1)S(1)}, bf16[2048,768]{1,0:T(8,128)(2,1)}, u32[]{:S(2)}) copy-start(bf16[2048,768]{1,0:T(8,128)(2,1)} %param.14) | copy-start | bytes 9437188
  6.4 42.9 %all-to-all-start = ((bf16[16,64,768]{2,1,0:T(8,128)(2,1)}), bf16[16,64,768]{2,1,0:T(8,128)(2,1)}, u32[]{:S(2)}, u32[]{:S(2)}) async-start(bf16[16,64,768]{2,1,0:T(8,128)(2,1)} %bitcast.2), calls=%async_computation | async-start | bytes 3145728 | tf_op jit(solution)/shard_map/all_to_all | solution.py:1066
  15.0 9.2 %collective-permute-start.1 = (bf16[768,1536]{1,0:T(8,128)(2,1)}, bf16[768,1536]{1,0:T(8,128)(2,1)}, u32[]{:S(2)}, u32[]{:S(2)}) collective-permute-start(bf16[768,1536]{1,0:T(8,128)(2,1)} %up_a.1), channel_id=1, source_target_pairs={{0,1},{1,0},{2,3},{3,2},{4,5},{5,4},{6,7},{7,6},{8,9},{9,8},{10,11... | collective-permute-start | bytes 7077896 | tf_op jit(solution)/shard_map/ppermute | solution.py:1062
  15.1 9.1 %collective-permute-start.2 = (bf16[1536,768]{1,0:T(8,128)(2,1)}, bf16[1536,768]{1,0:T(8,128)(2,1)}, u32[]{:S(2)}, u32[]{:S(2)}) collective-permute-start(bf16[1536,768]{1,0:T(8,128)(2,1)} %down_a.1), channel_id=1, source_target_pairs={{0,1},{1,0},{2,3},{3,2},{4,5},{5,4},{6,7},{7,6},{8,9},{9,8},{10,11... | collective-permute-start | bytes 7077896 | tf_op jit(solution)/shard_map/ppermute | solution.py:1062
  15.6 8.6 %collective-permute-start = (bf16[384,768]{1,0:T(8,128)(2,1)}, bf16[384,768]{1,0:T(8,128)(2,1)}, u32[]{:S(2)}, u32[]{:S(2)}) collective-permute-start(bf16[384,768]{1,0:T(8,128)(2,1)} %wo_a.1), channel_id=1, source_target_pairs={{0,1},{1,0},{2,3},{3,2},{4,5},{5,4},{6,7},{7,6},{8,9},{9,8},{10,11... | collective-permute-start | bytes 1769480 | tf_op jit(solution)/shard_map/ppermute | solution.py:1062
  15.7 1.9 copy-start.25
  17.8 1.6 copy-start.33
  18.7 41.0 %copy-start.14 = (s32[128]{0:T(128)}, s32[128]{0:T(128)S(1)}, u32[]{:S(2)}) copy-start(s32[128]{0:T(128)S(1)} %reshape.275.own_ref) | copy-start | bytes 1540
  18.8 40.9 %copy-start.16 = (s32[128]{0:T(128)}, s32[128]{0:T(128)S(1)}, u32[]{:S(2)}) copy-start(s32[128]{0:T(128)S(1)} %reshape.276.other_ref) | copy-start | bytes 1540
  18.8 40.9 %copy-start.13 = (f32[1,768]{1,0:T(1,128)}, f32[1,768]{1,0:T(1,128)S(1)}, u32[]{:S(2)}) copy-start(f32[1,768]{1,0:T(1,128)S(1)} %broadcast_in_dim.52.gain_ref) | copy-start | bytes 9220
  49.3 10.4 %collective-permute-start.3 = (bf16[1024,768]{1,0:T(8,128)(2,1)}, bf16[1024,768]{1,0:T(8,128)(2,1)}, u32[]{:S(2)}, u32[]{:S(2)}) collective-permute-start(bf16[1024,768]{1,0:T(8,128)(2,1)} %bitcast.3.x_ref), channel_id=1, source_target_pairs={{0,1},{1,0},{2,3},{3,2},{4,5},{5,4},{6,7},{7,6},{8,9},{9,8},{10,11... | collective-permute-start | bytes 4718600 | tf_op jit(solution)/shard_map/ppermute | solution.py:1062
  52.0 72.2 %all-to-all-start.1 = ((bf16[16,64,768]{2,1,0:T(8,128)(2,1)}), bf16[16,64,768]{2,1,0:T(8,128)(2,1)S(1)}, u32[]{:S(2)}, u32[]{:S(2)}) async-start(bf16[16,64,768]{2,1,0:T(8,128)(2,1)} %bitcast.14), calls=%async_computation.1 | async-start | bytes 3145728 | tf_op jit(solution)/shard_map/all_to_all | solution.py:1066
  75.1 1.1 copy-start.19
  76.3 1.1 copy-start.20
  77.4 1.2 copy-start.21
  78.6 1.1 copy-start.22
  79.7 1.2 copy-start.23
  80.9 1.1 copy-start.24
  82.1 32.2 %copy-start.27 = (s32[1,4]{1,0:T(1,128)S(1)}, s32[1,4]{1,0:T(1,128)}, u32[]{:S(2)}) copy-start(s32[1,4]{1,0:T(1,128)} %len_ref.3) | copy-start | bytes 52
  82.1 32.2 %copy-start.28 = (s32[1,4]{1,0:T(1,128)S(1)}, s32[1,4]{1,0:T(1,128)}, u32[]{:S(2)}) copy-start(s32[1,4]{1,0:T(1,128)} %cnt_ref.3) | copy-start | bytes 52
  82.1 40.4 %copy-start.15 = (s32[128]{0:T(128)S(1)}, s32[128]{0:T(128)}, u32[]{:S(2)}) copy-start(s32[128]{0:T(128)} %copy-done.14) | copy-start | bytes 1540
  114.0 10.2 %collective-permute-start.4 = (bf16[1024,384]{1,0:T(8,128)(2,1)}, bf16[1024,384]{1,0:T(8,128)(2,1)S(1)}, u32[]{:S(2)}, u32[]{:S(2)}) collective-permute-start(bf16[1024,384]{1,0:T(8,128)(2,1)} %bitcast.79), channel_id=1, source_target_pairs={{0,1},{1,0},{2,3},{3,2},{4,5},{5,4},{6,7},{7,6},{8,9},{9,8},{10,11... | collective-permute-start | bytes 2359304 | tf_op jit(solution)/shard_map/ppermute | solution.py:1062
  124.3 1.4 copy-start.26
  161.1 1.9 copy-start.5
  163.0 2.2 copy-start.17
  165.2 6.2 %copy-start.9 = (bf16[1024,768]{1,0:T(8,128)(2,1)S(1)}, bf16[1024,768]{1,0:T(8,128)(2,1)}, u32[]{:S(2)}) copy-start(bf16[1024,768]{1,0:T(8,128)(2,1)} %get-tuple-element.92) | copy-start | bytes 4718596
  165.2 6.2 %copy-start.18 = (bf16[1024,1536]{1,0:T(8,128)(2,1)S(1)}, bf16[1024,1536]{1,0:T(8,128)(2,1)}, u32[]{:S(2)}) copy-start(bf16[1024,1536]{1,0:T(8,128)(2,1)} %get-tuple-element.93.left_ref) | copy-start | bytes 9437188
  171.1 23.6 %collective-permute-start.8 = (bf16[4,512,768]{2,1,0:T(8,128)(2,1)}, bf16[4,512,768]{2,1,0:T(8,128)(2,1)}, u32[]{:S(2)}, u32[]{:S(2)}) collective-permute-start(bf16[4,512,768]{2,1,0:T(8,128)(2,1)} %weight_grads.6), channel_id=1, source_target_pairs={{0,1},{1,0},{2,3},{3,2},{4,5},{5,4},{6,7},{7,6},{8,9},{9,8},{10,11... | collective-permute-start | bytes 9437192 | tf_op jit(solution)/shard_map/ppermute | solution.py:1062
  176.5 5.8 %copy-start.7 = (bf16[1024,1536]{1,0:T(8,128)(2,1)S(1)}, bf16[1024,1536]{1,0:T(8,128)(2,1)}, u32[]{:S(2)}) copy-start(bf16[1024,1536]{1,0:T(8,128)(2,1)} %get-tuple-element.91.left_ref) | copy-start | bytes 9437188
  176.5 5.8 %collective-permute-start.5 = (bf16[4,384,768]{2,1,0:T(8,128)(2,1)}, bf16[4,384,768]{2,1,0:T(8,128)(2,1)}, u32[]{:S(2)}, u32[]{:S(2)}) collective-permute-start(bf16[4,384,768]{2,1,0:T(8,128)(2,1)} %weight_grads.4), channel_id=1, source_target_pairs={{0,1},{1,0},{2,3},{3,2},{4,5},{5,4},{6,7},{7,6},{8,9},{9,8},{10,11... | collective-permute-start | bytes 7077896 | tf_op jit(solution)/shard_map/ppermute | solution.py:1062
  176.8 24.2 %collective-permute-start.9 = (bf16[1024,384]{1,0:T(8,128)(2,1)}, bf16[1024,384]{1,0:T(8,128)(2,1)}, u32[]{:S(2)}, u32[]{:S(2)}) collective-permute-start(bf16[1024,384]{1,0:T(8,128)(2,1)} %get-tuple-element.99), channel_id=1, source_target_pairs={{0,1},{1,0},{2,3},{3,2},{4,5},{5,4},{6,7},{7,6},{8,9},{9,8},{10,11... | collective-permute-start | bytes 2359304 | tf_op jit(solution)/shard_map/ppermute | solution.py:1062
  177.0 60.4 %all-to-all-start.2 = ((bf16[16,64,768]{2,1,0:T(8,128)(2,1)}), bf16[16,64,768]{2,1,0:T(8,128)(2,1)}, u32[]{:S(2)}, u32[]{:S(2)}) async-start(bf16[16,64,768]{2,1,0:T(8,128)(2,1)} %bitcast.74), calls=%async_computation.2 | async-start | bytes 3145728 | tf_op jit(solution)/shard_map/all_to_all | solution.py:1066
  182.3 1.4 copy-start.10
  183.7 11.0 %copy-start.2 = (bf16[1024,2048]{1,0:T(8,128)(2,1)S(1)}, bf16[1024,2048]{1,0:T(8,128)(2,1)}, u32[]{:S(2)}) copy-start(bf16[1024,2048]{1,0:T(8,128)(2,1)} %get-tuple-element.95.left_ref) | copy-start | bytes 12582916
  189.6 1.8 copy-start
  189.6 5.1 %copy-start.6 = (bf16[2,1024,768]{2,1,0:T(8,128)(2,1)S(1)}, bf16[2,1024,768]{2,1,0:T(8,128)(2,1)}, u32[]{:S(2)}) copy-start(bf16[2,1024,768]{2,1,0:T(8,128)(2,1)} %get-tuple-element.96.right_ref) | copy-start | bytes 9437188
  191.4 46.0 %collective-permute-start.6 = (bf16[384,768]{1,0:T(8,128)(2,1)}, bf16[384,768]{1,0:T(8,128)(2,1)}, u32[]{:S(2)}, u32[]{:S(2)}) collective-permute-start(bf16[384,768]{1,0:T(8,128)(2,1)} %get-tuple-element.143), channel_id=1, source_target_pairs={{0,2},{2,0},{4,6},{6,4},{8,10},{10,8},{12,14},{14,12},{16,18},{18,... | collective-permute-start | bytes 1769480 | tf_op jit(solution)/shard_map/ppermute | solution.py:621
  193.3 44.2 %collective-permute-start.7 = (bf16[384,768]{1,0:T(8,128)(2,1)}, bf16[384,768]{1,0:T(8,128)(2,1)}, u32[]{:S(2)}, u32[]{:S(2)}) collective-permute-start(bf16[384,768]{1,0:T(8,128)(2,1)} %get-tuple-element.142), channel_id=1, source_target_pairs={{0,4},{2,6},{4,0},{6,2},{8,12},{10,14},{12,8},{14,10},{16,20},{18,... | collective-permute-start | bytes 1769480 | tf_op jit(solution)/shard_map/ppermute | solution.py:621
  202.3 35.2 %collective-permute-start.10 = (bf16[512,768]{1,0:T(8,128)(2,1)}, bf16[512,768]{1,0:T(8,128)(2,1)}, u32[]{:S(2)}, u32[]{:S(2)}) collective-permute-start(bf16[512,768]{1,0:T(8,128)(2,1)} %get-tuple-element.140), channel_id=1, source_target_pairs={{0,2},{2,0},{4,6},{6,4},{8,10},{10,8},{12,14},{14,12},{16,18},{18,... | collective-permute-start | bytes 2359304 | tf_op jit(solution)/shard_map/ppermute | solution.py:621
  202.9 34.6 %collective-permute-start.11 = (bf16[512,768]{1,0:T(8,128)(2,1)}, bf16[512,768]{1,0:T(8,128)(2,1)}, u32[]{:S(2)}, u32[]{:S(2)}) collective-permute-start(bf16[512,768]{1,0:T(8,128)(2,1)} %get-tuple-element.139), channel_id=1, source_target_pairs={{0,4},{2,6},{4,0},{6,2},{8,12},{10,14},{12,8},{14,10},{16,20},{18,... | collective-permute-start | bytes 2359304 | tf_op jit(solution)/shard_map/ppermute | solution.py:621
  204.8 61.3 %collective-permute-start.12 = (bf16[896,768]{1,0:T(8,128)(2,1)}, bf16[896,768]{1,0:T(8,128)(2,1)}, u32[]{:S(2)}, u32[]{:S(2)}) collective-permute-start(bf16[896,768]{1,0:T(8,128)(2,1)} %pad_maximum_fusion.1), channel_id=1, source_target_pairs={{0,6},{2,4},{4,2},{6,0},{8,14},{10,12},{12,10},{14,8},{16,22},{18,... | collective-permute-start | bytes 4128776 | tf_op jit(solution)/shard_map/ppermute | solution.py:621
  421.3 13.7 %collective-permute-start.13 = (bf16[1024,768]{1,0:T(8,128)(2,1)}, bf16[1024,768]{1,0:T(8,128)(2,1)S(1)}, u32[]{:S(2)}, u32[]{:S(2)}) collective-permute-start(bf16[1024,768]{1,0:T(8,128)(2,1)} %bitcast.34), channel_id=1, source_target_pairs={{0,1},{1,0},{2,3},{3,2},{4,5},{5,4},{6,7},{7,6},{8,9},{9,8},{10,11... | collective-permute-start | bytes 4718600 | tf_op jit(solution)/shard_map/ppermute | solution.py:1062
  421.8 2.6 copy-start.1
  424.4 1.5 copy-start.8
  425.9 5.9 %copy-start.11 = (bf16[16,64,768]{2,1,0:T(8,128)(2,1)S(1)}, bf16[16,64,768]{2,1,0:T(8,128)(2,1)}, u32[]{:S(2)}) copy-start(bf16[16,64,768]{2,1,0:T(8,128)(2,1)} %get-tuple-element.120) | copy-start | bytes 4718596
  425.9 5.9 %copy-start.12 = (bf16[16,64,768]{2,1,0:T(8,128)(2,1)S(1)}, bf16[16,64,768]{2,1,0:T(8,128)(2,1)}, u32[]{:S(2)}) copy-start(bf16[16,64,768]{2,1,0:T(8,128)(2,1)} %get-tuple-element.121) | copy-start | bytes 4718596
  431.8 2.6 copy-start.29
  (4 other events, 4.0 us)
where the time goes:
time: 443 us; the launch traced here: 439 us
  Pallas kernels  302 us (68%)
  waiting for transfers between devices  55.8 us (13%)
  local copies, waits for them, and re-layouts  31.3 us (7%)
  starting transfers between devices  30.5 us (7%)
  other arithmetic  9.66 us (2%)
  between operations  8.63 us (2%)
    pallas_call x1, Pallas kernels, close(): pl.pallas_call(functools.partial(close_kernel, size), out_shape=[struct((...  150 us
    pallas_call x1, Pallas kernels, feed(): pl.pallas_call(feed_kernel, grid=(rows // block,), out_shape=[struct((row...  35.4 us
    pallas_call x1, Pallas kernels, attend(): pl.pallas_call(attend_kernel, out_shape=[struct((width, rows), jnp.bfloat...  32 us
    pallas_call x1, Pallas kernels, attend_back(): pl.pallas_call(attend_back_kernel, out_shape=struct((3, rows, width), jnp...  30.5 us
    ppermute x5, waiting for transfers between devices, near_send(): return lax.ppermute(block, 'dp', [(i, i ^ d) for i in range(size)])  28.7 us
    all_to_all x3, waiting for transfers between devices, exchange(): return lax.all_to_all(value, 'dp', split_axis=0, concat_axis=0, tiled=True)  25.1 us
    pallas_call x4, Pallas kernels, weight_grads(): pl.pallas_call(weight_kernel if more is None else weight_add_kernel, grid...  23.1 us
    all_to_all x3, starting transfers between devices, exchange(): return lax.all_to_all(value, 'dp', split_axis=0, concat_axis=0, tiled=True)  21.5 us
  transfers between devices with their start and end apart: 17, of which 3 were waited for; matrix products, arithmetic and copies ran while one was open for 3% of the time, Pallas kernels for 24%

commit v1 on v0

--- a/solution.py
+++ b/solution.py
@@ -14,6 +14,9 @@
 MIB = 2**20
 VMEM = pl.BlockSpec(memory_space=pltpu.VMEM)
 SMEM = pl.BlockSpec(memory_space=pltpu.SMEM)
+NEAR = 4
+MESH = pl.DeviceIdType.MESH
+ANYWHERE = pl.BlockSpec(memory_space=pl.ANY)
 NT = (((1,), (1,)), ((), ()))
 TN = (((0,), (0,)), ((), ()))
 
@@ -79,7 +82,7 @@
         out_shape=struct((count, PIECE, width), source.dtype),
         in_specs=[SMEM, VMEM],
         out_specs=VMEM,
-        compiler_params=params(32),
+        compiler_params=params(60),
         cost_estimate=cost(0, 3 * rows * width),
         name="gather_pieces",
     )(index, source.reshape(rows // PIECE, PIECE, width))
@@ -103,7 +106,7 @@
         out_shape=[struct((count, PIECE, width), source.dtype)] * 2,
         in_specs=[SMEM, SMEM, VMEM],
         out_specs=[VMEM, VMEM],
-        compiler_params=params(32),
+        compiler_params=params(60),
         cost_estimate=cost(0, 4 * rows * width),
         name="split_pieces",
     )(own, other, source.reshape(rows // PIECE, PIECE, width))
@@ -126,7 +129,7 @@
         out_shape=struct((2 * rows // PIECE, PIECE, width), own_rows.dtype),
         in_specs=[SMEM, SMEM, VMEM, VMEM],
         out_specs=VMEM,
-        compiler_params=params(32),
+        compiler_params=params(60),
         cost_estimate=cost(0, 8 * rows * width),
         name="merge_pieces",
     )(
@@ -157,17 +160,16 @@
     unit, _ = norm_unit(x)
     h = (unit * gain_ref[...] + shift_ref[...]).astype(jnp.bfloat16)
     ht_ref[...] = h.T
-    natural = dot(h, w_ref[...]).astype(jnp.bfloat16)
-    turned = dot(wt_ref[...], h, NT).astype(jnp.bfloat16)
     for i, (n_ref, t_ref) in enumerate(((q_ref, qt_ref), (k_ref, kt_ref), (v_ref, vt_ref))):
-        n_ref[...] = natural[:, i * local : (i + 1) * local]
-        t_ref[...] = turned[i * local : (i + 1) * local]
+        scale = HEAD_DIM**-0.5 if i == 0 else 1.0
+        n_ref[...] = (dot(h, w_ref[i]) * scale).astype(jnp.bfloat16)
+        t_ref[...] = (dot(wt_ref[i], h, NT) * scale).astype(jnp.bfloat16)
 
 
 def project(own, other, x_own, x_other, gain, shift, w, wt):
     half, width = x_own.shape
-    rows, outs = 2 * half, w.shape[1]
-    local = outs // 3
+    rows, local = 2 * half, w.shape[2]
+    outs = 3 * local
     pieces = half // PIECE
     block = min(256, rows)
     bf16 = jnp.bfloat16
@@ -184,10 +186,10 @@
         in_specs=[SMEM, SMEM]
         + [whole((pieces, PIECE, width))] * 2
         + [whole((1, width))] * 2
-        + [whole((width, outs)), whole((outs, width))],
+        + [whole(w.shape), whole(wt.shape)],
         out_specs=[pl.BlockSpec((width, block), lambda i: (0, i))] + [natural] * 3 + [turned] * 3,
         scratch_shapes=[pltpu.VMEM((rows // PIECE, PIECE, width), bf16)],
-        compiler_params=params(40),
+        compiler_params=params(60),
         cost_estimate=cost(4 * rows * width * outs, 20e6),
         name="project",
     )(own, other, x_own.reshape(pieces, PIECE, width), x_other.reshape(pieces, PIECE, width), gain, shift, w, wt)
@@ -214,11 +216,20 @@
     return low, high
 
 
+def load_all(sems, *pairs):
+    loads = [pltpu.make_async_copy(source, target, sems.at[i]) for i, (source, target) in enumerate(pairs)]
+    for one in loads:
+        one.start()
+    for one in loads:
+        one.wait()
+
+
 def attend_kernel(
-    own_ref, other_ref, len_ref, cnt_ref, k_ref, qt_ref, vt_ref,
+    own_ref, other_ref, len_ref, cnt_ref, k_in, qt_in, vt_in,
     ot_ref, own_out, other_out, lse_ref,
-    natural, bias, top, total, acc,
+    k_ref, qt_ref, vt_ref, natural, bias, top, total, acc, load,
 ):
+    load_all(load, (k_in, k_ref), (qt_in, qt_ref), (vt_in, vt_ref))
     rows, width = k_ref.shape
     heads = width // HEAD_DIM
     bk, bq = bias.shape
@@ -308,16 +319,18 @@
             struct((count, PIECE, width), jnp.bfloat16),
             struct((8, rows), jnp.float32),
         ],
-        in_specs=[SMEM] * 4 + [VMEM] * 3,
+        in_specs=[SMEM] * 4 + [ANYWHERE] * 3,
         out_specs=[VMEM] * 4,
         scratch_shapes=[
+            *[pltpu.VMEM(one.shape, one.dtype) for one in (k, qt, vt)],
             pltpu.VMEM((rows // PIECE, PIECE, width), jnp.float32),
             pltpu.VMEM((bk, bq), jnp.float32),
             pltpu.VMEM((8, bq), jnp.float32),
             pltpu.VMEM((8, bq), jnp.float32),
             pltpu.VMEM((width, bq), jnp.float32),
+            pltpu.SemaphoreType.DMA((3,)),
         ],
-        compiler_params=params(56),
+        compiler_params=params(60),
         cost_estimate=cost(2e10, 10e6, heads * rows * rows // 2),
         name="attend",
     )(own, other, lengths, counts, k, qt, vt)
@@ -325,10 +338,14 @@
 
 
 def attend_back_kernel(
-    own_ref, other_ref, len_ref, cnt_ref, q_ref, k_ref, v_ref, qt_ref, kt_ref, ot_ref, lse_ref,
-    own_in, other_in, out_ref,
-    natural, do_t, do_m, q_m, delta, dq_t, dk_acc, dv_acc, bias,
+    own_ref, other_ref, len_ref, cnt_ref, q_in, k_in, v_in, qt_in, kt_in, ot_in, lse_in,
+    do_own, do_other, out_ref,
+    own_in, other_in, q_ref, ot_ref, k_ref, v_ref, qt_ref, kt_ref, lse_ref, natural, do_t, do_m, q_m, delta, dq_t, dk_acc, dv_acc, bias, load,
 ):
+    load_all(
+        load, (do_own, own_in), (do_other, other_in), (q_in, q_ref), (ot_in, ot_ref),
+        (k_in, k_ref), (v_in, v_ref), (qt_in, qt_ref), (kt_in, kt_ref), (lse_in, lse_ref),
+    )
     rows, width = k_ref.shape
     heads = width // HEAD_DIM
     bk, bq = bias.shape
@@ -439,9 +456,11 @@
     return pl.pallas_call(
         attend_back_kernel,
         out_shape=struct((3, rows, width), jnp.bfloat16),
-        in_specs=[SMEM] * 4 + [VMEM] * 9,
+        in_specs=[SMEM] * 4 + [ANYWHERE] * 9,
         out_specs=VMEM,
         scratch_shapes=[
+            *[pltpu.VMEM((count, PIECE, width), jnp.bfloat16)] * 2,
+            *[pltpu.VMEM(one.shape, one.dtype) for one in (q, ot, k, v, qt, kt, lse)],
             pltpu.VMEM((rows // PIECE, PIECE, width), jnp.float32),
             pltpu.VMEM((width, rows), jnp.bfloat16),
             pltpu.VMEM((heads, rows, 128), jnp.bfloat16),
@@ -451,8 +470,9 @@
             pltpu.VMEM((bk, width), jnp.float32),
             pltpu.VMEM((bk, width), jnp.float32),
             pltpu.VMEM((bk, bq), jnp.float32),
+            pltpu.SemaphoreType.DMA((9,)),
         ],
-        compiler_params=params(58),
+        compiler_params=params(60),
         cost_estimate=cost(5e10, 20e6, heads * rows * rows // 2),
         name="attend_back",
     )(
@@ -462,23 +482,23 @@
 
 
 def feed_kernel(
-    x_ref, oa_ref, ob_ref, dy_ref, real_ref, wo_a, wo_b, up_a, up_b, down_a, down_b, gain_ref, shift_ref,
-    out_ref, up_left_a, up_left_b, down_left_a, down_left_b, h_ref, right_ref, doa_ref, dob_ref, dy1_ref, norm_ref,
+    x_ref, oa_ref, ob_ref, dy_ref, real_ref, gain_ref, shift_ref, *refs,
 ):
+    weights, (out_ref, y1_ref, gr_ref, act_a, act_b, slope_a, slope_b), held = refs[:6], refs[6:13], refs[13:19]
+    wo_a, wo_b, up_a, down_a, up_b, down_b = held
+    ready = resident([pltpu.make_async_copy(w, h, refs[19].at[i]) for i, (w, h) in enumerate(zip(weights, held))])
+    ready(0)
+    ready(1)
     x = x_ref[...].astype(jnp.float32)
     y1 = x + dot(oa_ref[...], wo_a[...]) + dot(ob_ref[...], wo_b[...])
-    unit, inverse = norm_unit(y1)
+    y1_ref[...] = y1
+    unit, _ = norm_unit(y1)
     h = (unit * gain_ref[...] + shift_ref[...]).astype(jnp.bfloat16)
-    h_ref[...] = h
-    g = dy_ref[...].astype(jnp.float32) * real_ref[...]
-    gr = g.astype(jnp.bfloat16)
-    right_ref[0] = gr
+    gr_ref[...] = (dy_ref[...].astype(jnp.float32) * real_ref[...]).astype(jnp.bfloat16)
     mlp = None
-    dh = None
-    for up, down, up_left, down_left, o_ref in (
-        (up_a, down_a, up_left_a, down_left_a, oa_ref),
-        (up_b, down_b, up_left_b, down_left_b, ob_ref),
-    ):
+    for n, up, down, act_ref, slope_ref in ((2, up_a, down_a, act_a, slope_a), (4, up_b, down_b, act_b, slope_b)):
+        ready(n)
+        ready(n + 1)
         hidden = up.shape[1]
         part = min(768, hidden)
         for at in range(0, hidden, part):
@@ -486,18 +506,95 @@
             u = dot(h, up[:, cols])
             phi = 0.5 * (1.0 + lax.erf(u * 0.7071067811865476))
             act = (u * phi).astype(jnp.bfloat16)
-            down_left[:, cols] = act
-            slope = phi + u * 0.3989422804014327 * jnp.exp(-0.5 * u * u)
+            act_ref[:, cols] = act
+            slope_ref[:, cols] = (phi + u * 0.3989422804014327 * jnp.exp(-0.5 * u * u)).astype(jnp.bfloat16)
+            m = dot(act, down[cols, :])
+            mlp = m if mlp is None else mlp + m
+    out_ref[...] = (y1 + mlp).astype(jnp.bfloat16)
+
+
+def feed_back_kernel(
+    y1_ref, gr_ref, slope_a, slope_b, oa_ref, ob_ref, gain_ref, shift_ref, blocks_ref, *refs,
+):
+    weights, (left_a, left_b, right_ref, doa_ref, dob_ref, dy1_ref, norm_ref, sum_ref) = refs[:6], refs[6:14]
+    held = refs[14:20]
+    load, sent, got, more, send_sem, recv_sem = refs[20:]
+    wo_a, wo_b, up_a, down_a, up_b, down_b = held
+    loads = [pltpu.make_async_copy(w, h, load.at[i]) for i, (w, h) in enumerate(zip(weights, held))]
+    loads.append(pltpu.make_async_copy(blocks_ref, sent, load.at[6]))
+    ready = resident(loads)
+    me = lax.axis_index("dp")
+    e = me % NEAR
+    step = pl.program_id(0)
+    last = pl.num_programs(0) - 1
+    cut = sum_ref.shape[0] // 2
+    first, second = slice(0, cut), slice(cut, 2 * cut)
+
+    def flip(d):
+        return (e // 2 + d // 2) % 2 * 2 + (e % 2 + d % 2) % 2
+
+    def trade(n):
+        source, d = (
+            (sent.at[flip(1), first], 1),
+            (sent.at[flip(3), first], 1),
+            (sent.at[flip(2), second], 2),
+            (sent.at[flip(3), second], 2),
+            (more.at[0], 2),
+            (more.at[1], 1),
+        )[n]
+        return pltpu.make_async_remote_copy(
+            source, got.at[n], send_sem.at[n], recv_sem.at[n],
+            device_id={"dp": me // NEAR * NEAR + flip(d)}, device_id_type=MESH,
+        )
+
+    @pl.when(step == 0)
+    def _():
+        barrier = pltpu.get_barrier_semaphore()
+        for d in (1, 2):
+            to = me // NEAR * NEAR + flip(d)
+            pl.semaphore_signal(barrier, inc=1, device_id={"dp": to}, device_id_type=MESH)
+        pl.semaphore_wait(barrier, 2)
+
+    ready(6)
+
+    @pl.when(step == 0)
+    def _():
+        for n in (1, 3, 0, 2):
+            trade(n).start()
+
+    def second_trades():
+        @pl.when(step == jnp.maximum(last - 1, 0))
+        def _():
+            f32 = jnp.float32
+            for n, source in ((1, sent.at[flip(2), first]), (3, sent.at[flip(1), second])):
+                trade(n).wait()
+                more[n // 2] = (source[...].astype(f32) + got[n].astype(f32)).astype(jnp.bfloat16)
+                trade(4 + n // 2).start()
+
+    unit, inverse = norm_unit(y1_ref[...])
+    right_ref[0] = (unit * gain_ref[...] + shift_ref[...]).astype(jnp.bfloat16)
+    gr = gr_ref[...]
+    dh = None
+    for n, up, down, slope_ref, left, o_ref in (
+        (2, up_a, down_a, slope_a, left_a, oa_ref),
+        (4, up_b, down_b, slope_b, left_b, ob_ref),
+    ):
+        ready(n)
+        ready(n + 1)
+        hidden = up.shape[1]
+        part = min(768, hidden)
+        for at in range(0, hidden, part):
+            cols = slice(at, at + part)
+            slope = slope_ref[:, cols].astype(jnp.float32)
             du = (dot(gr, down[cols, :], NT) * slope).astype(jnp.bfloat16)
-            up_left[:, cols] = du
-            m = dot(act, down[cols, :])
+            left[:, cols] = du
             d = dot(du, up[:, cols], NT)
-            mlp = m if mlp is None else mlp + m
             dh = d if dh is None else dh + d
+        if n == 2:
+            second_trades()
         local = o_ref.shape[1]
-        down_left[:, hidden : hidden + local] = o_ref[...]
-        down_left[:, hidden + local :] = jnp.zeros_like(down_left[:, hidden + local :])
-    out_ref[...] = (y1 + mlp).astype(jnp.bfloat16)
+        left[:, hidden : hidden + local] = o_ref[...]
+        left[:, hidden + local :] = jnp.zeros_like(left[:, hidden + local :])
     sums = jnp.concatenate(
         [jnp.sum(dh * unit, axis=0, keepdims=True), jnp.sum(dh, axis=0, keepdims=True)], axis=0
     )
@@ -510,107 +607,220 @@
     def _():
         norm_ref[...] += sums
 
-    dy1 = g + norm_back(dh * gain_ref[...], unit, inverse)
+    ready(0)
+    ready(1)
+    dy1 = gr.astype(jnp.float32) + norm_back(dh * gain_ref[...], unit, inverse)
     dy1_ref[...] = dy1
     dar = dy1.astype(jnp.bfloat16)
     right_ref[1] = dar
     doa_ref[...] = dot(dar, wo_a[...], NT).astype(jnp.bfloat16)
     dob_ref[...] = dot(dar, wo_b[...], NT).astype(jnp.bfloat16)
 
+    @pl.when(step == last)
+    def _():
+        for at, n in ((first, 0), (second, 2)):
+            trade(n).wait()
+            trade(4 + n // 2).wait()
+            total = sent[e, at].astype(jnp.float32) + got[n].astype(jnp.float32)
+            sum_ref[at, :] = (total + got[4 + n // 2].astype(jnp.float32)).astype(jnp.bfloat16)
+
+
+def feed_specs(rows):
+    block = min(256, rows)
+
+    def tall(cols):
+        return pl.BlockSpec((block, cols), lambda i: (i, 0))
+
+    return block, tall
+
+
+def resident(loads):
+    @pl.when(pl.program_id(0) == 0)
+    def _():
+        for one in loads:
+            one.start()
+
+    def ready(i):
+        @pl.when(pl.program_id(0) == 0)
+        def _():
+            loads[i].wait()
+
+    return ready
+
 
 def feed(x, o_own, o_other, dy, real, wo, up, down, gain, shift):
     rows, width = x.shape
     local = o_own.shape[1]
     hidden = up[0].shape[1]
-    block = min(256, rows)
-
-    def tall(cols):
-        return pl.BlockSpec((block, cols), lambda i: (i, 0))
-
-    def whole(shape):
-        return pl.BlockSpec(shape, lambda i: (0, 0), pipeline_mode=pl.Buffered(1))
-
+    block, tall = feed_specs(rows)
+    weights = (*wo, up[0], down[0], up[1], down[1])
+    bf16 = jnp.bfloat16
+    return pl.pallas_call(
+        feed_kernel,
+        grid=(rows // block,),
+        out_shape=[struct((rows, width), bf16), struct((rows, width), jnp.float32), struct((rows, width), bf16)]
+        + [struct((rows, hidden), bf16)] * 4,
+        in_specs=[tall(width), tall(local), tall(local), tall(width), tall(1)] + [VMEM] * 2 + [ANYWHERE] * 6,
+        out_specs=[tall(width)] * 3 + [tall(hidden)] * 4,
+        scratch_shapes=[pltpu.VMEM(w.shape, bf16) for w in weights] + [pltpu.SemaphoreType.DMA((6,))],
+        compiler_params=params(60),
+        cost_estimate=cost(2 * rows * width * (hidden * 4 + local * 2), 45e6, rows * hidden * 4),
+        name="feed",
+    )(x, o_own, o_other, dy, real, gain, shift, *weights)
+
+
+def feed_back(y1, gr, slope, o_own, o_other, wo, up, down, gain, shift, blocks):
+    rows, width = y1.shape
+    local = o_own.shape[1]
+    hidden = up[0].shape[1]
+    block, tall = feed_specs(rows)
+    weights = (*wo, up[0], down[0], up[1], down[1])
     bf16 = jnp.bfloat16
     lefts = hidden // 3 * 4
     return pl.pallas_call(
-        feed_kernel,
+        feed_back_kernel,
         grid=(rows // block,),
         out_shape=[
-            struct((rows, width), bf16),
-            struct((rows, hidden), bf16),
-            struct((rows, hidden), bf16),
             struct((rows, lefts), bf16),
             struct((rows, lefts), bf16),
-            struct((rows, width), bf16),
             struct((2, rows, width), bf16),
             struct((rows, local), bf16),
             struct((rows, local), bf16),
             struct((rows, width), jnp.float32),
             struct((2, width), jnp.float32),
+            struct(blocks.shape[1:], bf16),
         ],
-        in_specs=[tall(width), tall(local), tall(local), tall(width), tall(1)]
-        + [whole((local, width))] * 2
-        + [whole((width, hidden))] * 2
-        + [whole((hidden, width))] * 2
-        + [whole((1, width))] * 2,
+        in_specs=[tall(width), tall(width), tall(hidden), tall(hidden), tall(local), tall(local)]
+        + [VMEM] * 2
+        + [ANYWHERE] * 7,
         out_specs=[
-            tall(width),
-            tall(hidden),
-            tall(hidden),
             tall(lefts),
             tall(lefts),
-            tall(width),
             pl.BlockSpec((2, block, width), lambda i: (0, i, 0)),
             tall(local),
             tall(local),
             tall(width),
             pl.BlockSpec((2, width), lambda i: (0, 0)),
+            pl.BlockSpec(blocks.shape[1:], lambda i: (0, 0)),
         ],
-        compiler_params=params(58),
-        cost_estimate=cost(2 * rows * width * (hidden * 8 + local * 4), 50e6, rows * hidden * 4),
-        name="feed",
-    )(x, o_own, o_other, dy, real, *wo, *up, *down, gain, shift)
-
-
-def weight_kernel(order_ref, left_ref, right_ref, out_ref):
-    out_ref[0] = dot(left_ref[...], right_ref[0], TN).astype(jnp.bfloat16)
-
-
-def weight_add_kernel(order_ref, left_ref, right_ref, more_ref, out_ref):
-    out_ref[0] = (dot(left_ref[...], right_ref[0], TN) + more_ref[0].astype(jnp.float32)).astype(jnp.bfloat16)
-
-
-def weight_grads(left, right, order, more=None):
-    rows, lefts = left.shape
+        scratch_shapes=[pltpu.VMEM(w.shape, bf16) for w in weights]
+        + [
+            pltpu.SemaphoreType.DMA((7,)),
+            pltpu.VMEM(blocks.shape, bf16),
+            pltpu.VMEM((6, blocks.shape[1] // 2, width), bf16),
+            pltpu.VMEM((2, blocks.shape[1] // 2, width), bf16),
+            pltpu.SemaphoreType.DMA((6,)),
+            pltpu.SemaphoreType.DMA((6,)),
+        ],
+        compiler_params=pltpu.CompilerParams(collective_id=1, has_side_effects=True, vmem_limit_bytes=60 * MIB),
+        cost_estimate=cost(2 * rows * width * (hidden * 4 + local * 2), 45e6),
+        name="feed_back",
+    )(y1, gr, *slope, o_own, o_other, gain, shift, blocks, *weights)
+
+
+def weight_kernel(size, hosted, other_ref, own_ref, right_ref, *refs):
+    if hosted:
+        chunk_ref, out_ref, share_ref, send, recv, send_sem, recv_sem, chunk, land, far_s, far_r, load = refs
+    else:
+        out_ref, send, recv, send_sem, recv_sem = refs
+    step = pl.program_id(0)
+    core = lax.axis_index("mp")
+    me = lax.axis_index("dp")
+    far = size // NEAR
+    f, e = me // NEAR, me % NEAR
+
+    def swapped(i):
+        return pltpu.make_async_remote_copy(
+            send.at[i], recv.at[i], send_sem.at[i], recv_sem.at[i],
+            device_id={"mp": 1 - core}, device_id_type=MESH,
+        )
+
+    def spread(d):
+        to = (f + d) % far
+        return pltpu.make_async_remote_copy(
+            chunk.at[to], land.at[d], far_s.at[d], far_r.at[d],
+            device_id={"dp": to * NEAR + e}, device_id_type=MESH,
+        )
+
+    @pl.when(step == 0)
+    def _():
+        barrier = pltpu.get_barrier_semaphore()
+        pl.semaphore_signal(barrier, inc=1, device_id={"mp": 1 - core}, device_id_type=MESH)
+        if hosted:
+            fetch = pltpu.make_async_copy(chunk_ref, chunk, load)
+            fetch.start()
+            for d in range(1, far):
+                to = (f + d) % far * NEAR + e
+                pl.semaphore_signal(barrier, inc=1, device_id={"dp": to}, device_id_type=MESH)
+            fetch.wait()
+        pl.semaphore_wait(barrier, far if hosted else 1)
+        if hosted:
+            for d in range(1, far):
+                spread(d).start()
+
+    @pl.when(step < NEAR)
+    def _():
+        send[step] = dot(other_ref[...], right_ref[0], TN).astype(jnp.bfloat16)
+        swapped(step).start()
+
+    @pl.when(step >= NEAR)
+    def _():
+        total = dot(own_ref[...], right_ref[0], TN)
+        swapped(step - NEAR).wait_recv()
+        out_ref[0] = (total + recv[step - NEAR].astype(jnp.float32)).astype(jnp.bfloat16)
+
+    @pl.when(step == 2 * NEAR - 1)
+    def _():
+        for i in range(NEAR):
+            swapped(i).wait_send()
+        if hosted:
+            total = chunk[f].astype(jnp.float32)
+            for d in range(1, far):
+                spread(d).wait()
+                total = total + land[d].astype(jnp.float32)
+            share_ref[...] = total.astype(jnp.bfloat16)
+
+
+def weight_grads(own, other, right, size, chunk=None):
+    rows, lefts = own.shape
     count, _, width = right.shape
     block = lefts // NEAR
-
-    def pick(i, order):
-        return (order[i] // (NEAR - 1) if count == 2 else 0, 0, 0)
-
-    out = pl.BlockSpec((1, block, width), lambda i, order: (i, 0, 0))
-    operands = (left, right) if more is None else (left, right, more)
+    far = size // NEAR
+    bf16 = jnp.bfloat16
+    dma = pltpu.SemaphoreType.DMA
+
+    def pick(i):
+        return (i % NEAR // (NEAR - 1) if count == 2 else 0, 0, 0)
+
+    out_shape = [struct((NEAR, block, width), bf16)]
+    in_specs = [
+        pl.BlockSpec((rows, block), lambda i: (0, jnp.minimum(i, NEAR - 1))),
+        pl.BlockSpec((rows, block), lambda i: (0, jnp.maximum(i - NEAR, 0))),
+        pl.BlockSpec((1, rows, width), pick),
+    ]
+    out_specs = [pl.BlockSpec((1, block, width), lambda i: (jnp.maximum(i - NEAR, 0), 0, 0))]
+    scratch = [pltpu.VMEM((NEAR, block, width), bf16)] * 2 + [dma((NEAR,))] * 2
+    operands = [other, own, right]
+    if chunk is not None:
+        share = chunk.shape[0] // far
+        out_shape.append(struct((share, width), bf16))
+        in_specs.append(ANYWHERE)
+        out_specs.append(pl.BlockSpec((share, width), lambda i: (0, 0)))
+        scratch += [pltpu.VMEM((far, share, width), bf16)] * 2 + [dma((far,))] * 2 + [dma]
+        operands.append(chunk.reshape(far, share, width))
     return pl.pallas_call(
-        weight_kernel if more is None else weight_add_kernel,
-        grid_spec=pltpu.PrefetchScalarGridSpec(
-            num_scalar_prefetch=1,
-            grid=(NEAR,),
-            in_specs=[
-                pl.BlockSpec((rows, block), lambda i, order: (0, order[i])),
-                pl.BlockSpec((1, rows, width), pick),
-            ]
-            + ([] if more is None else [pl.BlockSpec((1, block, width), lambda i, order: (order[i], 0, 0))]),
-            out_specs=out,
+        functools.partial(weight_kernel, size, chunk is not None),
+        grid=(2 * NEAR,),
+        out_shape=out_shape,
+        in_specs=in_specs,
+        out_specs=out_specs,
+        scratch_shapes=scratch,
+        compiler_params=pltpu.CompilerParams(
+            collective_id=2 if chunk is None else 3, has_side_effects=True, vmem_limit_bytes=60 * MIB
         ),
-        out_shape=struct((NEAR, block, width), jnp.bfloat16),
-        compiler_params=params(40),
-        cost_estimate=cost(2 * rows * width * lefts, 20e6),
+        cost_estimate=cost(4 * rows * width * lefts, 20e6),
         name="weight_grads",
-    )(order, *operands)
-
-
-NEAR = 4
-MESH = pl.DeviceIdType.MESH
+    )(*operands)
 
 
 def padded(rows, size):
@@ -629,11 +839,11 @@
 
 
 def close_kernel(
-    size, own_ref, other_ref, chunk_ref, grads_ref, ht_ref, w_ref, x_ref, dy1_ref, gain_ref, norm2_ref,
-    first_out, second_out, rows_own, rows_other, norms_out,
-    part, natural, swap_s, swap_r, dx, acc_a, acc_b, land_a, land_b, near_b, sum_b, norm_s, norm_r, norm_t,
+    size, own_ref, other_ref, up_in, down_in, gain_ref, norm2_ref, grads_in, ht_in, w_in, dy1_in, x_in,
+    up_out, down_out, second_out, rows_own, rows_other, norms_out,
+    grads_ref, ht_ref, w_ref, dy1_ref, x_ref, mine_a, mine_c, part, natural, swap_s, swap_r, dx, acc_a, acc_c, land_a, land_c, near_b, sum_b, norm_s, norm_r, norm_t,
     near_sem_s, near_sem_r, far_sem_s, far_sem_r, part_s, part_r, trade_s, trade_r, pass_s, pass_r,
-    small_s, small_r, mp_s, mp_r, local,
+    small_s, small_r, mp_s, mp_r, local, load, store,
 ):
     far = size // NEAR
     bits = [1 << b for b in range(far.bit_length() - 1)]
@@ -652,6 +862,15 @@
             b *= 2
         return out
 
+    loads = [
+        pltpu.make_async_copy(source, target, load.at[i])
+        for i, (source, target) in enumerate(
+            ((grads_in, grads_ref), (ht_in, ht_ref), (w_in, w_ref), (dy1_in, dy1_ref), (x_in, x_ref))
+        )
+    ]
+    for i in (0, 2, 1, 3, 4):
+        loads[i].start()
+
     barrier = pltpu.get_barrier_semaphore()
 
     def greet(d, carry):
@@ -672,14 +891,12 @@
             source, target, send, recv, device_id={"mp": 1 - core}, device_id_type=MESH
         )
 
-    cut = chunk_ref.shape[1] // 2
-    halves = (slice(0, cut), slice(cut, 2 * cut))
-
-    def views(first, second):
-        return lambda s, *at: first.at[(*at, halves[s])] if s < 2 else second.at[at]
-
-    inputs, accs = views(chunk_ref, sum_b), views(acc_a, acc_b)
-    lands, outs = views(land_a, land_b), views(first_out, second_out)
+    def views(*refs):
+        return lambda s, *at: refs[s].at[at]
+
+    inputs, accs = views(up_in, None, sum_b), views(acc_a, None, acc_c)
+    lands, outs = views(land_a, None, land_c), views(up_out, down_out, second_out)
+    mines = (mine_a, down_in, mine_c)
     held = {b: [m for m in range(far) if m % (2 * b) == 0] for b in bits}
     slot = {}
     for b in bits:
@@ -702,18 +919,25 @@
             base = inputs(s, flip(f, m, far)) if b == 1 else accs(s, m)
             total = (base[...].astype(jnp.float32) + lands(s, slot[b, m])[...].astype(jnp.float32)).astype(bf16)
             if 2 * b == far:
-                outs(s, e, f)[...] = total
+                mines[s][...] = total
             else:
                 accs(s, m)[...] = total
         if 2 * b < far:
             reduce_start(s, 2 * b)
         else:
+            kept(s).start()
             available(s, 0)
+
+    def kept(s):
+        return pltpu.make_async_copy(mines[s], outs(s, e, f), store.at[s])
+
+    def held_at(s, m):
+        return mines[s] if m == 0 else outs(s, e, flip(f, m, far))
 
     def spread_copy(s, b, m):
         piece = outs(s, e, flip(f, m, far))
         k = slot[b, m]
-        return remote(piece, piece, far_sem_s.at[3 + s, k], far_sem_r.at[3 + s, k], flip(f, b, far) * NEAR + e)
+        return remote(held_at(s, m), piece, far_sem_s.at[3 + s, k], far_sem_r.at[3 + s, k], flip(f, b, far) * NEAR + e)
 
     def spread_arrival(s, b, m):
         piece = outs(s, e, flip(f, m + b, far))
@@ -722,7 +946,7 @@
 
     def near_copy(s, d, m):
         piece = outs(s, e, flip(f, m, far))
-        return remote(piece, piece, near_sem_s.at[s, d, m], near_sem_r.at[s, d, m], f * NEAR + flip(e, d, NEAR))
+        return remote(held_at(s, m), piece, near_sem_s.at[s, d, m], near_sem_r.at[s, d, m], f * NEAR + flip(e, d, NEAR))
 
     def near_arrival(s, d, m):
         piece = outs(s, flip(e, d, NEAR), flip(f, m, far))
@@ -754,7 +978,7 @@
             near_arrival(s, d, m).wait_recv()
         near_pass(s, m).start()
 
-    share = land_b.shape[1]
+    share = land_c.shape[1]
 
     def near_block(index):
         return pl.ds(pl.multiple_of(index * (far * share), 16), far * share)
@@ -784,7 +1008,31 @@
         return remote(norm_s, norm_r.at[source], small_s.at[d], small_r.at[d], source)
 
     reduce_start(0, 1)
-    reduce_start(1, 1)
+    kept(1).start()
+    available(1, 0)
+
+    pieces = block // PIECE
+
+    def grad_step(i, carry):
+        at = pl.ds(pl.multiple_of(i * block, block), block)
+        value = dot(grads_ref[0, at, :], w_ref[0], NT)
+        value += dot(grads_ref[1, at, :], w_ref[1], NT)
+        value += dot(grads_ref[2, at, :], w_ref[2], NT)
+        natural[pl.ds(i * pieces, pieces)] = value.reshape(pieces, PIECE, width)
+        return carry
+
+    loads[0].wait()
+    loads[2].wait()
+    lax.fori_loop(0, rows_all // block, grad_step, 0)
+
+    def pack(j, carry):
+        swap_s[j] = natural[other_ref[j]].astype(bf16)
+        return carry
+
+    lax.fori_loop(0, swap_s.shape[0], pack, 0, unroll=8)
+    half = beside(swap_s, swap_r, mp_s.at[0], mp_r.at[0])
+    half.start()
+    reduce_step(0, 1)
 
     tall = width // 4
 
@@ -795,38 +1043,19 @@
             part[pl.ds(at, tall), :] = value.astype(bf16)
         return carry
 
+    loads[1].wait()
     lax.fori_loop(0, 3, part_step, 0)
     used = 3 * width
     if part.shape[0] > used:
         part[used:, :] = jnp.zeros((part.shape[0] - used, local_width), bf16)
     for d in range(1, NEAR):
         part_copy(d).start()
-    reduce_step(0, 1)
-
-    pieces = block // PIECE
-
-    def grad_step(i, carry):
-        at = pl.ds(pl.multiple_of(i * block, block), block)
-        value = dot(grads_ref[0, at, :], w_ref[0], NT)
-        value += dot(grads_ref[1, at, :], w_ref[1], NT)
-        value += dot(grads_ref[2, at, :], w_ref[2], NT)
-        natural[pl.ds(i * pieces, pieces)] = value.reshape(pieces, PIECE, width)
-        return carry
-
-    lax.fori_loop(0, rows_all // block, grad_step, 0)
-
-    def pack(j, carry):
-        swap_s[j] = natural[other_ref[j]].astype(bf16)
-        return carry
-
-    lax.fori_loop(0, swap_s.shape[0], pack, 0, unroll=8)
-    half = beside(swap_s, swap_r, mp_s.at[0], mp_r.at[0])
-    half.start()
-    reduce_step(1, 1)
     for b in bits[1:]:
         reduce_step(0, b)
 
     half.wait_recv()
+    loads[3].wait()
+    loads[4].wait()
     group_rows = dx.shape[1]
     norm_s[...] = jnp.zeros_like(norm_s)
     norm_s[2:4, :] = norm2_ref[...]
@@ -870,8 +1099,6 @@
     keep_small = pltpu.make_async_copy(norm_s, norm_r.at[me], local.at[1])
     keep_small.start()
 
-    for b in bits[1:]:
-        reduce_step(1, b)
     for d in range(1, NEAR):
         part_copy(d).wait_recv()
     own_part = part.at[near_block(e)]
@@ -883,21 +1110,20 @@
         sum_b[j] = total.astype(bf16)
     reduce_start(2, 1)
 
-    top = bits[-1]
+    pass_on(1, 0)
+    for b, m in arrivals:
+        arrive(1, b, m)
+    for b, m in arrivals:
+        pass_on(1, m + b)
+    reduce_step(2, 1)
     pass_on(0, 0)
-    arrive(0, top, 0)
-    pass_on(1, 0)
-    reduce_step(2, 1)
-    arrive(1, top, 0)
-    for b, m in arrivals[1:]:
-        arrive(0, b, m)
+    arrive(0, *arrivals[0])
     for b in bits[1:]:
         reduce_step(2, b)
     for b, m in arrivals[1:]:
-        arrive(1, b, m)
-    for s in range(2):
-        for b, m in arrivals:
-            pass_on(s, m + b)
+        arrive(0, b, m)
+    for b, m in arrivals:
+        pass_on(0, m + b)
     pass_on(2, 0)
     for b, m in arrivals:
         arrive(2, b, m)
@@ -936,12 +1162,15 @@
         for m in range(far):
             near_passed(s, m).wait_recv()
     half.wait_send()
+    for s in range(3):
+        kept(s).wait()
     for d in range(1, NEAR):
         part_copy(d).wait_send()
     for s in range(3):
         for b in bits:
             for m in held[b]:
-                reduce_copy(s, b, m).wait_send()
+                if s != 1:
+                    reduce_copy(s, b, m).wait_send()
                 spread_copy(s, b, m).wait_send()
         for m in range(far):
             near_copy(s, 1, m).wait_send()
@@ -958,36 +1187,45 @@
     lax.fori_loop(1, size, close, 0)
 
 
-def close(own, other, chunk, grads, ht, w, x, dy1, gain, norm2, size):
+def close(own, other, up_chunk, down_share, grads, ht, w, x, dy1, gain, norm2, size):
     far = size // NEAR
-    a, width = chunk.shape
     rows, local = grads.shape[1:]
+    width = w.shape[1]
     b = padded(3 * width, size)
     n = x.shape[0] // size
     bf16, f32 = jnp.bfloat16, jnp.float32
-    share_a, share_b = a // far, b // size
+    shares = (up_chunk.shape[0] // far, down_share.shape[0])
+    share_b = b // size
     dma = pltpu.SemaphoreType.DMA
     step = min(256, x.shape[0])
-    first, second, rows_own, rows_other, norms = pl.pallas_call(
+    up_sum, down_sum, second, rows_own, rows_other, norms = pl.pallas_call(
         functools.partial(close_kernel, size),
         out_shape=[
-            struct((NEAR, far, share_a, width), bf16),
+            struct((NEAR, far, shares[0], width), bf16),
+            struct((NEAR, far, shares[1], width), bf16),
             struct((NEAR, far, share_b, local), bf16),
             struct((size, n, width), bf16),
             struct((size, n, width), bf16),
             struct((8, width), f32),
         ],
-        in_specs=[SMEM, SMEM] + [VMEM] * 8,
-        out_specs=[VMEM] * 5,
+        in_specs=[SMEM, SMEM] + [VMEM] * 4 + [ANYWHERE] * 5,
+        out_specs=[ANYWHERE] * 5 + [VMEM],
         scratch_shapes=[
+            pltpu.VMEM(grads.shape, bf16),
+            pltpu.VMEM(ht.shape, bf16),
+            pltpu.VMEM(w.shape, bf16),
+            pltpu.VMEM(dy1.shape, f32),
+            pltpu.VMEM(x.shape, bf16),
+            pltpu.VMEM((shares[0], width), bf16),
+            pltpu.VMEM((share_b, local), bf16),
             pltpu.VMEM((b, local), bf16),
             pltpu.VMEM((rows // PIECE, PIECE, width), f32),
             pltpu.VMEM((x.shape[0] // PIECE, PIECE, width), bf16),
             pltpu.VMEM((x.shape[0] // PIECE, PIECE, width), bf16),
             pltpu.VMEM((size, n, width), bf16),
-            pltpu.VMEM((far, share_a, width), bf16),
+            pltpu.VMEM((far, shares[0], width), bf16),
             pltpu.VMEM((far, share_b, local), bf16),
-            pltpu.VMEM((far, share_a, width), bf16),
+            pltpu.VMEM((far, shares[0], width), bf16),
             pltpu.VMEM((far, share_b, local), bf16),
             pltpu.VMEM((NEAR, b // NEAR, local), bf16),
             pltpu.VMEM((far, share_b, local), bf16),
@@ -1009,15 +1247,21 @@
             dma((2,)),
             dma((2,)),
             dma((2,)),
+            dma((5,)),
+            dma((3,)),
         ],
         compiler_params=pltpu.CompilerParams(
             collective_id=0, has_side_effects=True, vmem_limit_bytes=60 * MIB
         ),
         cost_estimate=cost(8 * rows * width * local, 1e8),
         name="close",
-    )(own, other, chunk.reshape(far, share_a, width), grads, ht, w, x, dy1, gain, norm2)
+    )(
+        own, other, up_chunk.reshape(far, shares[0], width), down_share, gain, norm2,
+        grads, ht, w, dy1, x,
+    )
     return (
-        first.reshape(NEAR * a, width),
+        up_sum.reshape(NEAR, -1, width),
+        down_sum.reshape(NEAR, -1, width),
         second.reshape(b, local),
         rows_own.reshape(-1, width),
         rows_other.reshape(-1, width),
@@ -1025,37 +1269,48 @@
     )
 
 
-def widen_kernel(first_ref, second_ref, up_ref, down_ref, out_ref, qkv_ref):
+def widen_kernel(up_in, down_in, second_ref, up_ref, down_ref, out_ref, qkv_ref):
     f32 = jnp.float32
-    count = first_ref.shape[0]
-    up_rows = up_ref.shape[1] // count
-    down_rows = down_ref.shape[0] // (count - 1)
-    for e in range(count):
-        up_ref[:, e * up_rows : (e + 1) * up_rows] = first_ref[e, :up_rows, :].astype(f32).T
-    for e in range(count - 1):
-        at = slice(e * down_rows, (e + 1) * down_rows)
-        down_ref[at, :] = first_ref[e, up_rows : up_rows + down_rows, :].astype(f32)
-    out_ref[...] = first_ref[count - 1, up_rows : up_rows + out_ref.shape[0], :].astype(f32)
-    qkv_ref[...] = second_ref[: qkv_ref.shape[0], :].astype(f32)
-
-
-def widen(first, second, hidden, local, rows):
-    width = first.shape[2]
+    down_ref[...] = down_in[0, : down_ref.shape[0], :].astype(f32)
+    qkv_ref[...] = second_ref[...].astype(f32)
+
+    @pl.when(pl.program_id(0) < NEAR - 1)
+    def _():
+        up_ref[...] = up_in[0, : up_ref.shape[1], :].astype(f32).T
+
+    @pl.when(pl.program_id(0) == NEAR - 1)
+    def _():
+        out_ref[...] = up_in[0, : out_ref.shape[0], :].astype(f32)
+
+
+def widen(up_sum, down_sum, second, hidden, local, rows):
+    width = up_sum.shape[2]
     f32 = jnp.float32
+    up_rows, down_rows, part = hidden // (NEAR - 1), hidden // NEAR, rows // NEAR
     return pl.pallas_call(
         widen_kernel,
+        grid=(NEAR,),
         out_shape=[
             struct((width, hidden), f32),
             struct((hidden, width), f32),
             struct((local, width), f32),
             struct((rows, second.shape[1]), f32),
         ],
-        in_specs=[VMEM] * 2,
-        out_specs=[VMEM] * 4,
-        compiler_params=params(40),
+        in_specs=[
+            pl.BlockSpec((1, *up_sum.shape[1:]), lambda i: (i, 0, 0)),
+            pl.BlockSpec((1, *down_sum.shape[1:]), lambda i: (i, 0, 0)),
+            pl.BlockSpec((part, second.shape[1]), lambda i: (i, 0)),
+        ],
+        out_specs=[
+            pl.BlockSpec((width, up_rows), lambda i: (0, jnp.minimum(i, NEAR - 2))),
+            pl.BlockSpec((down_rows, width), lambda i: (i, 0)),
+            pl.BlockSpec((local, width), lambda i: (0, 0)),
+            pl.BlockSpec((part, second.shape[1]), lambda i: (i, 0)),
+        ],
+        compiler_params=params(60),
         cost_estimate=cost(0, 22e6),
         name="widen",
-    )(first, second)
+    )(up_sum, down_sum, second)
 
 
 def swap(value):
@@ -1097,78 +1352,63 @@
 
     x_own = exchange(gather_pieces(src_own, tokens))
     dy_send = gather_pieces(src_own, out_grad)
-    scaled = jnp.concatenate(
-        [qkv_weight[0] * jnp.asarray(HEAD_DIM**-0.5, bf16), qkv_weight[1], qkv_weight[2]], axis=1
-    )
-    scaled_t = scaled.T
-    wo_other, up_other, down_other = swap(out_weight), swap(up_weight), swap(down_weight)
-    gain1, shift1 = norm1_gain[None], norm1_shift[None]
-    gain2, shift2 = norm2_gain[None], norm2_shift[None]
-    x_own, dy_send, scaled, scaled_t, wo_other, up_other, down_other, own, other, gain1, shift1, gain2, shift2 = (
-        lax.optimization_barrier(
-            (
-                x_own, dy_send, scaled, scaled_t, wo_other, up_other, down_other,
-                own, other, gain1, shift1, gain2, shift2,
-            )
-        )
-    )
-    wo, up, down = (out_weight, wo_other), (up_weight, up_other), (down_weight, down_other)
-    x_other = swap(x_own)
-
-    h1_t, q, k, v, qt, kt, vt = project(own, other, x_own, x_other, gain1, shift1, scaled, scaled_t)
-
-    dy_own = exchange(dy_send)
-    ot, o_own, o_send, lse = attend(own, other, lengths, counts, k, qt, vt)
-    o_other = swap(o_send)
-
     place = (own[:, None] * PIECE + jnp.arange(PIECE, dtype=jnp.int32)[None, :]).reshape(-1, 1)
     real, start = jnp.zeros(place.shape, jnp.bool_), jnp.int32(0)
     for c in range(lengths.shape[1]):
         live = start + jnp.minimum(lengths[0, c], counts[0, c])
         real, start = real | ((place >= start) & (place < live)), start + lengths[0, c]
     real = real.astype(jnp.float32)
-
-    out_rows, up_own, up_other_left, down_own, down_other_left, h2, right, do_own, do_send, dy1, norm2 = feed(
+    turned_weight = jnp.swapaxes(qkv_weight, 1, 2)
+    wo_other, up_other, down_other = swap(out_weight), swap(up_weight), swap(down_weight)
+    gain1, shift1 = norm1_gain[None], norm1_shift[None]
+    gain2, shift2 = norm2_gain[None], norm2_shift[None]
+    x_own, dy_send, real, turned_weight, wo_other, up_other, down_other, own, other, gain1, shift1, gain2, shift2 = (
+        lax.optimization_barrier(
+            (
+                x_own, dy_send, real, turned_weight, wo_other, up_other, down_other,
+                own, other, gain1, shift1, gain2, shift2,
+            )
+        )
+    )
+    wo, up, down = (out_weight, wo_other), (up_weight, up_other), (down_weight, down_other)
+    x_other = swap(x_own)
+
+    h1_t, q, k, v, qt, kt, vt = project(own, other, x_own, x_other, gain1, shift1, qkv_weight, turned_weight)
+
+    dy_own = exchange(dy_send)
+    ot, o_own, o_send, lse = attend(own, other, lengths, counts, k, qt, vt)
+    o_other = swap(o_send)
+
+    out_rows, y1, gr, act_own, act_other, slope_own, slope_other = feed(
         x_own, o_own, o_other, dy_own, real, wo, up, down, gain2, shift2
     )
+    [down_blocks] = weight_grads(act_own, act_other, gr[None], groups)
+    left_own, left_other, right, do_own, do_send, dy1, norm2, down_chunk = feed_back(
+        y1, gr, (slope_own, slope_other), o_own, o_other, wo, up, down, gain2, shift2, down_blocks
+    )
     do_other = swap(do_send)
+    unit = 16 * (groups // NEAR)
+    down_chunk = jnp.pad(down_chunk, ((0, -down_chunk.shape[0] % unit), (0, 0)))
+    up_blocks, down_share = weight_grads(left_own, left_other, right, groups, down_chunk)
+    up_blocks, do_own, do_other, out_rows = lax.optimization_barrier((up_blocks, do_own, do_other, out_rows))
     out_back = exchange(out_rows)
-
     e = me % NEAR
-    natural_order = jnp.arange(NEAR, dtype=jnp.int32)
-    order = natural_order ^ e
-    up_more = swap(weight_grads(up_other_left, h2[None], natural_order))
-    down_send = weight_grads(down_other_left, right, natural_order)
-    up_blocks = weight_grads(up_own, h2[None], order, up_more)
-    down_own, up_blocks = lax.optimization_barrier((down_own, up_blocks))
-    up_got = [near_send(up_blocks[d], d, groups) for d in (1, 2)]
-    down_blocks = weight_grads(down_own, right, order, swap(down_send))
-    down_blocks, do_own, do_other = lax.optimization_barrier((down_blocks, do_own, do_other))
-    down_got = [near_send(down_blocks[d], d, groups) for d in (1, 2)]
-    both_got = near_send(jnp.concatenate([up_blocks[3], down_blocks[3]], axis=0), 3, groups)
+    up_mine = lax.dynamic_index_in_dim(up_blocks, e, 0, keepdims=False)
+    up_got = [
+        near_send(lax.dynamic_index_in_dim(up_blocks, e ^ d, 0, keepdims=False), d, groups) for d in range(1, NEAR)
+    ]
     grads = attend_back(own, other, lengths, counts, q, k, v, qt, kt, ot, lse, do_own, do_other)
-    up_got, down_got, both_got, grads, out_back = lax.optimization_barrier(
-        (up_got, down_got, both_got, grads, out_back)
-    )
-    up_rows = up_blocks.shape[1]
-    chunk = jnp.concatenate(
-        [
-            add_up([up_blocks[0], *up_got, both_got[:up_rows]]),
-            add_up([down_blocks[0], *down_got, both_got[up_rows:]]),
-        ],
-        axis=0,
-    )
-    used = chunk.shape[0]
-    chunk = jnp.pad(chunk, ((0, -used % (32 * (groups // NEAR))), (0, 0)))
-    weights, qkv_grad, dx_own, dx_other, norms = close(
-        own, other, chunk, grads, h1_t, qkv_weight, x_own, dy1, gain1, norm2, groups
-    )
-    weights, qkv_grad, dx_own, dx_other, norms, out_back = lax.optimization_barrier(
-        (weights, qkv_grad, dx_own, dx_other, norms, out_back)
-    )
-    hidden = up_weight.shape[1]
+    up_got, grads, out_back = lax.optimization_barrier((up_got, grads, out_back))
+    up_chunk = add_up([up_mine, *up_got])
+    up_chunk = jnp.pad(up_chunk, ((0, -up_chunk.shape[0] % unit), (0, 0)))
+    up_sum, down_sum, qkv_grad, dx_own, dx_other, norms = close(
+        own, other, up_chunk, down_share, grads, h1_t, qkv_weight, x_own, dy1, gain1, norm2, groups
+    )
+    up_sum, down_sum, qkv_grad, dx_own, dx_other, norms, out_back = lax.optimization_barrier(
+        (up_sum, down_sum, qkv_grad, dx_own, dx_other, norms, out_back)
+    )
     up_grad, down_grad, wo_grad, qkv_grad = widen(
-        weights.reshape(NEAR, -1, width), qkv_grad, hidden, local, 3 * width
+        up_sum, down_sum, qkv_grad, up_weight.shape[1], local, 3 * width
     )
     qkv_grad = qkv_grad.reshape(3, width, local)
 

time: 443 us -> 408 us (0.921)
  waiting for transfers between devices: 55.8 us -> 39.8 us
  local copies, waits for them, and re-layouts: 31.3 us -> 15.8 us
  Pallas kernels: 302 us -> 307 us
  other arithmetic: 9.66 us -> 4.66 us
    pallas_call x5 -> x4, Pallas kernels: 29 us -> 77.8 us  [the longest x1 39.2 us: feed_back(): pl.pallas_call(feed_back_kernel, grid=(rows // block,), out_shape=[struct...]
    pallas_call x1, Pallas kernels: 150 us -> 131 us  [close(): pl.pallas_call(functools.partial(close_kernel, size), out_shape=[struct((...]
    unnamed x73 -> x31, local copies, waits for them, and re-layouts: 21.2 us -> 4.88 us
    pallas_call x1, Pallas kernels: 35.4 us -> 21.6 us  [feed(): pl.pallas_call(feed_kernel, grid=(rows // block,), out_shape=[struct((row...]
    pallas_call x1, Pallas kernels: 30.5 us -> 20.1 us  [attend_back(): pl.pallas_call(attend_back_kernel, out_shape=struct((3, rows, width), jnp...]
    all_to_all x3, waiting for transfers between devices: 25.1 us -> 16.9 us  [exchange(): return lax.all_to_all(value, 'dp', split_axis=0, concat_axis=0, tiled=True)]
    ppermute x5 -> x3, waiting for transfers between devices: 28.7 us -> 21.6 us  [near_send(): return lax.ppermute(block, 'dp', [(i, i ^ d) for i in range(size)])]
    pallas_call x1, Pallas kernels: 32 us -> 25.3 us  [attend(): pl.pallas_call(attend_kernel, out_shape=[struct((width, rows), jnp.bfloat...]
  transfers between devices with their start and end apart: 17 -> 13, of which waited for: 3 -> 5; matrix products, arithmetic and copies ran while one was open for 3% -> 2% of each run, Pallas kernels for 24% -> 24%
where the time goes in v1:
time: 408 us; the launch traced here: 404 us
  Pallas kernels  307 us (75%)
  waiting for transfers between devices  39.8 us (10%)
  starting transfers between devices  27.9 us (7%)
  local copies, waits for them, and re-layouts  15.8 us (4%)
  between operations  8.71 us (2%)
  other arithmetic  4.66 us (1%)
    pallas_call x1, Pallas kernels, close(): pl.pallas_call(functools.partial(close_kernel, size), out_shape=[struct((...  131 us
    pallas_call x1, Pallas kernels, feed_back(): pl.pallas_call(feed_back_kernel, grid=(rows // block,), out_shape=[struct...  39.2 us
    pallas_call x2, Pallas kernels, weight_grads(): pl.pallas_call(functools.partial(weight_kernel, size, chunk is not None),...  29.5 us
    pallas_call x1, Pallas kernels, attend(): pl.pallas_call(attend_kernel, out_shape=[struct((width, rows), jnp.bfloat...  25.3 us
    all_to_all x3, starting transfers between devices, exchange(): return lax.all_to_all(value, 'dp', split_axis=0, concat_axis=0, tiled=True)  23.4 us
    pallas_call x1, Pallas kernels, feed(): pl.pallas_call(feed_kernel, grid=(rows // block,), out_shape=[struct((row...  21.6 us
    ppermute x3, waiting for transfers between devices, near_send(): return lax.ppermute(block, 'dp', [(i, i ^ d) for i in range(size)])  21.6 us
    pallas_call x1, Pallas kernels, attend_back(): pl.pallas_call(attend_back_kernel, out_shape=struct((3, rows, width), jnp...  20.1 us
  transfers between devices with their start and end apart: 13, of which 5 were waited for; matrix products, arithmetic and copies ran while one was open for 2% of the time, Pallas kernels for 24%

profile of v1, /device:TPU:0, one launch (start us, length us, event | category | flops | bytes accessed | tf_op | source)
XLA Modules:
  0.0 404.2 jit_solution(7112329674078690624)
XLA Ops:
  0.6 0.7 reshape.271
  1.4 0.2 fusion.3
  1.5 0.2 fusion.4
  1.7 0.4 select_reduce_fusion.1
  2.1 0.4 select_reduce_fusion
  2.5 0.6 reshape.272.index_ref.own_ref
  3.1 3.3 gather_pieces.2
  6.4 8.3 %all-to-all-start = ((bf16[16,64,768]{2,1,0:T(8,128)(2,1)}), bf16[16,64,768]{2,1,0:T(8,128)(2,1)S(1)}, u32[]{:S(2)}, u32[]{:S(2)}) async-start(bf16[16,64,768]{2,1,0:T(8,128)(2,1)} %bitcast.48), calls=%async_computation | async-start | bytes 3145728 | tf_op jit(solution)/shard_map/all_to_all | solution.py:1321
  14.8 0.5 collective-permute-start.2
  15.4 3.4 gather_pieces.3
  18.8 0.6 fusion.39
  27.2 0.7 fusion.30
  28.2 2.3 copy.29
  30.4 0.6 reshape.277.other_ref
  31.1 0.6 broadcast_in_dim.50.gain_ref
  31.6 0.6 broadcast_in_dim.51.shift_ref
  32.2 0.6 broadcast_in_dim.52.gain_ref
  32.8 0.6 broadcast_in_dim.53.shift_ref
  33.4 15.5 %all-to-all-done = bf16[16,64,768]{2,1,0:T(8,128)(2,1)S(1)} async-done(((bf16[16,64,768]{2,1,0:T(8,128)(2,1)}), bf16[16,64,768]{2,1,0:T(8,128)(2,1)S(1)}, u32[]{:S(2)}, u32[]{:S(2)}) %all-to-all-start) | async-done | bytes 1572896 | tf_op jit(solution)/shard_map/all_to_all | solution.py:1321
  48.9 7.6 %all-to-all-start.1 = ((bf16[16,64,768]{2,1,0:T(8,128)(2,1)}), bf16[16,64,768]{2,1,0:T(8,128)(2,1)S(1)}, u32[]{:S(2)}, u32[]{:S(2)}) async-start(bf16[16,64,768]{2,1,0:T(8,128)(2,1)} %bitcast.18), calls=%async_computation.1 | async-start | bytes 3145728 | tf_op jit(solution)/shard_map/all_to_all | solution.py:1321
  56.6 16.7 %project.1 = (bf16[768,2048]{1,0:T(8,128)(2,1)}, bf16[2048,384]{1,0:T(8,128)(2,1)}, bf16[2048,384]{1,0:T(8,128)(2,1)}, bf16[2048,384]{1,0:T(8,128)(2,1)}, bf16[3...) custom-call(s32[128]{0:T(128)} %copy-done.12, s32[128]{0:T(128)} %reshape.277.other_ref, ...), custom_call_target="tpu_custom_call" | custom-call | flops 7247757312 | bytes 20000000 | tf_op jit(solution)/shard_map/project/pallas_call | solution.py:182
  73.2 25.3 %attend.1 = (bf16[384,2048]{1,0:T(8,128)(2,1)}, bf16[128,8,384]{2,1,0:T(8,128)(2,1)}, bf16[128,8,384]{2,1,0:T(8,128)(2,1)}, f32[8,2048]{1,0:T(8,128)}) custom-call(s32[128]{0:T(128)} %copy-done.12, s32[128]{0:T(128)} %reshape.277.other_ref, s32[1,4]{1,0:T(1,128)} %len_ref.3, s32[1,4]{1,0:T(1,128)} %cnt_ref.3, bf16[2048,384]{1,0:T(8,128)(2,1)} %get-tuple-element.83.k_in, ...), custom_call_target="tpu_custom_call" | custom-call | flops 20000000000 | bytes 10000000 | tf_op jit(solution)/shard_map/attend/pallas_call | solution.py:314
  98.6 0.3 collective-permute-start.4
  98.9 1.0 copy.30.real_ref
  99.9 1.2 collective-permute-done.4.ob_ref
  101.1 0.9 copy-done.14
  102.0 0.5 copy-done.3
  102.5 21.6 %feed.1 = (bf16[1024,768]{1,0:T(8,128)(2,1)}, f32[1024,768]{1,0:T(8,128)}, bf16[1024,768]{1,0:T(8,128)(2,1)}, bf16[1024,1536]{1,0:T(8,128)(2,1)}, bf16[1024,1536...) custom-call(bf16[1024,768]{1,0:T(8,128)(2,1)} %bitcast.61, bf16[1024,384]{1,0:T(8,128)(2,1)} %bitcast.74, ...), custom_call_target="tpu_custom_call" | custom-call | flops 10871635968 | bytes 45000000 | tf_op jit(solution)/shard_map/feed/pallas_call | solution.py:658
  124.2 11.4 %weight_grads.2.blocks_ref = bf16[4,384,768]{2,1,0:T(8,128)(2,1)} custom-call(bf16[1024,1536]{1,0:T(8,128)(2,1)} %get-tuple-element.99.other_ref, bf16[1024,1536]{1,0:T(8,128)(2,1)} %get-tuple-element.100.own_ref, bf16[1,1024,768]{2,1,0:T(8,128)(2,1)} %bitcast.72), custom_call_target="tpu_custom_call" | custom-call | flops 4831838208 | bytes 20000000 | tf_op jit(solution)/shard_map/weight_grads/pallas_call | solution.py:811
  135.6 39.2 %feed_back.1 = (bf16[1024,2048]{1,0:T(8,128)(2,1)}, bf16[1024,2048]{1,0:T(8,128)(2,1)}, bf16[2,1024,768]{2,1,0:T(8,128)(2,1)}, bf16[1024,384]{1,0:T(8,128)(2,1)}...) custom-call(f32[1024,768]{1,0:T(8,128)} %get-tuple-element.95.y1_ref, ...), custom_call_target="tpu_custom_call" | custom-call | flops 10871635968 | bytes 45000000 | tf_op jit(solution)/shard_map/feed_back/pallas_call | solution.py:680
  175.0 18.1 %weight_grads.3 = (bf16[4,512,768]{2,1,0:T(8,128)(2,1)}, bf16[96,768]{1,0:T(8,128)(2,1)}) custom-call(bf16[1024,2048]{1,0:T(8,128)(2,1)} %get-tuple-element.101.other_ref, bf16[1024,2048]{1,0:T(8,128)(2,1)} %get-tuple-element.102.own_ref, bf16[2,1024,768]{2,1,0:T(8,128)(2,1)} %get-tuple-element.103.right_ref, bf16[4,96,768]{2,1,0:T(8,128)(2,1)} %bitcast.76), custom_call_target="tpu_custom_call" | custom-call | flops 6442450944 | bytes 20000000 | tf_op jit(solution)/shard_map/weight_grads/pallas_call | solution.py:811
  193.1 3.3 dynamic-slice_bitcast_fusion
  196.4 0.6 collective-permute-start.6
  197.1 1.5 collective-permute-start.7
  198.6 1.3 collective-permute-start.8
  199.9 7.4 %all-to-all-start.2 = ((bf16[16,64,768]{2,1,0:T(8,128)(2,1)}), bf16[16,64,768]{2,1,0:T(8,128)(2,1)S(1)}, u32[]{:S(2)}, u32[]{:S(2)}) async-start(bf16[16,64,768]{2,1,0:T(8,128)(2,1)} %bitcast.28), calls=%async_computation.2 | async-start | bytes 3145728 | tf_op jit(solution)/shard_map/all_to_all | solution.py:1321
  207.3 20.1 %attend_back.1.grads_in = bf16[3,2048,384]{2,1,0:T(8,128)(2,1)} custom-call(s32[128]{0:T(128)} %copy-done.12, s32[128]{0:T(128)} %reshape.277.other_ref, s32[1,4]{1,0:T(1,128)} %len_ref.3, s32[1,4]{1,0:T(1,128)} %cnt_ref.3, bf16[2048,384]{1,0:T(8,128)(2,1)} %get-tuple-element.110.q_in, bf16[2048,384]{1,0:T(8,128)(2,1)} %get-tuple-element.83.k_in, ...), custom_call_target="tpu_custom_call" | custom-call | flops 49999998976 | bytes 20000000 | tf_op jit(solution)/shard_map/attend_back/pallas_call | solution.py:456
  227.5 19.1 %collective-permute-done.7 = bf16[512,768]{1,0:T(8,128)(2,1)S(1)} collective-permute-done((bf16[512,768]{1,0:T(8,128)(2,1)}, bf16[512,768]{1,0:T(8,128)(2,1)S(1)}, u32[]{:S(2)}, u32[]{:S(2)}) %collective-permute-start.7) | collective-permute-done | bytes 786464 | tf_op jit(solution)/shard_map/ppermute | solution.py:831
  246.6 2.5 collective-permute-done.8
  249.1 1.5 all-to-all-done.2
  250.5 3.3 fusion.2
  253.8 130.8 %close.1 = (bf16[4,4,128,768]{3,2,1,0:T(8,128)(2,1)}, bf16[4,4,96,768]{3,2,1,0:T(8,128)(2,1)}, bf16[4,4,144,384]{3,2,1,0:T(8,128)(2,1)}, bf16[16,64,768]{2,1,0:T...) custom-call(s32[128]{0:T(128)} %copy-done.12, s32[128]{0:T(128)} %reshape.277.other_ref, ...), custom_call_target="tpu_custom_call" | custom-call | flops 4831838208 | bytes 100000000 | tf_op jit(solution)/shard_map/close/pallas_call | solution.py:1201
  384.7 0.7 reshape.273.other_ref
  385.4 4.0 merge_pieces.3
  389.4 9.0 %widen.1 = (f32[768,1536]{1,0:T(8,128)}, f32[1536,768]{1,0:T(8,128)}, f32[384,768]{1,0:T(8,128)}, f32[2304,384]{1,0:T(8,128)}) custom-call(bf16[4,512,768]{2,1,0:T(8,128)(2,1)} %bitcast.51, bf16[4,384,768]{2,1,0:T(8,128)(2,1)} %bitcast.56, bf16[2304,384]{1,0:T(8,128)(2,1)} %bitcast.57), custom_call_target="tpu_custom_call" | custom-call | bytes 22000000 | tf_op jit(solution)/shard_map/widen/pallas_call | solution.py:1290
  398.4 0.6 slice_reduce_fusion
  399.0 1.2 copy-done.4
  400.2 4.0 merge_pieces.2
  (47 shorter events, 0.8 us)
Async XLA Ops:
  6.4 42.5 %all-to-all-start = ((bf16[16,64,768]{2,1,0:T(8,128)(2,1)}), bf16[16,64,768]{2,1,0:T(8,128)(2,1)S(1)}, u32[]{:S(2)}, u32[]{:S(2)}) async-start(bf16[16,64,768]{2,1,0:T(8,128)(2,1)} %bitcast.48), calls=%async_computation | async-start | bytes 3145728 | tf_op jit(solution)/shard_map/all_to_all | solution.py:1321
  14.7 18.7 %collective-permute-start.1 = (bf16[768,1536]{1,0:T(8,128)(2,1)}, bf16[768,1536]{1,0:T(8,128)(2,1)}, u32[]{:S(2)}, u32[]{:S(2)}) collective-permute-start(bf16[768,1536]{1,0:T(8,128)(2,1)} %refs_2_.3), channel_id=1, source_target_pairs={{0,1},{1,0},{2,3},{3,2},{4,5},{5,4},{6,7},{7,6},{8,9},{9,8},{10,11... | collective-permute-start | bytes 7077896 | tf_op jit(solution)/shard_map/ppermute | solution.py:1317
  14.8 18.6 %collective-permute-start.2 = (bf16[1536,768]{1,0:T(8,128)(2,1)}, bf16[1536,768]{1,0:T(8,128)(2,1)}, u32[]{:S(2)}, u32[]{:S(2)}) collective-permute-start(bf16[1536,768]{1,0:T(8,128)(2,1)} %refs_3_.3), channel_id=1, source_target_pairs={{0,1},{1,0},{2,3},{3,2},{4,5},{5,4},{6,7},{7,6},{8,9},{9,8},{10,11... | collective-permute-start | bytes 7077896 | tf_op jit(solution)/shard_map/ppermute | solution.py:1317
  15.3 18.1 %collective-permute-start = (bf16[384,768]{1,0:T(8,128)(2,1)}, bf16[384,768]{1,0:T(8,128)(2,1)}, u32[]{:S(2)}, u32[]{:S(2)}) collective-permute-start(bf16[384,768]{1,0:T(8,128)(2,1)} %refs_0_.3), channel_id=1, source_target_pairs={{0,1},{1,0},{2,3},{3,2},{4,5},{5,4},{6,7},{7,6},{8,9},{9,8},{10,11... | collective-permute-start | bytes 1769480 | tf_op jit(solution)/shard_map/ppermute | solution.py:1317
  15.4 3.4 copy-start.5
  15.4 3.4 copy-start.6
  15.4 12.8 %copy-start.1 = (bf16[3,768,384]{2,1,0:T(8,128)(2,1)S(1)}, bf16[3,768,384]{2,1,0:T(8,128)(2,1)}, u32[]{:S(2)}) copy-start(bf16[3,768,384]{2,1,0:T(8,128)(2,1)} %w_in.1) | copy-start | bytes 5308420
  25.9 4.5 %copy-start.12 = (s32[128]{0:T(128)}, s32[128]{0:T(128)S(1)}, u32[]{:S(2)}) copy-start(s32[128]{0:T(128)S(1)} %broadcast_in_dim_reshape.3.own_ref) | copy-start | bytes 1540
  28.1 2.9 copy-start.8
  28.1 3.5 copy-start.9
  28.1 4.1 %copy-start.10 = (f32[768]{0:T(1024)S(1)}, f32[768]{0:T(1024)}, u32[]{:S(2)}) copy-start(f32[768]{0:T(1024)} %param.24) | copy-start | bytes 9220
  28.2 4.6 %copy-start.11 = (f32[768]{0:T(1024)S(1)}, f32[768]{0:T(1024)}, u32[]{:S(2)}) copy-start(f32[768]{0:T(1024)} %param.25) | copy-start | bytes 9220
  48.9 7.7 %copy-start.2 = (bf16[16,64,768]{2,1,0:T(8,128)(2,1)}, bf16[16,64,768]{2,1,0:T(8,128)(2,1)S(1)}, u32[]{:S(2)}) copy-start(bf16[16,64,768]{2,1,0:T(8,128)(2,1)S(1)} %all-to-all-done) | copy-start | bytes 4718596
  48.9 7.7 %collective-permute-start.3 = (bf16[1024,768]{1,0:T(8,128)(2,1)S(1)}, bf16[1024,768]{1,0:T(8,128)(2,1)}, u32[]{:S(2)}, u32[]{:S(2)}) collective-permute-start(bf16[1024,768]{1,0:T(8,128)(2,1)S(1)} %bitcast.59), channel_id=1, source_target_pairs={{0,1},{1,0},{2,3},{3,2},{4,5},{5,4},{6,7},{7,6},{8,9},{9,8},{10,11... | collective-permute-start | bytes 4718600 | tf_op jit(solution)/shard_map/ppermute | solution.py:1317
  48.9 52.2 %all-to-all-start.1 = ((bf16[16,64,768]{2,1,0:T(8,128)(2,1)}), bf16[16,64,768]{2,1,0:T(8,128)(2,1)S(1)}, u32[]{:S(2)}, u32[]{:S(2)}) async-start(bf16[16,64,768]{2,1,0:T(8,128)(2,1)} %bitcast.18), calls=%async_computation.1 | async-start | bytes 3145728 | tf_op jit(solution)/shard_map/all_to_all | solution.py:1321
  98.6 2.6 collective-permute-start.4
  101.1 0.9 copy-start.14
  101.1 1.4 copy-start.3
  174.9 18.2 %collective-permute-start.5 = (bf16[1024,384]{1,0:T(8,128)(2,1)}, bf16[1024,384]{1,0:T(8,128)(2,1)S(1)}, u32[]{:S(2)}, u32[]{:S(2)}) collective-permute-start(bf16[1024,384]{1,0:T(8,128)(2,1)} %get-tuple-element.107), channel_id=1, source_target_pairs={{0,1},{1,0},{2,3},{3,2},{4,5},{5,4},{6,7},{7,6},{8,9},{9,8},{10,11... | collective-permute-start | bytes 2359304 | tf_op jit(solution)/shard_map/ppermute | solution.py:1317
  193.1 3.4 copy-start.13
  196.4 31.1 %collective-permute-start.6 = (bf16[512,768]{1,0:T(8,128)(2,1)}, bf16[512,768]{1,0:T(8,128)(2,1)S(1)}, u32[]{:S(2)}, u32[]{:S(2)}) collective-permute-start(bf16[512,768]{1,0:T(8,128)(2,1)} %get-tuple-element.150), channel_id=1, source_target_pairs={{0,2},{2,0},{4,6},{6,4},{8,10},{10,8},{12,14},{14,12},{16,18},{18,... | collective-permute-start | bytes 2359304 | tf_op jit(solution)/shard_map/ppermute | solution.py:831
  197.1 49.5 %collective-permute-start.7 = (bf16[512,768]{1,0:T(8,128)(2,1)}, bf16[512,768]{1,0:T(8,128)(2,1)S(1)}, u32[]{:S(2)}, u32[]{:S(2)}) collective-permute-start(bf16[512,768]{1,0:T(8,128)(2,1)} %get-tuple-element.149), channel_id=1, source_target_pairs={{0,4},{2,6},{4,0},{6,2},{8,12},{10,14},{12,8},{14,10},{16,20},{18,... | collective-permute-start | bytes 2359304 | tf_op jit(solution)/shard_map/ppermute | solution.py:831
  198.6 50.5 %collective-permute-start.8 = (bf16[512,768]{1,0:T(8,128)(2,1)}, bf16[512,768]{1,0:T(8,128)(2,1)}, u32[]{:S(2)}, u32[]{:S(2)}) collective-permute-start(bf16[512,768]{1,0:T(8,128)(2,1)} %get-tuple-element.148), channel_id=1, source_target_pairs={{0,6},{2,4},{4,2},{6,0},{8,14},{10,12},{12,10},{14,8},{16,22},{18,... | collective-permute-start | bytes 2359304 | tf_op jit(solution)/shard_map/ppermute | solution.py:831
  199.9 50.6 %all-to-all-start.2 = ((bf16[16,64,768]{2,1,0:T(8,128)(2,1)}), bf16[16,64,768]{2,1,0:T(8,128)(2,1)S(1)}, u32[]{:S(2)}, u32[]{:S(2)}) async-start(bf16[16,64,768]{2,1,0:T(8,128)(2,1)} %bitcast.28), calls=%async_computation.2 | async-start | bytes 3145728 | tf_op jit(solution)/shard_map/all_to_all | solution.py:1321
  250.5 134.1 %copy-start = (bf16[16,64,768]{2,1,0:T(8,128)(2,1)}, bf16[16,64,768]{2,1,0:T(8,128)(2,1)S(1)}, u32[]{:S(2)}) copy-start(bf16[16,64,768]{2,1,0:T(8,128)(2,1)S(1)} %all-to-all-done.2) | copy-start | bytes 4718596
  384.6 14.4 %collective-permute-start.9 = (bf16[1024,768]{1,0:T(8,128)(2,1)S(1)}, bf16[1024,768]{1,0:T(8,128)(2,1)S(1)}, u32[]{:S(2)}, u32[]{:S(2)}) collective-permute-start(bf16[1024,768]{1,0:T(8,128)(2,1)S(1)} %bitcast.49), channel_id=1, source_target_pairs={{0,1},{1,0},{2,3},{3,2},{4,5},{5,4},{6,7},{7,6},{8,9},{9,8},{10,11... | collective-permute-start | bytes 4718600 | tf_op jit(solution)/shard_map/ppermute | solution.py:1317
  389.4 9.0 %copy-start.7 = (f32[8,768]{1,0:T(8,128)S(1)}, f32[8,768]{1,0:T(8,128)}, u32[]{:S(2)}) copy-start(f32[8,768]{1,0:T(8,128)} %get-tuple-element.143) | copy-start | bytes 73732
  399.0 1.2 copy-start.4

commit v2 on v1

--- a/solution.py
+++ b/solution.py
@@ -89,60 +89,8 @@
     return out.reshape(count * PIECE, width)
 
 
-def split_kernel(own_ref, other_ref, source_ref, own_out, other_out):
-    def step(j, carry):
-        own_out[j] = source_ref[own_ref[j]]
-        other_out[j] = source_ref[other_ref[j]]
-        return carry
-
-    lax.fori_loop(0, own_out.shape[0], step, 0, unroll=8)
-
-
-def split_pieces(own, other, source):
-    rows, width = source.shape
-    count = own.shape[0]
-    outs = pl.pallas_call(
-        split_kernel,
-        out_shape=[struct((count, PIECE, width), source.dtype)] * 2,
-        in_specs=[SMEM, SMEM, VMEM],
-        out_specs=[VMEM, VMEM],
-        compiler_params=params(60),
-        cost_estimate=cost(0, 4 * rows * width),
-        name="split_pieces",
-    )(own, other, source.reshape(rows // PIECE, PIECE, width))
-    return tuple(o.reshape(count * PIECE, width) for o in outs)
-
-
-def merge_kernel(own_ref, other_ref, own_in, other_in, out_ref):
-    def step(j, carry):
-        out_ref[own_ref[j]] = own_in[j]
-        out_ref[other_ref[j]] = other_in[j]
-        return carry
-
-    lax.fori_loop(0, own_in.shape[0], step, 0, unroll=8)
-
-
-def merge_pieces(own, other, own_rows, other_rows):
-    rows, width = own_rows.shape
-    out = pl.pallas_call(
-        merge_kernel,
-        out_shape=struct((2 * rows // PIECE, PIECE, width), own_rows.dtype),
-        in_specs=[SMEM, SMEM, VMEM, VMEM],
-        out_specs=VMEM,
-        compiler_params=params(60),
-        cost_estimate=cost(0, 8 * rows * width),
-        name="merge_pieces",
-    )(
-        own,
-        other,
-        own_rows.reshape(rows // PIECE, PIECE, width),
-        other_rows.reshape(rows // PIECE, PIECE, width),
-    )
-    return out.reshape(2 * rows, width)
-
-
 def project_kernel(
-    own_ref, other_ref, own_in, other_in, gain_ref, shift_ref, w_ref, wt_ref,
+    own_ref, other_ref, own_in, other_in, gain_ref, shift_ref, w_ref,
     ht_ref, q_ref, k_ref, v_ref, qt_ref, kt_ref, vt_ref, x_all,
 ):
     @pl.when(pl.program_id(0) == 0)
@@ -162,16 +110,17 @@
     ht_ref[...] = h.T
     for i, (n_ref, t_ref) in enumerate(((q_ref, qt_ref), (k_ref, kt_ref), (v_ref, vt_ref))):
         scale = HEAD_DIM**-0.5 if i == 0 else 1.0
-        n_ref[...] = (dot(h, w_ref[i]) * scale).astype(jnp.bfloat16)
-        t_ref[...] = (dot(wt_ref[i], h, NT) * scale).astype(jnp.bfloat16)
-
-
-def project(own, other, x_own, x_other, gain, shift, w, wt):
+        value = (dot(h, w_ref[i]) * scale).astype(jnp.bfloat16)
+        n_ref[...] = value
+        t_ref[...] = value.T
+
+
+def project(own, other, x_own, x_other, gain, shift, w):
     half, width = x_own.shape
     rows, local = 2 * half, w.shape[2]
     outs = 3 * local
     pieces = half // PIECE
-    block = min(256, rows)
+    block = min(512, rows)
     bf16 = jnp.bfloat16
 
     def whole(shape):
@@ -186,13 +135,13 @@
         in_specs=[SMEM, SMEM]
         + [whole((pieces, PIECE, width))] * 2
         + [whole((1, width))] * 2
-        + [whole(w.shape), whole(wt.shape)],
+        + [whole(w.shape)],
         out_specs=[pl.BlockSpec((width, block), lambda i: (0, i))] + [natural] * 3 + [turned] * 3,
         scratch_shapes=[pltpu.VMEM((rows // PIECE, PIECE, width), bf16)],
         compiler_params=params(60),
-        cost_estimate=cost(4 * rows * width * outs, 20e6),
+        cost_estimate=cost(2 * rows * width * outs, 20e6),
         name="project",
-    )(own, other, x_own.reshape(pieces, PIECE, width), x_other.reshape(pieces, PIECE, width), gain, shift, w, wt)
+    )(own, other, x_own.reshape(pieces, PIECE, width), x_other.reshape(pieces, PIECE, width), gain, shift, w)
 
 
 def cell_bounds(len_ref, cnt_ref):
@@ -484,9 +433,10 @@
 def feed_kernel(
     x_ref, oa_ref, ob_ref, dy_ref, real_ref, gain_ref, shift_ref, *refs,
 ):
-    weights, (out_ref, y1_ref, gr_ref, act_a, act_b, slope_a, slope_b), held = refs[:6], refs[6:13], refs[13:19]
+    weights, outs, held, load = refs[:6], refs[6:14], refs[14:20], refs[20]
+    out_ref, y1_ref, gr_ref, turned_ref, act_a, act_b, slope_a, slope_b = outs
     wo_a, wo_b, up_a, down_a, up_b, down_b = held
-    ready = resident([pltpu.make_async_copy(w, h, refs[19].at[i]) for i, (w, h) in enumerate(zip(weights, held))])
+    ready = resident([pltpu.make_async_copy(w, h, load.at[i]) for i, (w, h) in enumerate(zip(weights, held))])
     ready(0)
     ready(1)
     x = x_ref[...].astype(jnp.float32)
@@ -494,7 +444,9 @@
     y1_ref[...] = y1
     unit, _ = norm_unit(y1)
     h = (unit * gain_ref[...] + shift_ref[...]).astype(jnp.bfloat16)
-    gr_ref[...] = (dy_ref[...].astype(jnp.float32) * real_ref[...]).astype(jnp.bfloat16)
+    gr = (dy_ref[...].astype(jnp.float32) * real_ref[...]).astype(jnp.bfloat16)
+    gr_ref[...] = gr
+    turned_ref[0] = gr.T
     mlp = None
     for n, up, down, act_ref, slope_ref in ((2, up_a, down_a, act_a, slope_a), (4, up_b, down_b, act_b, slope_b)):
         ready(n)
@@ -572,7 +524,7 @@
                 trade(4 + n // 2).start()
 
     unit, inverse = norm_unit(y1_ref[...])
-    right_ref[0] = (unit * gain_ref[...] + shift_ref[...]).astype(jnp.bfloat16)
+    right_ref[0] = (unit * gain_ref[...] + shift_ref[...]).astype(jnp.bfloat16).T
     gr = gr_ref[...]
     dh = None
     for n, up, down, slope_ref, left, o_ref in (
@@ -612,7 +564,7 @@
     dy1 = gr.astype(jnp.float32) + norm_back(dh * gain_ref[...], unit, inverse)
     dy1_ref[...] = dy1
     dar = dy1.astype(jnp.bfloat16)
-    right_ref[1] = dar
+    right_ref[1] = dar.T
     doa_ref[...] = dot(dar, wo_a[...], NT).astype(jnp.bfloat16)
     dob_ref[...] = dot(dar, wo_b[...], NT).astype(jnp.bfloat16)
 
@@ -658,10 +610,15 @@
     return pl.pallas_call(
         feed_kernel,
         grid=(rows // block,),
-        out_shape=[struct((rows, width), bf16), struct((rows, width), jnp.float32), struct((rows, width), bf16)]
+        out_shape=[
+            struct((rows, width), bf16),
+            struct((rows, width), jnp.float32),
+            struct((rows, width), bf16),
+            struct((1, width, rows), bf16),
+        ]
         + [struct((rows, hidden), bf16)] * 4,
         in_specs=[tall(width), tall(local), tall(local), tall(width), tall(1)] + [VMEM] * 2 + [ANYWHERE] * 6,
-        out_specs=[tall(width)] * 3 + [tall(hidden)] * 4,
+        out_specs=[tall(width)] * 3 + [pl.BlockSpec((1, width, block), lambda i: (0, 0, i))] + [tall(hidden)] * 4,
         scratch_shapes=[pltpu.VMEM(w.shape, bf16) for w in weights] + [pltpu.SemaphoreType.DMA((6,))],
         compiler_params=params(60),
         cost_estimate=cost(2 * rows * width * (hidden * 4 + local * 2), 45e6, rows * hidden * 4),
@@ -683,7 +640,7 @@
         out_shape=[
             struct((rows, lefts), bf16),
             struct((rows, lefts), bf16),
-            struct((2, rows, width), bf16),
+            struct((2, width, rows), bf16),
             struct((rows, local), bf16),
             struct((rows, local), bf16),
             struct((rows, width), jnp.float32),
@@ -696,7 +653,7 @@
         out_specs=[
             tall(lefts),
             tall(lefts),
-            pl.BlockSpec((2, block, width), lambda i: (0, i, 0)),
+            pl.BlockSpec((2, width, block), lambda i: (0, 0, i)),
             tall(local),
             tall(local),
             tall(width),
@@ -707,8 +664,8 @@
         + [
             pltpu.SemaphoreType.DMA((7,)),
             pltpu.VMEM(blocks.shape, bf16),
-            pltpu.VMEM((6, blocks.shape[1] // 2, width), bf16),
-            pltpu.VMEM((2, blocks.shape[1] // 2, width), bf16),
+            pltpu.VMEM((6, blocks.shape[1] // 2, blocks.shape[2]), bf16),
+            pltpu.VMEM((2, blocks.shape[1] // 2, blocks.shape[2]), bf16),
             pltpu.SemaphoreType.DMA((6,)),
             pltpu.SemaphoreType.DMA((6,)),
         ],
@@ -720,7 +677,8 @@
 
 def weight_kernel(size, hosted, other_ref, own_ref, right_ref, *refs):
     if hosted:
-        chunk_ref, out_ref, share_ref, send, recv, send_sem, recv_sem, chunk, land, far_s, far_r, load = refs
+        chunk_ref, *outs = refs[:5]
+        share_ref, send, recv, send_sem, recv_sem, chunk, land, far_s, far_r, load, tiles, store = refs[5:]
     else:
         out_ref, send, recv, send_sem, recv_sem = refs
     step = pl.program_id(0)
@@ -741,6 +699,12 @@
             chunk.at[to], land.at[d], far_s.at[d], far_r.at[d],
             device_id={"dp": to * NEAR + e}, device_id_type=MESH,
         )
+
+    def flip(d):
+        return (e // 2 + d // 2) % 2 * 2 + (e % 2 + d % 2) % 2
+
+    def kept(d):
+        return pltpu.make_async_copy(tiles.at[flip(d)], outs[d], store.at[d])
 
     @pl.when(step == 0)
     def _():
@@ -760,20 +724,33 @@
 
     @pl.when(step < NEAR)
     def _():
-        send[step] = dot(other_ref[...], right_ref[0], TN).astype(jnp.bfloat16)
+        send[step] = dot(right_ref[0], other_ref[...]).astype(jnp.bfloat16)
         swapped(step).start()
 
     @pl.when(step >= NEAR)
     def _():
-        total = dot(own_ref[...], right_ref[0], TN)
-        swapped(step - NEAR).wait_recv()
-        out_ref[0] = (total + recv[step - NEAR].astype(jnp.float32)).astype(jnp.bfloat16)
+        total = dot(right_ref[0], own_ref[...])
+        tile = step - NEAR
+        swapped(tile).wait_recv()
+        value = (total + recv[tile].astype(jnp.float32)).astype(jnp.bfloat16)
+        if hosted:
+            tiles[tile] = value
+            for d in range(NEAR):
+
+                @pl.when(flip(d) == tile)
+                def _(d=d):
+                    kept(d).start()
+
+        else:
+            out_ref[0] = value
 
     @pl.when(step == 2 * NEAR - 1)
     def _():
         for i in range(NEAR):
             swapped(i).wait_send()
         if hosted:
+            for d in range(NEAR):
+                kept(d).wait()
             total = chunk[f].astype(jnp.float32)
             for d in range(1, far):
                 spread(d).wait()
@@ -783,7 +760,7 @@
 
 def weight_grads(own, other, right, size, chunk=None):
     rows, lefts = own.shape
-    count, _, width = right.shape
+    count, width, _ = right.shape
     block = lefts // NEAR
     far = size // NEAR
     bf16 = jnp.bfloat16
@@ -792,22 +769,24 @@
     def pick(i):
         return (i % NEAR // (NEAR - 1) if count == 2 else 0, 0, 0)
 
-    out_shape = [struct((NEAR, block, width), bf16)]
+    out_shape = [struct((NEAR, width, block), bf16)]
     in_specs = [
         pl.BlockSpec((rows, block), lambda i: (0, jnp.minimum(i, NEAR - 1))),
         pl.BlockSpec((rows, block), lambda i: (0, jnp.maximum(i - NEAR, 0))),
-        pl.BlockSpec((1, rows, width), pick),
+        pl.BlockSpec((1, width, rows), pick),
     ]
-    out_specs = [pl.BlockSpec((1, block, width), lambda i: (jnp.maximum(i - NEAR, 0), 0, 0))]
-    scratch = [pltpu.VMEM((NEAR, block, width), bf16)] * 2 + [dma((NEAR,))] * 2
+    out_specs = [pl.BlockSpec((1, width, block), lambda i: (jnp.maximum(i - NEAR, 0), 0, 0))]
+    scratch = [pltpu.VMEM((NEAR, width, block), bf16)] * 2 + [dma((NEAR,))] * 2
     operands = [other, own, right]
     if chunk is not None:
-        share = chunk.shape[0] // far
-        out_shape.append(struct((share, width), bf16))
+        share, cols = chunk.shape[0] // far, chunk.shape[1]
+        out_shape = [struct((width, block), bf16)] * NEAR + [struct((share, cols), bf16)]
+        out_specs = [ANYWHERE] * NEAR
         in_specs.append(ANYWHERE)
-        out_specs.append(pl.BlockSpec((share, width), lambda i: (0, 0)))
-        scratch += [pltpu.VMEM((far, share, width), bf16)] * 2 + [dma((far,))] * 2 + [dma]
-        operands.append(chunk.reshape(far, share, width))
+        out_specs.append(pl.BlockSpec((share, cols), lambda i: (0, 0)))
+        scratch += [pltpu.VMEM((far, share, cols), bf16)] * 2 + [dma((far,))] * 2 + [dma]
+        scratch += [pltpu.VMEM((NEAR, width, block), bf16), dma((NEAR,))]
+        operands.append(chunk.reshape(far, share, cols))
     return pl.pallas_call(
         functools.partial(weight_kernel, size, chunk is not None),
         grid=(2 * NEAR,),
@@ -841,7 +820,7 @@
 def close_kernel(
     size, own_ref, other_ref, up_in, down_in, gain_ref, norm2_ref, grads_in, ht_in, w_in, dy1_in, x_in,
     up_out, down_out, second_out, rows_own, rows_other, norms_out,
-    grads_ref, ht_ref, w_ref, dy1_ref, x_ref, mine_a, mine_c, part, natural, swap_s, swap_r, dx, acc_a, acc_c, land_a, land_c, near_b, sum_b, norm_s, norm_r, norm_t,
+    grads_ref, ht_ref, w_ref, dy1_ref, x_ref, mine_a, mine_c, part, natural, swap_s, swap_r, dx, acc_a, acc_c, land_a, land_c, near_b, near_m, sum_b, norm_s, norm_r, norm_t,
     near_sem_s, near_sem_r, far_sem_s, far_sem_r, part_s, part_r, trade_s, trade_r, pass_s, pass_r,
     small_s, small_r, mp_s, mp_r, local, load, store,
 ):
@@ -868,7 +847,7 @@
             ((grads_in, grads_ref), (ht_in, ht_ref), (w_in, w_ref), (dy1_in, dy1_ref), (x_in, x_ref))
         )
     ]
-    for i in (0, 2, 1, 3, 4):
+    for i in (0, 1, 2, 3, 4):
         loads[i].start()
 
     barrier = pltpu.get_barrier_semaphore()
@@ -980,12 +959,21 @@
 
     share = land_c.shape[1]
 
-    def near_block(index):
-        return pl.ds(pl.multiple_of(index * (far * share), 16), far * share)
-
-    def part_copy(d):
-        to = flip(e, d, NEAR)
-        return remote(part.at[near_block(to)], near_b.at[d], part_s.at[d], part_r.at[d], f * NEAR + to)
+    half_block = far * share // 2
+
+    def near_half(index, h):
+        return pl.ds(pl.multiple_of(index * (2 * half_block) + h * half_block, 16), half_block)
+
+    def part_copy(n):
+        source, d = (
+            (part.at[near_half(flip(e, 1, NEAR), 0)], 1),
+            (part.at[near_half(flip(e, 3, NEAR), 0)], 1),
+            (part.at[near_half(flip(e, 2, NEAR), 1)], 2),
+            (part.at[near_half(flip(e, 3, NEAR), 1)], 2),
+            (near_m.at[0], 2),
+            (near_m.at[1], 1),
+        )[n]
+        return remote(source, near_b.at[n], part_s.at[n], part_r.at[n], f * NEAR + flip(e, d, NEAR))
 
     def trade(d):
         to = (me + d) % size
@@ -1010,6 +998,24 @@
     reduce_start(0, 1)
     kept(1).start()
     available(1, 0)
+
+    tall = width // 4
+
+    def part_step(i, carry):
+        for c in range(4):
+            value = dot(ht_ref[c * tall : (c + 1) * tall, :], grads_ref[i])
+            at = pl.multiple_of(i * width + c * tall, 16)
+            part[pl.ds(at, tall), :] = value.astype(bf16)
+        return carry
+
+    loads[0].wait()
+    loads[1].wait()
+    lax.fori_loop(0, 3, part_step, 0)
+    used = 3 * width
+    if part.shape[0] > used:
+        part[used:, :] = jnp.zeros((part.shape[0] - used, local_width), bf16)
+    for n in (1, 3, 0, 2):
+        part_copy(n).start()
 
     pieces = block // PIECE
 
@@ -1021,7 +1027,6 @@
         natural[pl.ds(i * pieces, pieces)] = value.reshape(pieces, PIECE, width)
         return carry
 
-    loads[0].wait()
     loads[2].wait()
     lax.fori_loop(0, rows_all // block, grad_step, 0)
 
@@ -1033,25 +1038,8 @@
     half = beside(swap_s, swap_r, mp_s.at[0], mp_r.at[0])
     half.start()
     reduce_step(0, 1)
-
-    tall = width // 4
-
-    def part_step(i, carry):
-        for c in range(4):
-            value = dot(ht_ref[c * tall : (c + 1) * tall, :], grads_ref[i])
-            at = pl.multiple_of(i * width + c * tall, 16)
-            part[pl.ds(at, tall), :] = value.astype(bf16)
-        return carry
-
-    loads[1].wait()
-    lax.fori_loop(0, 3, part_step, 0)
-    used = 3 * width
-    if part.shape[0] > used:
-        part[used:, :] = jnp.zeros((part.shape[0] - used, local_width), bf16)
-    for d in range(1, NEAR):
-        part_copy(d).start()
-    for b in bits[1:]:
-        reduce_step(0, b)
+    for b, m in arrivals[:1]:
+        arrive(1, b, m)
 
     half.wait_recv()
     loads[3].wait()
@@ -1099,19 +1087,25 @@
     keep_small = pltpu.make_async_copy(norm_s, norm_r.at[me], local.at[1])
     keep_small.start()
 
-    for d in range(1, NEAR):
-        part_copy(d).wait_recv()
-    own_part = part.at[near_block(e)]
-    for j in range(far):
-        at = slice(j * share, (j + 1) * share)
-        total = own_part[at, :].astype(jnp.float32)
-        for d in range(1, NEAR):
-            total = total + near_b[d, at, :].astype(jnp.float32)
-        sum_b[j] = total.astype(bf16)
+    for b in bits[1:]:
+        reduce_step(0, b)
+    f32 = jnp.float32
+    for h, n in ((0, 1), (1, 3)):
+        part_copy(n).wait_recv()
+        base = part[near_half(flip(e, 2 - h, NEAR), h), :]
+        near_m[h] = (base.astype(f32) + near_b[n].astype(f32)).astype(bf16)
+        part_copy(4 + h).start()
+    for h, n in ((0, 0), (1, 2)):
+        part_copy(n).wait_recv()
+        part_copy(4 + h).wait_recv()
+        base = part[near_half(e, h), :]
+        total = base.astype(f32) + near_b[n].astype(f32) + near_b[4 + h].astype(f32)
+        for j in range(far // 2):
+            sum_b[h * (far // 2) + j] = total[j * share : (j + 1) * share].astype(bf16)
     reduce_start(2, 1)
 
     pass_on(1, 0)
-    for b, m in arrivals:
+    for b, m in arrivals[1:]:
         arrive(1, b, m)
     for b, m in arrivals:
         pass_on(1, m + b)
@@ -1127,8 +1121,6 @@
     pass_on(2, 0)
     for b, m in arrivals:
         arrive(2, b, m)
-    for b, m in arrivals:
-        pass_on(2, m + b)
     keep.wait()
     passing(0).start()
 
@@ -1158,14 +1150,16 @@
     last.wait()
     norms_out[...] = norm_s[...] + norm_r[size]
 
+    for b, m in arrivals:
+        pass_on(2, m + b)
     for s in range(3):
         for m in range(far):
             near_passed(s, m).wait_recv()
     half.wait_send()
     for s in range(3):
         kept(s).wait()
-    for d in range(1, NEAR):
-        part_copy(d).wait_send()
+    for n in range(6):
+        part_copy(n).wait_send()
     for s in range(3):
         for b in bits:
             for m in held[b]:
@@ -1195,14 +1189,15 @@
     n = x.shape[0] // size
     bf16, f32 = jnp.bfloat16, jnp.float32
     shares = (up_chunk.shape[0] // far, down_share.shape[0])
+    cols = (up_chunk.shape[1], down_share.shape[1])
     share_b = b // size
     dma = pltpu.SemaphoreType.DMA
     step = min(256, x.shape[0])
     up_sum, down_sum, second, rows_own, rows_other, norms = pl.pallas_call(
         functools.partial(close_kernel, size),
         out_shape=[
-            struct((NEAR, far, shares[0], width), bf16),
-            struct((NEAR, far, shares[1], width), bf16),
+            struct((NEAR, far, shares[0], cols[0]), bf16),
+            struct((NEAR, far, shares[1], cols[1]), bf16),
             struct((NEAR, far, share_b, local), bf16),
             struct((size, n, width), bf16),
             struct((size, n, width), bf16),
@@ -1216,18 +1211,19 @@
             pltpu.VMEM(w.shape, bf16),
             pltpu.VMEM(dy1.shape, f32),
             pltpu.VMEM(x.shape, bf16),
-            pltpu.VMEM((shares[0], width), bf16),
+            pltpu.VMEM((shares[0], cols[0]), bf16),
             pltpu.VMEM((share_b, local), bf16),
             pltpu.VMEM((b, local), bf16),
             pltpu.VMEM((rows // PIECE, PIECE, width), f32),
             pltpu.VMEM((x.shape[0] // PIECE, PIECE, width), bf16),
             pltpu.VMEM((x.shape[0] // PIECE, PIECE, width), bf16),
             pltpu.VMEM((size, n, width), bf16),
-            pltpu.VMEM((far, shares[0], width), bf16),
+            pltpu.VMEM((far, shares[0], cols[0]), bf16),
             pltpu.VMEM((far, share_b, local), bf16),
-            pltpu.VMEM((far, shares[0], width), bf16),
+            pltpu.VMEM((far, shares[0], cols[0]), bf16),
             pltpu.VMEM((far, share_b, local), bf16),
-            pltpu.VMEM((NEAR, b // NEAR, local), bf16),
+            pltpu.VMEM((6, b // NEAR // 2, local), bf16),
+            pltpu.VMEM((2, b // NEAR // 2, local), bf16),
             pltpu.VMEM((far, share_b, local), bf16),
             pltpu.VMEM((8, width), f32),
             pltpu.VMEM((size + 1, 8, width), f32),
@@ -1236,8 +1232,8 @@
             dma((3, NEAR, far)),
             dma((6, far)),
             dma((6, far)),
-            dma((NEAR,)),
-            dma((NEAR,)),
+            dma((6,)),
+            dma((6,)),
             dma((size,)),
             dma((size,)),
             dma((size,)),
@@ -1256,12 +1252,12 @@
         cost_estimate=cost(8 * rows * width * local, 1e8),
         name="close",
     )(
-        own, other, up_chunk.reshape(far, shares[0], width), down_share, gain, norm2,
+        own, other, up_chunk.reshape(far, shares[0], cols[0]), down_share, gain, norm2,
         grads, ht, w, dy1, x,
     )
     return (
-        up_sum.reshape(NEAR, -1, width),
-        down_sum.reshape(NEAR, -1, width),
+        up_sum.reshape(NEAR, -1, cols[0]),
+        down_sum.reshape(NEAR, -1, cols[1]),
         second.reshape(b, local),
         rows_own.reshape(-1, width),
         rows_other.reshape(-1, width),
@@ -1269,52 +1265,107 @@
     )
 
 
-def widen_kernel(up_in, down_in, second_ref, up_ref, down_ref, out_ref, qkv_ref):
+def settle_kernel(
+    own_ref, other_ref, mixed_a, mixed_b, dx_a, dx_b, up_in, down_in, qkv_in,
+    mixed_out, dx_out, up_out, down_out, wo_out, qkv_out,
+    halves, mixed, dx, up_v, down_v, qkv_v, up, down, wo, qkv, load, store,
+):
     f32 = jnp.float32
-    down_ref[...] = down_in[0, : down_ref.shape[0], :].astype(f32)
-    qkv_ref[...] = second_ref[...].astype(f32)
-
-    @pl.when(pl.program_id(0) < NEAR - 1)
-    def _():
-        up_ref[...] = up_in[0, : up_ref.shape[1], :].astype(f32).T
-
-    @pl.when(pl.program_id(0) == NEAR - 1)
-    def _():
-        out_ref[...] = up_in[0, : out_ref.shape[0], :].astype(f32)
-
-
-def widen(up_sum, down_sum, second, hidden, local, rows):
-    width = up_sum.shape[2]
-    f32 = jnp.float32
-    up_rows, down_rows, part = hidden // (NEAR - 1), hidden // NEAR, rows // NEAR
-    return pl.pallas_call(
-        widen_kernel,
-        grid=(NEAR,),
-        out_shape=[
-            struct((width, hidden), f32),
-            struct((hidden, width), f32),
-            struct((local, width), f32),
-            struct((rows, second.shape[1]), f32),
-        ],
-        in_specs=[
-            pl.BlockSpec((1, *up_sum.shape[1:]), lambda i: (i, 0, 0)),
-            pl.BlockSpec((1, *down_sum.shape[1:]), lambda i: (i, 0, 0)),
-            pl.BlockSpec((part, second.shape[1]), lambda i: (i, 0)),
-        ],
-        out_specs=[
-            pl.BlockSpec((width, up_rows), lambda i: (0, jnp.minimum(i, NEAR - 2))),
-            pl.BlockSpec((down_rows, width), lambda i: (i, 0)),
-            pl.BlockSpec((local, width), lambda i: (0, 0)),
-            pl.BlockSpec((part, second.shape[1]), lambda i: (i, 0)),
+    sources = (mixed_a, mixed_b, dx_a, dx_b)
+    loads = [pltpu.make_async_copy(one, halves.at[i], load.at[i]) for i, one in enumerate(sources)]
+    more = ((up_in, up_v), (down_in, down_v), (qkv_in, qkv_v))
+    loads += [pltpu.make_async_copy(one, to, load.at[4 + i]) for i, (one, to) in enumerate(more)]
+    for one in loads:
+        one.start()
+    stores = []
+
+    def keep(source, target):
+        stores.append(pltpu.make_async_copy(source, target, store.at[len(stores)]))
+        stores[-1].start()
+
+    for i, (merged, target) in enumerate(((mixed, mixed_out), (dx, dx_out))):
+        loads[2 * i].wait()
+        loads[2 * i + 1].wait()
+
+        def step(j, carry):
+            merged[own_ref[j]] = halves[2 * i, j]
+            merged[other_ref[j]] = halves[2 * i + 1, j]
+            return carry
+
+        lax.fori_loop(0, halves.shape[1], step, 0, unroll=8)
+        keep(merged, target)
+    loads[4].wait()
+    width = up.shape[0]
+    cols = up.shape[1] // (NEAR - 1)
+    for e in range(NEAR - 1):
+        up[:, e * cols : (e + 1) * cols] = up_v[e, :width, :].astype(f32)
+    keep(up, up_out)
+    wo[...] = up_v[NEAR - 1, :width, : wo.shape[0]].astype(f32).T
+    keep(wo, wo_out)
+    loads[5].wait()
+    cols = down.shape[0] // NEAR
+    for e in range(NEAR):
+        down[e * cols : (e + 1) * cols, :] = down_v[e, :width, :].astype(f32).T
+    keep(down, down_out)
+    loads[6].wait()
+    qkv[...] = qkv_v[: qkv.shape[0], :].astype(f32)
+    keep(qkv, qkv_out)
+    for one in stores:
+        one.wait()
+
+
+def settle(own, other, mixed, dx, up_sum, down_sum, qkv_sum, hidden, local):
+    rows, width = mixed[0].shape
+    count = rows // PIECE
+    pieces = (count, PIECE, width)
+    f32, bf16 = jnp.float32, jnp.bfloat16
+    outs = [
+        struct((2 * count, PIECE, width), bf16),
+        struct((2 * count, PIECE, width), bf16),
+        struct((width, hidden), f32),
+        struct((hidden, width), f32),
+        struct((local, width), f32),
+        struct((3 * width, local), f32),
+    ]
+    held = [pltpu.VMEM(one.shape, one.dtype) for one in outs]
+    sums = [pltpu.VMEM(one.shape, bf16) for one in (up_sum, down_sum, qkv_sum)]
+    mixed_out, dx_out, *grads = pl.pallas_call(
+        settle_kernel,
+        out_shape=outs,
+        in_specs=[SMEM] * 2 + [ANYWHERE] * 7,
+        out_specs=[ANYWHERE] * 6,
+        scratch_shapes=[
+            pltpu.VMEM((4, *pieces), bf16),
+            *held[:2],
+            *sums,
+            *held[2:],
+            pltpu.SemaphoreType.DMA((7,)),
+            pltpu.SemaphoreType.DMA((6,)),
         ],
         compiler_params=params(60),
-        cost_estimate=cost(0, 22e6),
-        name="widen",
-    )(up_sum, down_sum, second)
+        cost_estimate=cost(0, 34e6),
+        name="settle",
+    )(own, other, *[one.reshape(pieces) for one in (*mixed, *dx)], up_sum, down_sum, qkv_sum)
+    return mixed_out.reshape(2 * rows, width), dx_out.reshape(2 * rows, width), *grads
 
 
 def swap(value):
     return lax.ppermute(value, "mp", [(0, 1), (1, 0)])
+
+
+def held_kernel(value_ref, after_ref, out_ref):
+    del value_ref, after_ref, out_ref
+
+
+def held_until(value, after):
+    return pl.pallas_call(
+        held_kernel,
+        out_shape=struct(value.shape, value.dtype),
+        in_specs=[ANYWHERE] * 2,
+        out_specs=ANYWHERE,
+        input_output_aliases={0: 0},
+        name="held_until",
+    )(value, after)
 
 
 def exchange(value):
@@ -1358,14 +1409,13 @@
         live = start + jnp.minimum(lengths[0, c], counts[0, c])
         real, start = real | ((place >= start) & (place < live)), start + lengths[0, c]
     real = real.astype(jnp.float32)
-    turned_weight = jnp.swapaxes(qkv_weight, 1, 2)
     wo_other, up_other, down_other = swap(out_weight), swap(up_weight), swap(down_weight)
     gain1, shift1 = norm1_gain[None], norm1_shift[None]
     gain2, shift2 = norm2_gain[None], norm2_shift[None]
-    x_own, dy_send, real, turned_weight, wo_other, up_other, down_other, own, other, gain1, shift1, gain2, shift2 = (
+    x_own, dy_send, real, wo_other, up_other, down_other, own, other, gain1, shift1, gain2, shift2 = (
         lax.optimization_barrier(
             (
-                x_own, dy_send, real, turned_weight, wo_other, up_other, down_other,
+                x_own, dy_send, real, wo_other, up_other, down_other,
                 own, other, gain1, shift1, gain2, shift2,
             )
         )
@@ -1373,47 +1423,40 @@
     wo, up, down = (out_weight, wo_other), (up_weight, up_other), (down_weight, down_other)
     x_other = swap(x_own)
 
-    h1_t, q, k, v, qt, kt, vt = project(own, other, x_own, x_other, gain1, shift1, qkv_weight, turned_weight)
+    h1_t, q, k, v, qt, kt, vt = project(own, other, x_own, x_other, gain1, shift1, qkv_weight)
 
     dy_own = exchange(dy_send)
     ot, o_own, o_send, lse = attend(own, other, lengths, counts, k, qt, vt)
     o_other = swap(o_send)
 
-    out_rows, y1, gr, act_own, act_other, slope_own, slope_other = feed(
+    out_rows, y1, gr, gr_turned, act_own, act_other, slope_own, slope_other = feed(
         x_own, o_own, o_other, dy_own, real, wo, up, down, gain2, shift2
     )
-    [down_blocks] = weight_grads(act_own, act_other, gr[None], groups)
+    [down_blocks] = weight_grads(act_own, act_other, gr_turned, groups)
     left_own, left_other, right, do_own, do_send, dy1, norm2, down_chunk = feed_back(
         y1, gr, (slope_own, slope_other), o_own, o_other, wo, up, down, gain2, shift2, down_blocks
     )
     do_other = swap(do_send)
     unit = 16 * (groups // NEAR)
     down_chunk = jnp.pad(down_chunk, ((0, -down_chunk.shape[0] % unit), (0, 0)))
-    up_blocks, down_share = weight_grads(left_own, left_other, right, groups, down_chunk)
-    up_blocks, do_own, do_other, out_rows = lax.optimization_barrier((up_blocks, do_own, do_other, out_rows))
-    out_back = exchange(out_rows)
-    e = me % NEAR
-    up_mine = lax.dynamic_index_in_dim(up_blocks, e, 0, keepdims=False)
-    up_got = [
-        near_send(lax.dynamic_index_in_dim(up_blocks, e ^ d, 0, keepdims=False), d, groups) for d in range(1, NEAR)
-    ]
+    *up_blocks, down_share = weight_grads(left_own, left_other, right, groups, down_chunk)
+    up_blocks, do_own, do_other = lax.optimization_barrier((up_blocks, do_own, do_other))
+    up_got = [near_send(up_blocks[d], d, groups) for d in range(1, NEAR)]
+    out_back = exchange(held_until(out_rows, swap(up_blocks[0][:16, :128])))
     grads = attend_back(own, other, lengths, counts, q, k, v, qt, kt, ot, lse, do_own, do_other)
     up_got, grads, out_back = lax.optimization_barrier((up_got, grads, out_back))
-    up_chunk = add_up([up_mine, *up_got])
+    out_other = swap(out_back)
+    up_chunk = add_up([up_blocks[0], *up_got])
     up_chunk = jnp.pad(up_chunk, ((0, -up_chunk.shape[0] % unit), (0, 0)))
     up_sum, down_sum, qkv_grad, dx_own, dx_other, norms = close(
         own, other, up_chunk, down_share, grads, h1_t, qkv_weight, x_own, dy1, gain1, norm2, groups
     )
-    up_sum, down_sum, qkv_grad, dx_own, dx_other, norms, out_back = lax.optimization_barrier(
-        (up_sum, down_sum, qkv_grad, dx_own, dx_other, norms, out_back)
-    )
-    up_grad, down_grad, wo_grad, qkv_grad = widen(
-        up_sum, down_sum, qkv_grad, up_weight.shape[1], local, 3 * width
+    mixed_out, input_grad, up_grad, down_grad, wo_grad, qkv_grad = settle(
+        src_own, src_other, (out_back, out_other), (dx_own, dx_other), up_sum, down_sum, qkv_grad,
+        up_weight.shape[1], local,
     )
     qkv_grad = qkv_grad.reshape(3, width, local)
 
-    mixed_out = merge_pieces(src_own, src_other, out_back, swap(out_back))
-    input_grad = merge_pieces(src_own, src_other, dx_own, dx_other)
     return (
         mixed_out, input_grad, qkv_grad, wo_grad, up_grad, down_grad,
         norms[0], norms[1], norms[2], norms[3],

time: 408 us -> 399 us (0.978)
  waiting for transfers between devices: 39.8 us -> 30.2 us
    pallas_call x1, Pallas kernels: 20.1 us -> 33.7 us  [attend_back(): pl.pallas_call(attend_back_kernel, out_shape=struct((3, rows, width), jnp...]
    ppermute x3, waiting for transfers between devices: 21.6 us -> 8.99 us  [near_send(): return lax.ppermute(block, 'dp', [(i, i ^ d) for i in range(size)])]
    pallas_call x1, Pallas kernels: 131 us -> 125 us  [close(): pl.pallas_call(functools.partial(close_kernel, size), out_shape=[struct((...]
    pallas_call x1, Pallas kernels: 39.2 us -> 33.7 us  [feed_back(): pl.pallas_call(feed_back_kernel, grid=(rows // block,), out_shape=[struct...]
    pallas_call x1, Pallas kernels: 25.3 us -> 30.8 us  [attend(): pl.pallas_call(attend_kernel, out_shape=[struct((width, rows), jnp.bfloat...]
    pallas_call x3 -> x2, Pallas kernels: 17 us -> 11.9 us  [the longest x1 11.9 us: settle(): pl.pallas_call(settle_kernel, out_shape=outs, in_specs=[SMEM] * 2 + [ANYW...]
    pallas_call x1, Pallas kernels: 16.7 us -> 11.6 us  [project(): pl.pallas_call(project_kernel, grid=(rows // block,), out_shape=[struct((...]
  transfers between devices with their start and end apart: 13 -> 14, of which waited for: 5 -> 4; matrix products, arithmetic and copies ran while one was open for 2% -> 3% of each run, Pallas kernels for 24% -> 57%
where the time goes in v2:
time: 399 us; the launch traced here: 395 us
  Pallas kernels  307 us (77%)
  waiting for transfers between devices  30.2 us (8%)
  starting transfers between devices  28.9 us (7%)
  local copies, waits for them, and re-layouts  14.7 us (4%)
  between operations  8.98 us (2%)
  other arithmetic  4.52 us (1%)
    pallas_call x1, Pallas kernels, close(): pl.pallas_call(functools.partial(close_kernel, size), out_shape=[struct((...  125 us
    pallas_call x1, Pallas kernels, feed_back(): pl.pallas_call(feed_back_kernel, grid=(rows // block,), out_shape=[struct...  33.7 us
    pallas_call x1, Pallas kernels, attend_back(): pl.pallas_call(attend_back_kernel, out_shape=struct((3, rows, width), jnp...  33.7 us
    pallas_call x2, Pallas kernels, weight_grads(): pl.pallas_call(functools.partial(weight_kernel, size, chunk is not None),...  31.9 us
    pallas_call x1, Pallas kernels, attend(): pl.pallas_call(attend_kernel, out_shape=[struct((width, rows), jnp.bfloat...  30.8 us
    all_to_all x3, starting transfers between devices, exchange(): return lax.all_to_all(value, 'dp', split_axis=0, concat_axis=0, tiled=True)  23.4 us
    pallas_call x1, Pallas kernels, feed(): pl.pallas_call(feed_kernel, grid=(rows // block,), out_shape=[struct((row...  22.3 us
    all_to_all x3, waiting for transfers between devices, exchange(): return lax.all_to_all(value, 'dp', split_axis=0, concat_axis=0, tiled=True)  19.7 us
  transfers between devices with their start and end apart: 14, of which 4 were waited for; matrix products, arithmetic and copies ran while one was open for 3% of the time, Pallas kernels for 57%

profile of v2, /device:TPU:0, one launch (start us, length us, event | category | flops | bytes accessed | tf_op | source)
XLA Modules:
  0.0 394.9 jit_solution(4528747719293678962)
XLA Ops:
  0.6 0.7 reshape.257
  1.4 0.2 fusion
  1.5 0.2 fusion.1
  1.7 0.4 select_reduce_fusion.1
  2.1 0.3 select_reduce_fusion
  2.5 0.7 reshape.258.index_ref.own_ref
  3.2 3.3 gather_pieces.2
  6.5 8.5 %all-to-all-start = ((bf16[16,64,768]{2,1,0:T(8,128)(2,1)}), bf16[16,64,768]{2,1,0:T(8,128)(2,1)S(1)}, u32[]{:S(2)}, u32[]{:S(2)}) async-start(bf16[16,64,768]{2,1,0:T(8,128)(2,1)} %bitcast.35), calls=%async_computation | async-start | bytes 3145728 | tf_op jit(solution)/shard_map/all_to_all | solution.py:1372
  15.0 0.5 collective-permute-start.2
  15.6 0.6 broadcast_in_dim.47.gain_ref
  16.2 0.6 broadcast_in_dim.48.shift_ref
  16.8 0.6 broadcast_in_dim.49.gain_ref
  17.4 0.6 broadcast_in_dim.50.shift_ref
  17.9 0.7 fusion.36
  25.2 0.7 reshape.263.other_ref
  27.2 0.7 fusion.27
  27.9 0.1 copy.26
  28.0 0.1 reshape.282
  28.1 3.3 gather_pieces.3
  31.4 17.7 %all-to-all-done = bf16[16,64,768]{2,1,0:T(8,128)(2,1)S(1)} async-done(((bf16[16,64,768]{2,1,0:T(8,128)(2,1)}), bf16[16,64,768]{2,1,0:T(8,128)(2,1)S(1)}, u32[]{:S(2)}, u32[]{:S(2)}) %all-to-all-start) | async-done | bytes 1572896 | tf_op jit(solution)/shard_map/all_to_all | solution.py:1372
  49.1 1.2 copy-done.1
  50.3 7.6 %all-to-all-start.1 = ((bf16[16,64,768]{2,1,0:T(8,128)(2,1)}), bf16[16,64,768]{2,1,0:T(8,128)(2,1)S(1)}, u32[]{:S(2)}, u32[]{:S(2)}) async-start(bf16[16,64,768]{2,1,0:T(8,128)(2,1)} %bitcast.37), calls=%async_computation.1 | async-start | bytes 3145728 | tf_op jit(solution)/shard_map/all_to_all | solution.py:1372
  58.0 11.6 %project.1 = (bf16[768,2048]{1,0:T(8,128)(2,1)}, bf16[2048,384]{1,0:T(8,128)(2,1)}, bf16[2048,384]{1,0:T(8,128)(2,1)}, bf16[2048,384]{1,0:T(8,128)(2,1)}, bf16[3...) custom-call(s32[128]{0:T(128)} %copy-done.13, s32[128]{0:T(128)} %reshape.263.other_ref, ...), custom_call_target="tpu_custom_call" | custom-call | flops 3623878656 | bytes 20000000 | tf_op jit(solution)/shard_map/project/pallas_call | solution.py:131
  69.6 30.8 %attend.1 = (bf16[384,2048]{1,0:T(8,128)(2,1)}, bf16[128,8,384]{2,1,0:T(8,128)(2,1)}, bf16[128,8,384]{2,1,0:T(8,128)(2,1)}, f32[8,2048]{1,0:T(8,128)}) custom-call(s32[128]{0:T(128)} %copy-done.13, s32[128]{0:T(128)} %reshape.263.other_ref, s32[1,4]{1,0:T(1,128)} %len_ref.3, s32[1,4]{1,0:T(1,128)} %cnt_ref.3, bf16[2048,384]{1,0:T(8,128)(2,1)} %get-tuple-element.82.k_in, ...), custom_call_target="tpu_custom_call" | custom-call | flops 20000000000 | bytes 10000000 | tf_op jit(solution)/shard_map/attend/pallas_call | solution.py:263
  100.4 1.0 copy.27.real_ref
  101.5 1.5 collective-permute-done.4.ob_ref
  102.9 0.9 copy-done.15
  103.8 0.5 copy-done.2
  104.3 22.3 %feed.1 = (bf16[1024,768]{1,0:T(8,128)(2,1)}, f32[1024,768]{1,0:T(8,128)}, bf16[1024,768]{1,0:T(8,128)(2,1)}, bf16[1,768,1024]{2,1,0:T(8,128)(2,1)}, bf16[1024,1...) custom-call(bf16[1024,768]{1,0:T(8,128)(2,1)} %bitcast.47, ...), custom_call_target="tpu_custom_call" | custom-call | flops 10871635968 | bytes 45000000 | tf_op jit(solution)/shard_map/feed/pallas_call | solution.py:610
  126.6 12.1 %weight_grads.2.blocks_ref = bf16[4,768,384]{2,1,0:T(8,128)(2,1)} custom-call(bf16[1024,1536]{1,0:T(8,128)(2,1)} %get-tuple-element.98.other_ref, bf16[1024,1536]{1,0:T(8,128)(2,1)} %get-tuple-element.99.own_ref, bf16[1,768,1024]{2,1,0:T(8,128)(2,1)} %get-tuple-element.100.right_ref), custom_call_target="tpu_custom_call" | custom-call | flops 4831838208 | bytes 20000000 | tf_op jit(solution)/shard_map/weight_grads/pallas_call | solution.py:790
  138.8 33.7 %feed_back.1 = (bf16[1024,2048]{1,0:T(8,128)(2,1)}, bf16[1024,2048]{1,0:T(8,128)(2,1)}, bf16[2,768,1024]{2,1,0:T(8,128)(2,1)}, bf16[1024,384]{1,0:T(8,128)(2,1)}...) custom-call(f32[1024,768]{1,0:T(8,128)} %get-tuple-element.94.y1_ref, ...), custom_call_target="tpu_custom_call" | custom-call | flops 10871635968 | bytes 45000000 | tf_op jit(solution)/shard_map/feed_back/pallas_call | solution.py:637
  172.6 19.7 %weight_grads.3 = (bf16[768,512]{1,0:T(8,128)(2,1)}, bf16[768,512]{1,0:T(8,128)(2,1)}, bf16[768,512]{1,0:T(8,128)(2,1)}, bf16[768,512]{1,0:T(8,128)(2,1)}, bf16[192,384]{1,0:T(8,128)(2,1)}) custom-call(bf16[1024,2048]{1,0:T(8,128)(2,1)} %get-tuple-element.101.other_ref, bf16[1024,2048]{1,0:T(8,128)(2,1)} %get-tuple-element.102.own_ref, ...), custom_call_target="tpu_custom_call" | custom-call | flops 6442450944 | bytes 20000000 | tf_op jit(solution)/shard_map/weight_grads/pallas_call | solution.py:790
  192.4 0.9 copy-done.14
  193.2 0.7 slice.50
  193.9 0.2 collective-permute-start.9
  194.1 2.9 collective-permute-start.6
  197.0 1.5 collective-permute-start.8
  198.5 0.6 copy-done.8
  199.1 7.3 %all-to-all-start.2 = ((bf16[16,64,768]{2,1,0:T(8,128)(2,1)}), bf16[16,64,768]{2,1,0:T(8,128)(2,1)S(1)}, u32[]{:S(2)}, u32[]{:S(2)}) async-start(bf16[16,64,768]{2,1,0:T(8,128)(2,1)} %bitcast.36), calls=%async_computation.2 | async-start | bytes 3145728 | tf_op jit(solution)/shard_map/all_to_all | solution.py:1372
  206.4 33.7 %attend_back.1.grads_in = bf16[3,2048,384]{2,1,0:T(8,128)(2,1)} custom-call(s32[128]{0:T(128)} %copy-done.13, s32[128]{0:T(128)} %reshape.263.other_ref, s32[1,4]{1,0:T(1,128)} %len_ref.3, s32[1,4]{1,0:T(1,128)} %cnt_ref.3, bf16[2048,384]{1,0:T(8,128)(2,1)} %get-tuple-element.114.q_in, bf16[2048,384]{1,0:T(8,128)(2,1)} %get-tuple-element.82.k_in, ...), custom_call_target="tpu_custom_call" | custom-call | flops 49999998976 | bytes 20000000 | tf_op jit(solution)/shard_map/attend_back/pallas_call | solution.py:405
  240.2 9.0 %collective-permute-done.8 = bf16[768,512]{1,0:T(8,128)(2,1)} collective-permute-done((bf16[768,512]{1,0:T(8,128)(2,1)}, bf16[768,512]{1,0:T(8,128)(2,1)}, u32[]{:S(2)}, u32[]{:S(2)}) %collective-permute-start.8) | collective-permute-done | bytes 786464 | tf_op jit(solution)/shard_map/ppermute | solution.py:810
  249.2 2.0 all-to-all-done.2
  251.2 0.8 reshape.259.other_ref
  252.0 3.1 add_convert_fusion
  255.2 124.9 %close.1 = (bf16[4,4,192,512]{3,2,1,0:T(8,128)(2,1)}, bf16[4,4,192,384]{3,2,1,0:T(8,128)(2,1)}, bf16[4,4,144,384]{3,2,1,0:T(8,128)(2,1)}, bf16[16,64,768]{2,1,0:...) custom-call(s32[128]{0:T(128)} %copy-done.13, s32[128]{0:T(128)} %reshape.263.other_ref, ...), custom_call_target="tpu_custom_call" | custom-call | flops 4831838208 | bytes 100000000 | tf_op jit(solution)/shard_map/close/pallas_call | solution.py:1196
  380.1 1.5 slice_reduce_fusion
  381.6 1.2 copy-done.3
  382.8 11.9 %settle.1 = (bf16[256,8,768]{2,1,0:T(8,128)(2,1)}, bf16[256,8,768]{2,1,0:T(8,128)(2,1)}, f32[768,1536]{1,0:T(8,128)}, f32[1536,768]{1,0:T(8,128)}, f32[384,768]{1,0:T(8,128)}, /*index=5*/f32[2304,384]{1,0:T(8,128)}) custom-call(s32[128]{0:T(128)} %reshape.258.index_ref.own_ref, s32[128]{0:T(128)} %reshape.259.other_ref, bf16[128,8,768]{2,1,0:T(8,128)(2,1)} %bitcast.39, ...), custom_call_target="tpu_custom_call" | custom-call | bytes 34000000 | tf_op jit(solution)/shard_map/settle/pallas_call | solution.py:1332
  (53 shorter events, 0.7 us)
Async XLA Ops:
  6.4 9.1 %copy-start.16 = (bf16[384,768]{1,0:T(8,128)(2,1)S(1)}, bf16[384,768]{1,0:T(8,128)(2,1)}, u32[]{:S(2)}) copy-start(bf16[384,768]{1,0:T(8,128)(2,1)} %refs_0_.3) | copy-start | bytes 1769476
  6.4 9.2 %copy-start.9 = (f32[768]{0:T(1024)S(1)}, f32[768]{0:T(1024)}, u32[]{:S(2)}) copy-start(f32[768]{0:T(1024)} %param.22) | copy-start | bytes 9220
  6.4 9.8 %copy-start.10 = (f32[768]{0:T(1024)S(1)}, f32[768]{0:T(1024)}, u32[]{:S(2)}) copy-start(f32[768]{0:T(1024)} %param.23) | copy-start | bytes 9220
  6.4 10.3 %copy-start.11 = (f32[768]{0:T(1024)S(1)}, f32[768]{0:T(1024)}, u32[]{:S(2)}) copy-start(f32[768]{0:T(1024)} %param.24) | copy-start | bytes 9220
  6.4 10.9 %copy-start.12 = (f32[768]{0:T(1024)S(1)}, f32[768]{0:T(1024)}, u32[]{:S(2)}) copy-start(f32[768]{0:T(1024)} %param.25) | copy-start | bytes 9220
  6.4 11.5 %copy-start.6 = (s32[1,4]{1,0:T(1,128)S(1)}, s32[1,4]{1,0:T(1,128)}, u32[]{:S(2)}) copy-start(s32[1,4]{1,0:T(1,128)} %len_ref.3) | copy-start | bytes 52
  6.5 11.5 %copy-start.7 = (s32[1,4]{1,0:T(1,128)S(1)}, s32[1,4]{1,0:T(1,128)}, u32[]{:S(2)}) copy-start(s32[1,4]{1,0:T(1,128)} %cnt_ref.3) | copy-start | bytes 52
  6.5 42.6 %all-to-all-start = ((bf16[16,64,768]{2,1,0:T(8,128)(2,1)}), bf16[16,64,768]{2,1,0:T(8,128)(2,1)S(1)}, u32[]{:S(2)}, u32[]{:S(2)}) async-start(bf16[16,64,768]{2,1,0:T(8,128)(2,1)} %bitcast.35), calls=%async_computation | async-start | bytes 3145728 | tf_op jit(solution)/shard_map/all_to_all | solution.py:1372
  14.9 16.4 %collective-permute-start.1 = (bf16[768,1536]{1,0:T(8,128)(2,1)}, bf16[768,1536]{1,0:T(8,128)(2,1)}, u32[]{:S(2)}, u32[]{:S(2)}) collective-permute-start(bf16[768,1536]{1,0:T(8,128)(2,1)} %refs_2_.3), channel_id=1, source_target_pairs={{0,1},{1,0},{2,3},{3,2},{4,5},{5,4},{6,7},{7,6},{8,9},{9,8},{10,11... | collective-permute-start | bytes 7077896 | tf_op jit(solution)/shard_map/ppermute | solution.py:1353
  15.0 16.4 %collective-permute-start.2 = (bf16[1536,768]{1,0:T(8,128)(2,1)}, bf16[1536,768]{1,0:T(8,128)(2,1)}, u32[]{:S(2)}, u32[]{:S(2)}) collective-permute-start(bf16[1536,768]{1,0:T(8,128)(2,1)} %refs_3_.3), channel_id=1, source_target_pairs={{0,1},{1,0},{2,3},{3,2},{4,5},{5,4},{6,7},{7,6},{8,9},{9,8},{10,11... | collective-permute-start | bytes 7077896 | tf_op jit(solution)/shard_map/ppermute | solution.py:1353
  15.5 15.8 %collective-permute-start = (bf16[384,768]{1,0:T(8,128)(2,1)S(1)}, bf16[384,768]{1,0:T(8,128)(2,1)S(1)}, u32[]{:S(2)}, u32[]{:S(2)}) collective-permute-start(bf16[384,768]{1,0:T(8,128)(2,1)S(1)} %copy-done.16), channel_id=1, source_target_pairs={{0,1},{1,0},{2,3},{3,2},{4,5},{5,4},{6,7},{7,6},{8,9},{9,8},{10,11... | collective-permute-start | bytes 1769480 | tf_op jit(solution)/shard_map/ppermute | solution.py:1353
  25.2 6.1 %copy-start.13 = (s32[128]{0:T(128)}, s32[128]{0:T(128)S(1)}, u32[]{:S(2)}) copy-start(s32[128]{0:T(128)S(1)} %broadcast_in_dim_reshape.3.own_ref) | copy-start | bytes 1540
  31.4 17.8 %copy-start.17 = (bf16[384,768]{1,0:T(8,128)(2,1)}, bf16[384,768]{1,0:T(8,128)(2,1)S(1)}, u32[]{:S(2)}) copy-start(bf16[384,768]{1,0:T(8,128)(2,1)S(1)} %collective-permute-done.refs_1_) | copy-start | bytes 1769476
  49.1 1.2 copy-start.1
  49.1 8.8 %collective-permute-start.3 = (bf16[1024,768]{1,0:T(8,128)(2,1)S(1)}, bf16[1024,768]{1,0:T(8,128)(2,1)}, u32[]{:S(2)}, u32[]{:S(2)}) collective-permute-start(bf16[1024,768]{1,0:T(8,128)(2,1)S(1)} %bitcast.45), channel_id=1, source_target_pairs={{0,1},{1,0},{2,3},{3,2},{4,5},{5,4},{6,7},{7,6},{8,9},{9,8},{10,11... | collective-permute-start | bytes 4718600 | tf_op jit(solution)/shard_map/ppermute | solution.py:1353
  50.3 52.6 %all-to-all-start.1 = ((bf16[16,64,768]{2,1,0:T(8,128)(2,1)}), bf16[16,64,768]{2,1,0:T(8,128)(2,1)S(1)}, u32[]{:S(2)}, u32[]{:S(2)}) async-start(bf16[16,64,768]{2,1,0:T(8,128)(2,1)} %bitcast.37), calls=%async_computation.1 | async-start | bytes 3145728 | tf_op jit(solution)/shard_map/all_to_all | solution.py:1372
  100.4 2.6 collective-permute-start.4
  102.9 0.9 copy-start.15
  102.9 1.4 copy-start.2
  172.5 19.8 %collective-permute-start.5 = (bf16[1024,384]{1,0:T(8,128)(2,1)}, bf16[1024,384]{1,0:T(8,128)(2,1)S(1)}, u32[]{:S(2)}, u32[]{:S(2)}) collective-permute-start(bf16[1024,384]{1,0:T(8,128)(2,1)} %get-tuple-element.110), channel_id=1, source_target_pairs={{0,1},{1,0},{2,3},{3,2},{4,5},{5,4},{6,7},{7,6},{8,9},{9,8},{10,11... | collective-permute-start | bytes 2359304 | tf_op jit(solution)/shard_map/ppermute | solution.py:1353
  192.3 0.9 copy-start.14
  193.9 4.6 %collective-permute-start.9 = (bf16[16,128]{1,0:T(8,128)(2,1)S(1)}, bf16[16,128]{1,0:T(8,128)(2,1)S(1)}, u32[]{:S(2)}, u32[]{:S(2)}) collective-permute-start(bf16[16,128]{1,0:T(8,128)(2,1)S(1)} %slice.50), channel_id=1, source_target_pairs={{0,1},{1,0},{2,3},{3,2},{4,5},{5,4},{6,7},{7,6},{8,9},{9,8},{10,11... | collective-permute-start | bytes 12296 | tf_op jit(solution)/shard_map/ppermute | solution.py:1353
  194.1 46.1 %collective-permute-start.6 = (bf16[768,512]{1,0:T(8,128)(2,1)}, bf16[768,512]{1,0:T(8,128)(2,1)S(1)}, u32[]{:S(2)}, u32[]{:S(2)}) collective-permute-start(bf16[768,512]{1,0:T(8,128)(2,1)} %get-tuple-element.111), channel_id=1, source_target_pairs={{0,2},{2,0},{4,6},{6,4},{8,10},{10,8},{12,14},{14,12},{16,18},{18,... | collective-permute-start | bytes 2359304 | tf_op jit(solution)/shard_map/ppermute | solution.py:810
  197.0 43.2 %collective-permute-start.7 = (bf16[768,512]{1,0:T(8,128)(2,1)}, bf16[768,512]{1,0:T(8,128)(2,1)S(1)}, u32[]{:S(2)}, u32[]{:S(2)}) collective-permute-start(bf16[768,512]{1,0:T(8,128)(2,1)} %get-tuple-element.112), channel_id=1, source_target_pairs={{0,4},{2,6},{4,0},{6,2},{8,12},{10,14},{12,8},{14,10},{16,20},{18,... | collective-permute-start | bytes 2359304 | tf_op jit(solution)/shard_map/ppermute | solution.py:810
  197.0 52.2 %collective-permute-start.8 = (bf16[768,512]{1,0:T(8,128)(2,1)}, bf16[768,512]{1,0:T(8,128)(2,1)}, u32[]{:S(2)}, u32[]{:S(2)}) collective-permute-start(bf16[768,512]{1,0:T(8,128)(2,1)} %get-tuple-element.113), channel_id=1, source_target_pairs={{0,6},{2,4},{4,2},{6,0},{8,14},{10,12},{12,10},{14,8},{16,22},{18,... | collective-permute-start | bytes 2359304 | tf_op jit(solution)/shard_map/ppermute | solution.py:810
  198.5 0.6 copy-start.8
  199.1 52.1 %all-to-all-start.2 = ((bf16[16,64,768]{2,1,0:T(8,128)(2,1)}), bf16[16,64,768]{2,1,0:T(8,128)(2,1)S(1)}, u32[]{:S(2)}, u32[]{:S(2)}) async-start(bf16[16,64,768]{2,1,0:T(8,128)(2,1)} %bitcast.36), calls=%async_computation.2 | async-start | bytes 3145728 | tf_op jit(solution)/shard_map/all_to_all | solution.py:1372
  240.1 11.0 %copy-start.4 = (bf16[768,512]{1,0:T(8,128)(2,1)}, bf16[768,512]{1,0:T(8,128)(2,1)S(1)}, u32[]{:S(2)}) copy-start(bf16[768,512]{1,0:T(8,128)(2,1)S(1)} %collective-permute-done.6) | copy-start | bytes 2359300
  240.2 11.0 %copy-start.5 = (bf16[768,512]{1,0:T(8,128)(2,1)}, bf16[768,512]{1,0:T(8,128)(2,1)S(1)}, u32[]{:S(2)}) copy-start(bf16[768,512]{1,0:T(8,128)(2,1)S(1)} %collective-permute-done.7) | copy-start | bytes 2359300
  251.2 4.0 %copy-start = (bf16[16,64,768]{2,1,0:T(8,128)(2,1)}, bf16[16,64,768]{2,1,0:T(8,128)(2,1)S(1)}, u32[]{:S(2)}) copy-start(bf16[16,64,768]{2,1,0:T(8,128)(2,1)S(1)} %all-to-all-done.2) | copy-start | bytes 4718596
  251.2 130.4 %collective-permute-start.10 = (bf16[1024,768]{1,0:T(8,128)(2,1)S(1)}, bf16[1024,768]{1,0:T(8,128)(2,1)S(1)}, u32[]{:S(2)}, u32[]{:S(2)}) collective-permute-start(bf16[1024,768]{1,0:T(8,128)(2,1)S(1)} %bitcast.38), channel_id=1, source_target_pairs={{0,1},{1,0},{2,3},{3,2},{4,5},{5,4},{6,7},{7,6},{8,9},{9,8},{10,11... | collective-permute-start | bytes 4718600 | tf_op jit(solution)/shard_map/ppermute | solution.py:1353
  381.6 1.2 copy-start.3

commit v3 on v2

--- a/solution.py
+++ b/solution.py
@@ -605,6 +605,7 @@
     local = o_own.shape[1]
     hidden = up[0].shape[1]
     block, tall = feed_specs(rows)
+    row = pl.BlockSpec((1, width), lambda i: (0, 0))
     weights = (*wo, up[0], down[0], up[1], down[1])
     bf16 = jnp.bfloat16
     return pl.pallas_call(
@@ -617,7 +618,7 @@
             struct((1, width, rows), bf16),
         ]
         + [struct((rows, hidden), bf16)] * 4,
-        in_specs=[tall(width), tall(local), tall(local), tall(width), tall(1)] + [VMEM] * 2 + [ANYWHERE] * 6,
+        in_specs=[tall(width), tall(local), tall(local), tall(width), tall(1)] + [row] * 2 + [ANYWHERE] * 6,
         out_specs=[tall(width)] * 3 + [pl.BlockSpec((1, width, block), lambda i: (0, 0, i))] + [tall(hidden)] * 4,
         scratch_shapes=[pltpu.VMEM(w.shape, bf16) for w in weights] + [pltpu.SemaphoreType.DMA((6,))],
         compiler_params=params(60),
@@ -631,6 +632,7 @@
     local = o_own.shape[1]
     hidden = up[0].shape[1]
     block, tall = feed_specs(rows)
+    row = pl.BlockSpec((1, width), lambda i: (0, 0))
     weights = (*wo, up[0], down[0], up[1], down[1])
     bf16 = jnp.bfloat16
     lefts = hidden // 3 * 4
@@ -648,7 +650,7 @@
             struct(blocks.shape[1:], bf16),
         ],
         in_specs=[tall(width), tall(width), tall(hidden), tall(hidden), tall(local), tall(local)]
-        + [VMEM] * 2
+        + [row] * 2
         + [ANYWHERE] * 7,
         out_specs=[
             tall(lefts),
@@ -810,17 +812,11 @@
     return lax.ppermute(block, "dp", [(i, i ^ d) for i in range(size)])
 
 
-def add_up(blocks):
-    total = blocks[0].astype(jnp.float32)
-    for block in blocks[1:]:
-        total = total + block.astype(jnp.float32)
-    return total.astype(jnp.bfloat16)
-
-
 def close_kernel(
-    size, own_ref, other_ref, up_in, down_in, gain_ref, norm2_ref, grads_in, ht_in, w_in, dy1_in, x_in,
+    size, own_ref, other_ref, down_in, gain_ref, norm2_ref,
+    block_0, block_1, block_2, block_3, grads_in, ht_in, w_in, dy1_in, x_in,
     up_out, down_out, second_out, rows_own, rows_other, norms_out,
-    grads_ref, ht_ref, w_ref, dy1_ref, x_ref, mine_a, mine_c, part, natural, swap_s, swap_r, dx, acc_a, acc_c, land_a, land_c, near_b, near_m, sum_b, norm_s, norm_r, norm_t,
+    blocks, up_in, grads_ref, ht_ref, w_ref, dy1_ref, x_ref, mine_a, mine_c, part, natural, swap_s, swap_r, dx, acc_a, acc_c, land_a, land_c, near_b, near_m, sum_b, norm_s, norm_r, norm_t,
     near_sem_s, near_sem_r, far_sem_s, far_sem_r, part_s, part_r, trade_s, trade_r, pass_s, pass_r,
     small_s, small_r, mp_s, mp_r, local, load, store,
 ):
@@ -847,8 +843,12 @@
             ((grads_in, grads_ref), (ht_in, ht_ref), (w_in, w_ref), (dy1_in, dy1_ref), (x_in, x_ref))
         )
     ]
-    for i in (0, 1, 2, 3, 4):
-        loads[i].start()
+    ups = [
+        pltpu.make_async_copy(one, blocks.at[i], load.at[5 + i])
+        for i, one in enumerate((block_0, block_1, block_2, block_3))
+    ]
+    for one in (*ups, *loads):
+        one.start()
 
     barrier = pltpu.get_barrier_semaphore()
 
@@ -995,6 +995,13 @@
         source = (me - d + size) % size
         return remote(norm_s, norm_r.at[source], small_s.at[d], small_r.at[d], source)
 
+    for one in ups:
+        one.wait()
+    for j in range(far):
+        total = blocks[0, j].astype(jnp.float32)
+        for d in range(1, NEAR):
+            total = total + blocks[d, j].astype(jnp.float32)
+        up_in[j] = total.astype(bf16)
     reduce_start(0, 1)
     kept(1).start()
     available(1, 0)
@@ -1181,15 +1188,16 @@
     lax.fori_loop(1, size, close, 0)
 
 
-def close(own, other, up_chunk, down_share, grads, ht, w, x, dy1, gain, norm2, size):
+def close(own, other, up_blocks, down_share, grads, ht, w, x, dy1, gain, norm2, size):
     far = size // NEAR
     rows, local = grads.shape[1:]
     width = w.shape[1]
     b = padded(3 * width, size)
     n = x.shape[0] // size
     bf16, f32 = jnp.bfloat16, jnp.float32
-    shares = (up_chunk.shape[0] // far, down_share.shape[0])
-    cols = (up_chunk.shape[1], down_share.shape[1])
+    shares = (up_blocks[0].shape[0] // far, down_share.shape[0])
+    cols = (up_blocks[0].shape[1], down_share.shape[1])
+    up_blocks = [one.reshape(far, shares[0], cols[0]) for one in up_blocks]
     share_b = b // size
     dma = pltpu.SemaphoreType.DMA
     step = min(256, x.shape[0])
@@ -1203,9 +1211,11 @@
             struct((size, n, width), bf16),
             struct((8, width), f32),
         ],
-        in_specs=[SMEM, SMEM] + [VMEM] * 4 + [ANYWHERE] * 5,
+        in_specs=[SMEM, SMEM] + [VMEM] * 3 + [ANYWHERE] * 9,
         out_specs=[ANYWHERE] * 5 + [VMEM],
         scratch_shapes=[
+            pltpu.VMEM((NEAR, far, shares[0], cols[0]), bf16),
+            pltpu.VMEM((far, shares[0], cols[0]), bf16),
             pltpu.VMEM(grads.shape, bf16),
             pltpu.VMEM(ht.shape, bf16),
             pltpu.VMEM(w.shape, bf16),
@@ -1243,7 +1253,7 @@
             dma((2,)),
             dma((2,)),
             dma((2,)),
-            dma((5,)),
+            dma((9,)),
             dma((3,)),
         ],
         compiler_params=pltpu.CompilerParams(
@@ -1252,8 +1262,7 @@
         cost_estimate=cost(8 * rows * width * local, 1e8),
         name="close",
     )(
-        own, other, up_chunk.reshape(far, shares[0], cols[0]), down_share, gain, norm2,
-        grads, ht, w, dy1, x,
+        own, other, down_share, gain, norm2, *up_blocks, grads, ht, w, dy1, x,
     )
     return (
         up_sum.reshape(NEAR, -1, cols[0]),
@@ -1412,11 +1421,11 @@
     wo_other, up_other, down_other = swap(out_weight), swap(up_weight), swap(down_weight)
     gain1, shift1 = norm1_gain[None], norm1_shift[None]
     gain2, shift2 = norm2_gain[None], norm2_shift[None]
-    x_own, dy_send, real, wo_other, up_other, down_other, own, other, gain1, shift1, gain2, shift2 = (
+    x_own, dy_send, real, wo_other, up_other, down_other, own, other, gain1, shift1, gain2, shift2, src_other = (
         lax.optimization_barrier(
             (
                 x_own, dy_send, real, wo_other, up_other, down_other,
-                own, other, gain1, shift1, gain2, shift2,
+                own, other, gain1, shift1, gain2, shift2, src_other,
             )
         )
     )
@@ -1446,10 +1455,9 @@
     grads = attend_back(own, other, lengths, counts, q, k, v, qt, kt, ot, lse, do_own, do_other)
     up_got, grads, out_back = lax.optimization_barrier((up_got, grads, out_back))
     out_other = swap(out_back)
-    up_chunk = add_up([up_blocks[0], *up_got])
-    up_chunk = jnp.pad(up_chunk, ((0, -up_chunk.shape[0] % unit), (0, 0)))
+    parts = [jnp.pad(one, ((0, -one.shape[0] % unit), (0, 0))) for one in (up_blocks[0], *up_got)]
     up_sum, down_sum, qkv_grad, dx_own, dx_other, norms = close(
-        own, other, up_chunk, down_share, grads, h1_t, qkv_weight, x_own, dy1, gain1, norm2, groups
+        own, other, parts, down_share, grads, h1_t, qkv_weight, x_own, dy1, gain1, norm2, groups
     )
     mixed_out, input_grad, up_grad, down_grad, wo_grad, qkv_grad = settle(
         src_own, src_other, (out_back, out_other), (dx_own, dx_other), up_sum, down_sum, qkv_grad,

time: 399 us -> 393 us (0.985); the launches traced: 395 us -> 394 us
  waiting for transfers between devices: 30.2 us -> 37.6 us
    pallas_call x2, Pallas kernels: 31.9 us -> 40.8 us  [weight_grads(): pl.pallas_call(functools.partial(weight_kernel, size, chunk is not None),...]
    pallas_call x1, Pallas kernels: 33.7 us -> 25.2 us  [attend_back(): pl.pallas_call(attend_back_kernel, out_shape=struct((3, rows, width), jnp...]
    ppermute x3, waiting for transfers between devices: 8.99 us -> 16.6 us  [near_send(): return lax.ppermute(block, 'dp', [(i, i ^ d) for i in range(size)])]
    pallas_call x1, Pallas kernels: 30.8 us -> 25.2 us  [attend(): pl.pallas_call(attend_kernel, out_shape=[struct((width, rows), jnp.bfloat...]
  transfers between devices with their start and end apart: 14 -> 14, of which waited for: 4 -> 5; matrix products, arithmetic and copies ran while one was open for 3% -> 2% of each run, Pallas kernels for 57% -> 56%
where the time goes in v3:
time: 393 us; the launch traced here: 394 us
  Pallas kernels  305 us (78%)
  waiting for transfers between devices  37.6 us (10%)
  starting transfers between devices  27.6 us (7%)
  local copies, waits for them, and re-layouts  13.4 us (3%)
  between operations  8.97 us (2%)
    pallas_call x1, Pallas kernels, close(): pl.pallas_call(functools.partial(close_kernel, size), out_shape=[struct((...  128 us
    pallas_call x2, Pallas kernels, weight_grads(): pl.pallas_call(functools.partial(weight_kernel, size, chunk is not None),...  40.8 us
    pallas_call x1, Pallas kernels, feed_back(): pl.pallas_call(feed_back_kernel, grid=(rows // block,), out_shape=[struct...  33.8 us
    pallas_call x1, Pallas kernels, attend(): pl.pallas_call(attend_kernel, out_shape=[struct((width, rows), jnp.bfloat...  25.2 us
    pallas_call x1, Pallas kernels, attend_back(): pl.pallas_call(attend_back_kernel, out_shape=struct((3, rows, width), jnp...  25.2 us
    all_to_all x3, starting transfers between devices, exchange(): return lax.all_to_all(value, 'dp', split_axis=0, concat_axis=0, tiled=True)  23 us
    pallas_call x1, Pallas kernels, feed(): pl.pallas_call(feed_kernel, grid=(rows // block,), out_shape=[struct((row...  22.3 us
    all_to_all x3, waiting for transfers between devices, exchange(): return lax.all_to_all(value, 'dp', split_axis=0, concat_axis=0, tiled=True)  19.7 us
  transfers between devices with their start and end apart: 14, of which 5 were waited for; matrix products, arithmetic and copies ran while one was open for 2% of the time, Pallas kernels for 56%

profile of v3, /device:TPU:0, one launch (start us, length us, event | category | flops | bytes accessed | tf_op | source)
XLA Modules:
  0.0 394.1 jit_solution(2094536479361970096)
XLA Ops:
  0.6 0.7 reshape.266
  1.4 0.2 fusion
  1.5 0.2 fusion.1
  1.7 0.4 select_reduce_fusion.1
  2.1 0.3 select_reduce_fusion
  2.5 0.7 reshape.267.index_ref.own_ref
  3.2 3.3 gather_pieces.2
  6.5 8.5 %all-to-all-start = ((bf16[16,64,768]{2,1,0:T(8,128)(2,1)}), bf16[16,64,768]{2,1,0:T(8,128)(2,1)S(1)}, u32[]{:S(2)}, u32[]{:S(2)}) async-start(bf16[16,64,768]{2,1,0:T(8,128)(2,1)} %bitcast.38), calls=%async_computation | async-start | bytes 3145728 | tf_op jit(solution)/shard_map/all_to_all | solution.py:1381
  15.0 0.5 collective-permute-start.2
  15.6 0.6 broadcast_in_dim.47.gain_ref
  16.2 0.6 broadcast_in_dim.48.shift_ref
  16.8 0.6 broadcast_in_dim.49.gain_ref
  17.4 0.6 broadcast_in_dim.50.shift_ref
  17.9 0.7 fusion.36
  25.1 0.7 reshape.271.other_ref
  25.8 0.1 broadcast_in_dim_reshape.3.own_ref
  25.9 0.6 reshape.272.other_ref
  27.9 0.7 fusion.27
  28.5 0.1 copy.26
  28.6 0.1 reshape.294
  28.7 3.3 gather_pieces.3
  32.0 17.1 %all-to-all-done = bf16[16,64,768]{2,1,0:T(8,128)(2,1)S(1)} async-done(((bf16[16,64,768]{2,1,0:T(8,128)(2,1)}), bf16[16,64,768]{2,1,0:T(8,128)(2,1)S(1)}, u32[]{:S(2)}, u32[]{:S(2)}) %all-to-all-start) | async-done | bytes 1572896 | tf_op jit(solution)/shard_map/all_to_all | solution.py:1381
  49.1 7.6 %all-to-all-start.1 = ((bf16[16,64,768]{2,1,0:T(8,128)(2,1)}), bf16[16,64,768]{2,1,0:T(8,128)(2,1)S(1)}, u32[]{:S(2)}, u32[]{:S(2)}) async-start(bf16[16,64,768]{2,1,0:T(8,128)(2,1)} %bitcast.40), calls=%async_computation.1 | async-start | bytes 3145728 | tf_op jit(solution)/shard_map/all_to_all | solution.py:1381
  56.8 11.6 %project.1 = (bf16[768,2048]{1,0:T(8,128)(2,1)}, bf16[2048,384]{1,0:T(8,128)(2,1)}, bf16[2048,384]{1,0:T(8,128)(2,1)}, bf16[2048,384]{1,0:T(8,128)(2,1)}, bf16[3...) custom-call(s32[128]{0:T(128)} %copy-done.11, s32[128]{0:T(128)} %reshape.271.other_ref, ...), custom_call_target="tpu_custom_call" | custom-call | flops 3623878656 | bytes 20000000 | tf_op jit(solution)/shard_map/project/pallas_call | solution.py:131
  68.4 25.2 %attend.1 = (bf16[384,2048]{1,0:T(8,128)(2,1)}, bf16[128,8,384]{2,1,0:T(8,128)(2,1)}, bf16[128,8,384]{2,1,0:T(8,128)(2,1)}, f32[8,2048]{1,0:T(8,128)}) custom-call(s32[128]{0:T(128)} %copy-done.11, s32[128]{0:T(128)} %reshape.271.other_ref, s32[1,4]{1,0:T(1,128)} %len_ref.3, s32[1,4]{1,0:T(1,128)} %cnt_ref.3, bf16[2048,384]{1,0:T(8,128)(2,1)} %get-tuple-element.84.k_in, ...), custom_call_target="tpu_custom_call" | custom-call | flops 20000000000 | bytes 10000000 | tf_op jit(solution)/shard_map/attend/pallas_call | solution.py:263
  93.7 0.3 collective-permute-start.4
  93.9 1.0 copy.27.real_ref
  95.0 1.3 collective-permute-done.4.ob_ref
  96.2 0.9 copy-done.15
  97.1 0.5 copy-done.2
  97.6 22.3 %feed.1 = (bf16[1024,768]{1,0:T(8,128)(2,1)}, f32[1024,768]{1,0:T(8,128)}, bf16[1024,768]{1,0:T(8,128)(2,1)}, bf16[1,768,1024]{2,1,0:T(8,128)(2,1)}, bf16[1024,1...) custom-call(bf16[1024,768]{1,0:T(8,128)(2,1)} %bitcast.50, ...), custom_call_target="tpu_custom_call" | custom-call | flops 10871635968 | bytes 45000000 | tf_op jit(solution)/shard_map/feed/pallas_call | solution.py:611
  119.9 12.2 %weight_grads.2.blocks_ref = bf16[4,768,384]{2,1,0:T(8,128)(2,1)} custom-call(bf16[1024,1536]{1,0:T(8,128)(2,1)} %get-tuple-element.100.other_ref, bf16[1024,1536]{1,0:T(8,128)(2,1)} %get-tuple-element.101.own_ref, bf16[1,768,1024]{2,1,0:T(8,128)(2,1)} %get-tuple-element.102.right_ref), custom_call_target="tpu_custom_call" | custom-call | flops 4831838208 | bytes 20000000 | tf_op jit(solution)/shard_map/weight_grads/pallas_call | solution.py:792
  132.1 33.8 %feed_back.1 = (bf16[1024,2048]{1,0:T(8,128)(2,1)}, bf16[1024,2048]{1,0:T(8,128)(2,1)}, bf16[2,768,1024]{2,1,0:T(8,128)(2,1)}, bf16[1024,384]{1,0:T(8,128)(2,1)}...) custom-call(f32[1024,768]{1,0:T(8,128)} %get-tuple-element.96.y1_ref, ...), custom_call_target="tpu_custom_call" | custom-call | flops 10871635968 | bytes 45000000 | tf_op jit(solution)/shard_map/feed_back/pallas_call | solution.py:639
  166.0 28.6 %weight_grads.3 = (bf16[768,512]{1,0:T(8,128)(2,1)}, bf16[768,512]{1,0:T(8,128)(2,1)}, bf16[768,512]{1,0:T(8,128)(2,1)}, bf16[768,512]{1,0:T(8,128)(2,1)}, bf16[192,384]{1,0:T(8,128)(2,1)}) custom-call(bf16[1024,2048]{1,0:T(8,128)(2,1)} %get-tuple-element.103.other_ref, bf16[1024,2048]{1,0:T(8,128)(2,1)} %get-tuple-element.104.own_ref, ...), custom_call_target="tpu_custom_call" | custom-call | flops 6442450944 | bytes 20000000 | tf_op jit(solution)/shard_map/weight_grads/pallas_call | solution.py:792
  194.6 0.9 copy-done.14
  195.5 0.7 slice.50
  196.1 2.1 collective-permute-start.7
  198.3 1.3 collective-permute-start.8
  199.6 0.6 copy-done.6
  200.2 6.9 %all-to-all-start.2 = ((bf16[16,64,768]{2,1,0:T(8,128)(2,1)}), bf16[16,64,768]{2,1,0:T(8,128)(2,1)S(1)}, u32[]{:S(2)}, u32[]{:S(2)}) async-start(bf16[16,64,768]{2,1,0:T(8,128)(2,1)} %bitcast.39), calls=%async_computation.2 | async-start | bytes 3145728 | tf_op jit(solution)/shard_map/all_to_all | solution.py:1381
  207.1 25.2 %attend_back.1.grads_in = bf16[3,2048,384]{2,1,0:T(8,128)(2,1)} custom-call(s32[128]{0:T(128)} %copy-done.11, s32[128]{0:T(128)} %reshape.271.other_ref, s32[1,4]{1,0:T(1,128)} %len_ref.3, s32[1,4]{1,0:T(1,128)} %cnt_ref.3, bf16[2048,384]{1,0:T(8,128)(2,1)} %get-tuple-element.116.q_in, bf16[2048,384]{1,0:T(8,128)(2,1)} %get-tuple-element.84.k_in, ...), custom_call_target="tpu_custom_call" | custom-call | flops 49999998976 | bytes 20000000 | tf_op jit(solution)/shard_map/attend_back/pallas_call | solution.py:405
  232.3 5.1 %collective-permute-done.7 = bf16[768,512]{1,0:T(8,128)(2,1)S(1)} collective-permute-done((bf16[768,512]{1,0:T(8,128)(2,1)}, bf16[768,512]{1,0:T(8,128)(2,1)S(1)}, u32[]{:S(2)}, u32[]{:S(2)}) %collective-permute-start.7) | collective-permute-done | bytes 786464 | tf_op jit(solution)/shard_map/ppermute | solution.py:812
  237.4 11.5 %collective-permute-done.8 = bf16[768,512]{1,0:T(8,128)(2,1)} collective-permute-done((bf16[768,512]{1,0:T(8,128)(2,1)}, bf16[768,512]{1,0:T(8,128)(2,1)}, u32[]{:S(2)}, u32[]{:S(2)}) %collective-permute-start.8) | collective-permute-done | bytes 786464 | tf_op jit(solution)/shard_map/ppermute | solution.py:812
  248.9 2.6 all-to-all-done.2
  251.6 127.7 %close.1 = (bf16[4,4,192,512]{3,2,1,0:T(8,128)(2,1)}, bf16[4,4,192,384]{3,2,1,0:T(8,128)(2,1)}, bf16[4,4,144,384]{3,2,1,0:T(8,128)(2,1)}, bf16[16,64,768]{2,1,0:...) custom-call(s32[128]{0:T(128)} %copy-done.11, s32[128]{0:T(128)} %reshape.271.other_ref, ...), custom_call_target="tpu_custom_call" | custom-call | flops 4831838208 | bytes 100000000 | tf_op jit(solution)/shard_map/close/pallas_call | solution.py:1204
  379.3 1.5 slice_reduce_fusion
  380.8 1.2 copy-done.3
  382.0 11.9 %settle.1 = (bf16[256,8,768]{2,1,0:T(8,128)(2,1)}, bf16[256,8,768]{2,1,0:T(8,128)(2,1)}, f32[768,1536]{1,0:T(8,128)}, f32[1536,768]{1,0:T(8,128)}, f32[384,768]{1,0:T(8,128)}, /*index=5*/f32[2304,384]{1,0:T(8,128)}) custom-call(s32[128]{0:T(128)} %reshape.267.index_ref.own_ref, s32[128]{0:T(128)} %reshape.272.other_ref, bf16[128,8,768]{2,1,0:T(8,128)(2,1)} %bitcast.42, ...), custom_call_target="tpu_custom_call" | custom-call | bytes 34000000 | tf_op jit(solution)/shard_map/settle/pallas_call | solution.py:1341
  (52 shorter events, 0.5 us)
Async XLA Ops:
  6.4 9.1 %copy-start.16 = (bf16[384,768]{1,0:T(8,128)(2,1)S(1)}, bf16[384,768]{1,0:T(8,128)(2,1)}, u32[]{:S(2)}) copy-start(bf16[384,768]{1,0:T(8,128)(2,1)} %refs_0_.3) | copy-start | bytes 1769476
  6.4 9.2 %copy-start.7 = (f32[768]{0:T(1024)S(1)}, f32[768]{0:T(1024)}, u32[]{:S(2)}) copy-start(f32[768]{0:T(1024)} %param.22) | copy-start | bytes 9220
  6.4 9.8 %copy-start.8 = (f32[768]{0:T(1024)S(1)}, f32[768]{0:T(1024)}, u32[]{:S(2)}) copy-start(f32[768]{0:T(1024)} %param.23) | copy-start | bytes 9220
  6.4 10.3 %copy-start.9 = (f32[768]{0:T(1024)S(1)}, f32[768]{0:T(1024)}, u32[]{:S(2)}) copy-start(f32[768]{0:T(1024)} %param.24) | copy-start | bytes 9220
  6.4 10.9 %copy-start.10 = (f32[768]{0:T(1024)S(1)}, f32[768]{0:T(1024)}, u32[]{:S(2)}) copy-start(f32[768]{0:T(1024)} %param.25) | copy-start | bytes 9220
  6.5 11.5 %copy-start.4 = (s32[1,4]{1,0:T(1,128)S(1)}, s32[1,4]{1,0:T(1,128)}, u32[]{:S(2)}) copy-start(s32[1,4]{1,0:T(1,128)} %len_ref.3) | copy-start | bytes 52
  6.5 11.5 %copy-start.5 = (s32[1,4]{1,0:T(1,128)S(1)}, s32[1,4]{1,0:T(1,128)}, u32[]{:S(2)}) copy-start(s32[1,4]{1,0:T(1,128)} %cnt_ref.3) | copy-start | bytes 52
  6.5 42.6 %all-to-all-start = ((bf16[16,64,768]{2,1,0:T(8,128)(2,1)}), bf16[16,64,768]{2,1,0:T(8,128)(2,1)S(1)}, u32[]{:S(2)}, u32[]{:S(2)}) async-start(bf16[16,64,768]{2,1,0:T(8,128)(2,1)} %bitcast.38), calls=%async_computation | async-start | bytes 3145728 | tf_op jit(solution)/shard_map/all_to_all | solution.py:1381
  14.9 17.0 %collective-permute-start.1 = (bf16[768,1536]{1,0:T(8,128)(2,1)}, bf16[768,1536]{1,0:T(8,128)(2,1)}, u32[]{:S(2)}, u32[]{:S(2)}) collective-permute-start(bf16[768,1536]{1,0:T(8,128)(2,1)} %refs_2_.3), channel_id=1, source_target_pairs={{0,1},{1,0},{2,3},{3,2},{4,5},{5,4},{6,7},{7,6},{8,9},{9,8},{10,11... | collective-permute-start | bytes 7077896 | tf_op jit(solution)/shard_map/ppermute | solution.py:1362
  15.0 17.0 %collective-permute-start.2 = (bf16[1536,768]{1,0:T(8,128)(2,1)}, bf16[1536,768]{1,0:T(8,128)(2,1)}, u32[]{:S(2)}, u32[]{:S(2)}) collective-permute-start(bf16[1536,768]{1,0:T(8,128)(2,1)} %refs_3_.3), channel_id=1, source_target_pairs={{0,1},{1,0},{2,3},{3,2},{4,5},{5,4},{6,7},{7,6},{8,9},{9,8},{10,11... | collective-permute-start | bytes 7077896 | tf_op jit(solution)/shard_map/ppermute | solution.py:1362
  15.5 16.5 %collective-permute-start = (bf16[384,768]{1,0:T(8,128)(2,1)S(1)}, bf16[384,768]{1,0:T(8,128)(2,1)S(1)}, u32[]{:S(2)}, u32[]{:S(2)}) collective-permute-start(bf16[384,768]{1,0:T(8,128)(2,1)S(1)} %copy-done.16), channel_id=1, source_target_pairs={{0,1},{1,0},{2,3},{3,2},{4,5},{5,4},{6,7},{7,6},{8,9},{9,8},{10,11... | collective-permute-start | bytes 1769480 | tf_op jit(solution)/shard_map/ppermute | solution.py:1362
  25.9 6.1 %copy-start.11 = (s32[128]{0:T(128)}, s32[128]{0:T(128)S(1)}, u32[]{:S(2)}) copy-start(s32[128]{0:T(128)S(1)} %broadcast_in_dim_reshape.3.own_ref) | copy-start | bytes 1540
  32.0 17.1 %copy-start.17 = (bf16[384,768]{1,0:T(8,128)(2,1)}, bf16[384,768]{1,0:T(8,128)(2,1)S(1)}, u32[]{:S(2)}) copy-start(bf16[384,768]{1,0:T(8,128)(2,1)S(1)} %collective-permute-done.refs_1_) | copy-start | bytes 1769476
  49.1 7.7 %copy-start.1 = (bf16[16,64,768]{2,1,0:T(8,128)(2,1)}, bf16[16,64,768]{2,1,0:T(8,128)(2,1)S(1)}, u32[]{:S(2)}) copy-start(bf16[16,64,768]{2,1,0:T(8,128)(2,1)S(1)} %all-to-all-done) | copy-start | bytes 4718596
  49.1 7.7 %collective-permute-start.3 = (bf16[1024,768]{1,0:T(8,128)(2,1)S(1)}, bf16[1024,768]{1,0:T(8,128)(2,1)}, u32[]{:S(2)}, u32[]{:S(2)}) collective-permute-start(bf16[1024,768]{1,0:T(8,128)(2,1)S(1)} %bitcast.48), channel_id=1, source_target_pairs={{0,1},{1,0},{2,3},{3,2},{4,5},{5,4},{6,7},{7,6},{8,9},{9,8},{10,11... | collective-permute-start | bytes 4718600 | tf_op jit(solution)/shard_map/ppermute | solution.py:1362
  49.1 47.1 %all-to-all-start.1 = ((bf16[16,64,768]{2,1,0:T(8,128)(2,1)}), bf16[16,64,768]{2,1,0:T(8,128)(2,1)S(1)}, u32[]{:S(2)}, u32[]{:S(2)}) async-start(bf16[16,64,768]{2,1,0:T(8,128)(2,1)} %bitcast.40), calls=%async_computation.1 | async-start | bytes 3145728 | tf_op jit(solution)/shard_map/all_to_all | solution.py:1381
  93.7 2.6 collective-permute-start.4
  96.2 0.9 copy-start.15
  96.2 1.4 copy-start.2
  165.9 28.7 %collective-permute-start.5 = (bf16[1024,384]{1,0:T(8,128)(2,1)}, bf16[1024,384]{1,0:T(8,128)(2,1)S(1)}, u32[]{:S(2)}, u32[]{:S(2)}) collective-permute-start(bf16[1024,384]{1,0:T(8,128)(2,1)} %get-tuple-element.112), channel_id=1, source_target_pairs={{0,1},{1,0},{2,3},{3,2},{4,5},{5,4},{6,7},{7,6},{8,9},{9,8},{10,11... | collective-permute-start | bytes 2359304 | tf_op jit(solution)/shard_map/ppermute | solution.py:1362
  194.6 0.9 copy-start.14
  196.1 3.5 collective-permute-start.9
  196.1 36.2 %collective-permute-start.6 = (bf16[768,512]{1,0:T(8,128)(2,1)}, bf16[768,512]{1,0:T(8,128)(2,1)S(1)}, u32[]{:S(2)}, u32[]{:S(2)}) collective-permute-start(bf16[768,512]{1,0:T(8,128)(2,1)} %get-tuple-element.113), channel_id=1, source_target_pairs={{0,2},{2,0},{4,6},{6,4},{8,10},{10,8},{12,14},{14,12},{16,18},{18,... | collective-permute-start | bytes 2359304 | tf_op jit(solution)/shard_map/ppermute | solution.py:812
  196.1 41.3 %collective-permute-start.7 = (bf16[768,512]{1,0:T(8,128)(2,1)}, bf16[768,512]{1,0:T(8,128)(2,1)S(1)}, u32[]{:S(2)}, u32[]{:S(2)}) collective-permute-start(bf16[768,512]{1,0:T(8,128)(2,1)} %get-tuple-element.114), channel_id=1, source_target_pairs={{0,4},{2,6},{4,0},{6,2},{8,12},{10,14},{12,8},{14,10},{16,20},{18,... | collective-permute-start | bytes 2359304 | tf_op jit(solution)/shard_map/ppermute | solution.py:812
  198.3 50.6 %collective-permute-start.8 = (bf16[768,512]{1,0:T(8,128)(2,1)}, bf16[768,512]{1,0:T(8,128)(2,1)}, u32[]{:S(2)}, u32[]{:S(2)}) collective-permute-start(bf16[768,512]{1,0:T(8,128)(2,1)} %get-tuple-element.115), channel_id=1, source_target_pairs={{0,6},{2,4},{4,2},{6,0},{8,14},{10,12},{12,10},{14,8},{16,22},{18,... | collective-permute-start | bytes 2359304 | tf_op jit(solution)/shard_map/ppermute | solution.py:812
  199.6 0.6 copy-start.6
  200.2 51.3 %all-to-all-start.2 = ((bf16[16,64,768]{2,1,0:T(8,128)(2,1)}), bf16[16,64,768]{2,1,0:T(8,128)(2,1)S(1)}, u32[]{:S(2)}, u32[]{:S(2)}) async-start(bf16[16,64,768]{2,1,0:T(8,128)(2,1)} %bitcast.39), calls=%async_computation.2 | async-start | bytes 3145728 | tf_op jit(solution)/shard_map/all_to_all | solution.py:1381
  232.3 19.2 %copy-start.12 = (bf16[768,512]{1,0:T(8,128)(2,1)}, bf16[768,512]{1,0:T(8,128)(2,1)S(1)}, u32[]{:S(2)}) copy-start(bf16[768,512]{1,0:T(8,128)(2,1)S(1)} %collective-permute-done.6) | copy-start | bytes 2359300
  237.4 14.1 %copy-start.13 = (bf16[768,512]{1,0:T(8,128)(2,1)}, bf16[768,512]{1,0:T(8,128)(2,1)S(1)}, u32[]{:S(2)}) copy-start(bf16[768,512]{1,0:T(8,128)(2,1)S(1)} %collective-permute-done.7) | copy-start | bytes 2359300
  251.5 127.7 %copy-start = (bf16[16,64,768]{2,1,0:T(8,128)(2,1)}, bf16[16,64,768]{2,1,0:T(8,128)(2,1)S(1)}, u32[]{:S(2)}) copy-start(bf16[16,64,768]{2,1,0:T(8,128)(2,1)S(1)} %all-to-all-done.2) | copy-start | bytes 4718596
  251.5 129.3 %collective-permute-start.10 = (bf16[1024,768]{1,0:T(8,128)(2,1)S(1)}, bf16[1024,768]{1,0:T(8,128)(2,1)S(1)}, u32[]{:S(2)}, u32[]{:S(2)}) collective-permute-start(bf16[1024,768]{1,0:T(8,128)(2,1)S(1)} %bitcast.41), channel_id=1, source_target_pairs={{0,1},{1,0},{2,3},{3,2},{4,5},{5,4},{6,7},{7,6},{8,9},{9,8},{10,11... | collective-permute-start | bytes 4718600 | tf_op jit(solution)/shard_map/ppermute | solution.py:1362
  380.8 1.2 copy-start.3
